TPU v7x, 512 devices: a whole 4x4x16 slice. The times are simulated.
512 devices in a mesh: island: 8 (over y_hi, x), local: 64 (over z, y_lo, core).
Axes of the slice: x: 4, y: 4 (y_hi: 2, y_lo: 2; y = y_hi * 2 + y_lo), z: 16, core: 2. Of those that a mesh axis runs over, the one named last changes fastest.
Arguments:
- activations: bfloat16 [65536, 4096], P(('island', 'local')), may hold values from -8 to 8
- norm_gain: float32 [4096], replicated, may hold values from 0.25 to 1.75
- qkv_weight: bfloat16 [4096, 384], P('local'), may hold values from -3 to 3
- positions: int32 [65536], P(('island', 'local')), may hold values from 0 to 127, as said below
- cotangent: bfloat16 [65536, 128], P(('island', 'local')), may hold values from -0.0625 to 0.0625
Outputs:
- qkv_gradient: float32 [4096, 384], P(('island', 'local'))
- gain_gradient: float32 [4096], P(('island', 'local'))
Inputs may be any that keep to these rules, and one draw needn't show every extreme that they name: `positions`: every block of 128 tokens begins a document with position 0; within a block a position is one more than the one before it or 0 where a new document starts; in some block no new document starts.
All inputs are finite; a program needn't handle non-finite values.
Results may differ from a plain program's by a relative error of at most 0.007.
The roundings to bfloat16 on the way count: a program that leaves them out, or rounds other values in their place, can miss the bound.
Values may be sent and summed in bfloat16 or wider, within the bound.
No kernel may reach another device: no remote copies, remote signals or barrier semaphores. Data moves between devices by JAX's collectives and lax.ppermute only.
A program may use at most 64 MiB of HBM per device.

v0:
```python
import jax
import jax.numpy as jnp
from jax import lax
from jax.sharding import PartitionSpec as P

rope_base = 10000.0
norm_eps = 1e-05


def rope_tables(positions, head_size):
    half_width = head_size // 2
    exponent = jnp.arange(half_width, dtype=jnp.float32) * (-2.0 / head_size)
    frequency = jnp.power(jnp.float32(rope_base), exponent)
    angle_table = positions.astype(jnp.float32)[:, None] * frequency[None, :]
    angle_table = jnp.concatenate([angle_table, angle_table], axis=1)
    return (jnp.cos(angle_table), jnp.sin(angle_table))


def rotate(vectors, cosine_table, sine_table):
    half_width = vectors.shape[1] // 2
    turned = jnp.concatenate([-vectors[:, half_width:], vectors[:, :half_width]], axis=1)
    return vectors * cosine_table + turned * sine_table


def unrotate(gradient, cosine_table, sine_table):
    half_width = gradient.shape[1] // 2
    sined = gradient * sine_table
    turned = jnp.concatenate([sined[:, half_width:], -sined[:, :half_width]], axis=1)
    return gradient * cosine_table + turned


def normalize(activations, norm_gain):
    widened = activations.astype(jnp.float32)
    inverse_rms = lax.rsqrt(jnp.mean(widened * widened, axis=1, keepdims=True) + norm_eps)
    normed = (widened * inverse_rms * norm_gain[None, :]).astype(jnp.bfloat16)
    return (normed, inverse_rms, widened)


def attention_grads(projected, positions, cotangent):
    head_size = cotangent.shape[1]
    cosine_table, sine_table = rope_tables(positions, head_size)
    queries = rotate(projected[:, :head_size], cosine_table, sine_table).astype(jnp.bfloat16)
    keys_rot = rotate(projected[:, head_size : 2 * head_size], cosine_table, sine_table).astype(
        jnp.bfloat16
    )
    values = projected[:, 2 * head_size :].astype(jnp.bfloat16)
    score_scale = head_size ** (-0.5)
    scores = (
        lax.dot_general(
            queries, keys_rot, (((1,), (1,)), ((), ())), preferred_element_type=jnp.float32
        )
        * score_scale
    )
    token_count = positions.shape[0]
    row_index = jnp.arange(token_count, dtype=jnp.int32)[:, None]
    column_index = jnp.arange(token_count, dtype=jnp.int32)[None, :]
    visible = (column_index <= row_index) & (row_index - column_index <= positions[:, None])
    scores = jnp.where(visible, scores, -jnp.inf)
    row_peak = jnp.max(scores, axis=1, keepdims=True)
    exp_terms = jnp.exp(scores - row_peak)
    attention = exp_terms / jnp.sum(exp_terms, axis=1, keepdims=True)
    attention_low = attention.astype(jnp.bfloat16)
    prob_grad = lax.dot_general(
        cotangent, values, (((1,), (1,)), ((), ())), preferred_element_type=jnp.float32
    )
    score_grad = (
        attention
        * (prob_grad - jnp.sum(attention * prob_grad, axis=1, keepdims=True))
        * score_scale
    ).astype(jnp.bfloat16)
    query_grad = jnp.dot(score_grad, keys_rot, preferred_element_type=jnp.float32)
    key_grad = lax.dot_general(
        score_grad, queries, (((0,), (0,)), ((), ())), preferred_element_type=jnp.float32
    )
    value_grad = lax.dot_general(
        attention_low, cotangent, (((0,), (0,)), ((), ())), preferred_element_type=jnp.float32
    )
    joined = jnp.concatenate(
        [
            unrotate(query_grad, cosine_table, sine_table),
            unrotate(key_grad, cosine_table, sine_table),
            value_grad,
        ],
        axis=1,
    )
    return joined.astype(jnp.bfloat16)


def shards(activations, norm_gain, qkv_weight, positions, cotangent):
    normed, inverse_rms, widened = normalize(activations, norm_gain)
    proj_width = qkv_weight.shape[1]
    whole_weight = lax.all_gather(qkv_weight, "local", axis=0, tiled=True)
    projected = jnp.dot(normed, whole_weight, preferred_element_type=jnp.float32)
    qkv_grads = attention_grads(projected, positions, cotangent)
    weight_term = lax.dot_general(
        normed, qkv_grads, (((0,), (0,)), ((), ())), preferred_element_type=jnp.float32
    )
    normed_grad = lax.dot_general(
        qkv_grads, whole_weight, (((1,), (1,)), ((), ())), preferred_element_type=jnp.float32
    )
    gain_term = jnp.sum(normed_grad * widened * inverse_rms, axis=0)
    island_count = lax.axis_size("island")
    local_count = lax.axis_size("local")
    full_rows = weight_term.shape[0]
    row_count = full_rows // (island_count * local_count)
    weight_parts = weight_term.reshape(island_count, local_count, row_count, proj_width)
    gain_parts = gain_term.reshape(island_count, local_count, row_count)
    received = (
        lax.all_to_all(weight_parts, "local", split_axis=1, concat_axis=1, tiled=True),
        lax.all_to_all(gain_parts, "local", split_axis=1, concat_axis=1, tiled=True),
    )
    weight_sums = jnp.sum(received[0], axis=1)
    gain_sums = jnp.sum(received[1], axis=1)
    second = (
        lax.all_to_all(weight_sums, "island", split_axis=0, concat_axis=0, tiled=True),
        lax.all_to_all(gain_sums, "island", split_axis=0, concat_axis=0, tiled=True),
    )
    qkv_share = jnp.sum(second[0], axis=0)
    gain_share = jnp.sum(second[1], axis=0)
    return (qkv_share, gain_share)


def solution(mesh):
    placed = (
        P(("island", "local"), None),
        P(),
        P("local", None),
        P(("island", "local")),
        P(("island", "local"), None),
    )
    return jax.shard_map(
        shards,
        mesh=mesh,
        in_specs=placed,
        out_specs=(P(("island", "local"), None), P(("island", "local"))),
        check_vma=False,
    )
```

profile of v0, /device:TPU:1, one launch (start us, length us, event | category | flops | bytes accessed | tf_op | source)
XLA Modules:
  0.0 486.7 jit_solution(6081273150093234626)
XLA Ops:
  7.2 0.7 all-gather.2.cloned.1.call-update
  7.9 0.7 convert_element_type.25
  8.6 1.5 fusion.1
  10.1 0.1 broadcast_multiply_fusion
  10.2 129.2 %all-gather.2.cloned.1.call-done = bf16[4096,384]{1,0:T(8,128)(2,1)} async-done(((bf16[64,384]{1,0:T(8,128)(2,1)}), bf16[4096,384]{1,0:T(8,128)(2,1)}) %all-gather.2.cloned.1.call-update) | async-done | bytes 3145744 | tf_op jit(solution)/shard_map/all_gather | solution.py:92
  139.4 3.1 fusion.8
  142.5 0.1 slice_negate_fusion.2
  142.6 0.3 fusion.11
  143.0 0.2 fusion.29
  143.2 0.2 multiply_reduce_fusion
  143.4 0.1 convolution_convert_fusion
  143.6 0.3 fusion.23
  143.9 0.1 fusion.27
  144.0 0.3 fusion.14
  144.4 0.3 fusion.15
  144.8 1.1 fusion.4
  145.9 0.2 reshape.32
  146.0 0.8 copy.31
  146.9 8.8 %all-to-all-start.2 = ((f32[8,64,8]{2,0,1:T(8,128)}), f32[8,64,8]{2,0,1:T(8,128)S(1)}, u32[]{:S(2)}, u32[]{:S(2)}) async-start(f32[8,64,8]{2,0,1:T(8,128)} %copy.31), calls=%async_computation.2 | async-start | bytes 524288 | tf_op jit(solution)/shard_map/all_to_all | solution.py:110
  155.7 1.1 fusion.6
  156.8 3.5 copy.30
  160.3 17.7 %all-to-all-done.2 = f32[8,64,8]{2,0,1:T(8,128)S(1)} async-done(((f32[8,64,8]{2,0,1:T(8,128)}), f32[8,64,8]{2,0,1:T(8,128)S(1)}, u32[]{:S(2)}, u32[]{:S(2)}) %all-to-all-start.2) | async-done | bytes 16416 | tf_op jit(solution)/shard_map/all_to_all | solution.py:110
  178.0 5.7 %all-to-all-start = ((f32[8,64,8,384]{3,2,0,1:T(8,128)}), f32[8,64,8,384]{3,2,0,1:T(8,128)}, u32[]{:S(2)}, u32[]{:S(2)}) async-start(f32[8,64,8,384]{3,2,0,1:T(8,128)} %copy.30), calls=%async_computation | async-start | bytes 12582912 | tf_op jit(solution)/shard_map/all_to_all | solution.py:109
  183.7 0.7 reduce_sum.78
  184.3 271.6 %all-to-all-done = f32[8,64,8,384]{3,2,0,1:T(8,128)} async-done(((f32[8,64,8,384]{3,2,0,1:T(8,128)}), f32[8,64,8,384]{3,2,0,1:T(8,128)}, u32[]{:S(2)}, u32[]{:S(2)}) %all-to-all-start) | async-done | bytes 6291488 | tf_op jit(solution)/shard_map/all_to_all | solution.py:109
  455.9 6.1 %all-to-all-start.3 = ((f32[8,1,8]{2,1,0:T(1,128)}), f32[8,1,8]{2,1,0:T(1,128)S(1)}, u32[]{:S(2)}, u32[]{:S(2)}) async-start(f32[8,1,8]{2,1,0:T(1,128)} %bitcast.3), calls=%async_computation.3 | async-start | bytes 8192 | tf_op jit(solution)/shard_map/all_to_all | solution.py:116
  462.1 3.7 reduce_sum.75
  465.8 2.7 all-to-all-done.3
  468.5 3.9 all-to-all-start.1
  472.4 0.5 reduce_sum.79
  473.0 6.3 %all-to-all-done.1 = f32[8,8,384]{2,1,0:T(8,128)S(1)} async-done(((f32[8,8,384]{2,1,0:T(8,128)}), f32[8,8,384]{2,1,0:T(8,128)S(1)}, u32[]{:S(2)}, u32[]{:S(2)}) %all-to-all-start.1) | async-done | bytes 98336 | tf_op jit(solution)/shard_map/all_to_all | solution.py:115
  479.2 0.6 reduce_sum.76
  (16 shorter events, 0.2 us)
Async XLA Ops:
  7.2 136.1 %copy-start = (bf16[128,128]{1,0:T(8,128)(2,1)S(1)}, bf16[128,128]{1,0:T(8,128)(2,1)}, u32[]{:S(2)}) copy-start(bf16[128,128]{1,0:T(8,128)(2,1)} %param.9) | copy-start | bytes 98308
  7.2 132.2 %all-gather.2.cloned.1.call-start = ((), (), s32[]{:S(2)}) async-start(), calls=%async_computation.4 | async-start | bytes 3194880 | tf_op jit(solution)/shard_map/all_gather | solution.py:92
  10.2 132.8 %copy-start.4 = (s32[128]{0:T(128)S(1)}, s32[128]{0:T(128)}, u32[]{:S(2)}) copy-start(s32[128]{0:T(128)} %param.8) | copy-start | bytes 1540
  139.4 5.3 %copy-start.3 = (bf16[4096,384]{1,0:T(8,128)(2,1)S(1)}, bf16[4096,384]{1,0:T(8,128)(2,1)}, u32[]{:S(2)}) copy-start(bf16[4096,384]{1,0:T(8,128)(2,1)} %all-gather.2.cloned.1.call-done) | copy-start | bytes 9437188
  142.5 2.2 copy-start.1
  144.7 10.9 %copy-start.2 = (f32[4096]{0:T(1024)S(1)}, f32[4096]{0:T(1024)}, u32[]{:S(2)}) copy-start(f32[4096]{0:T(1024)} %param.6) | copy-start | bytes 49156
  146.9 31.1 %all-to-all-start.2 = ((f32[8,64,8]{2,0,1:T(8,128)}), f32[8,64,8]{2,0,1:T(8,128)S(1)}, u32[]{:S(2)}, u32[]{:S(2)}) async-start(f32[8,64,8]{2,0,1:T(8,128)} %copy.31), calls=%async_computation.2 | async-start | bytes 524288 | tf_op jit(solution)/shard_map/all_to_all | solution.py:110
  178.0 277.9 %all-to-all-start = ((f32[8,64,8,384]{3,2,0,1:T(8,128)}), f32[8,64,8,384]{3,2,0,1:T(8,128)}, u32[]{:S(2)}, u32[]{:S(2)}) async-start(f32[8,64,8,384]{3,2,0,1:T(8,128)} %copy.30), calls=%async_computation | async-start | bytes 12582912 | tf_op jit(solution)/shard_map/all_to_all | solution.py:109
  455.9 12.6 %all-to-all-start.3 = ((f32[8,1,8]{2,1,0:T(1,128)}), f32[8,1,8]{2,1,0:T(1,128)S(1)}, u32[]{:S(2)}, u32[]{:S(2)}) async-start(f32[8,1,8]{2,1,0:T(1,128)} %bitcast.3), calls=%async_computation.3 | async-start | bytes 8192 | tf_op jit(solution)/shard_map/all_to_all | solution.py:116
  468.5 10.7 %all-to-all-start.1 = ((f32[8,8,384]{2,1,0:T(8,128)}), f32[8,8,384]{2,1,0:T(8,128)S(1)}, u32[]{:S(2)}, u32[]{:S(2)}) async-start(f32[8,8,384]{2,1,0:T(8,128)} %reduce_sum.75), calls=%async_computation.1 | async-start | bytes 196608 | tf_op jit(solution)/shard_map/all_to_all | solution.py:115
Sparse Core Ops, SparseCore 0:
  10.2 129.1 all-gather.1
where the time goes:
time: 496 us; the launch traced here: 487 us
  waiting for transfers between devices  428 us (86%)
  starting transfers between devices  24.6 us (5%)
  between operations  14.2 us (3%)
  other arithmetic  8.79 us (2%)
  matrix products  6.5 us (1%)
    all_to_all x1, waiting for transfers between devices, shards(): lax.all_to_all(weight_parts, 'local', split_axis=1, concat_axis=1, tiled=...  272 us
    all_gather x1, waiting for transfers between devices, shards(): whole_weight = lax.all_gather(qkv_weight, 'local', axis=0, tiled=True)  129 us
    all_to_all x1, waiting for transfers between devices, shards(): lax.all_to_all(gain_parts, 'local', split_axis=1, concat_axis=1, tiled=True)  17.7 us
  transfers between devices with their start and end apart: 5, of which 5 were waited for; matrix products, arithmetic and copies ran while one was open for 2% of the time, Pallas kernels for 0%

commit v1 on v0

--- a/solution.py
+++ b/solution.py
@@ -1,7 +1,8 @@
 import jax
 import jax.numpy as jnp
 from jax import lax
-from jax.sharding import PartitionSpec as P
+from jax.experimental import pallas as pl
+from jax.sharding import Mesh, PartitionSpec as P
 
 rope_base = 10000.0
 norm_eps = 1e-05
@@ -86,52 +87,157 @@
     return joined.astype(jnp.bfloat16)
 
 
+AXES = ("y_hi", "x", "z", "y_lo", "core")
+STEPS = 64.0
+FULL = 32767.0
+
+
+def broadcast_rows(block, count):
+    rows, width = block.shape
+    return jnp.broadcast_to(block[None], (count, rows, width)).reshape(count * rows, width)
+
+
+def swap_cores(array):
+    return lax.ppermute(array, "core", [(0, 1), (1, 0)])
+
+
+def gather_plane(qkv_weight):
+    width = qkv_weight.shape[1]
+    member = lax.axis_index("y_hi") * 4 + lax.axis_index("x")
+    part = lax.dynamic_slice(qkv_weight, (member * 8, 0), (8, width))
+    along_z = lax.all_to_all(broadcast_rows(part, 16), "z", 0, 0, tiled=True)
+    return lax.all_to_all(broadcast_rows(along_z, 16), ("y_hi", "x", "y_lo"), 0, 0, tiled=True)
+
+
+def join_weight(own, other, core):
+    width = own.shape[1]
+    first = jnp.where(core == 0, own, other).reshape(8, 2, 16, 8, width)
+    second = jnp.where(core == 0, other, own).reshape(8, 2, 16, 8, width)
+    return jnp.stack([first, second]).transpose(3, 2, 0, 1, 4, 5).reshape(4096, width)
+
+
+def split_exact(row):
+    high = lax.reduce_precision(row, 8, 7)
+    rest = row - high
+    middle = lax.reduce_precision(rest, 8, 7)
+    return jnp.concatenate([high, middle, rest - middle]).astype(jnp.bfloat16)
+
+
+def redistribute(activations, inverse_rms, x_index, core):
+    tokens = activations.shape[0]
+    extra = split_exact(inverse_rms.reshape(1, tokens))
+    extra = jnp.tile(jnp.pad(extra, ((0, 13), (0, 0))), (1, 4))[None]
+    extra = jnp.concatenate([extra, extra])
+    ordered = jnp.zeros((4, 2, tokens + 16, 512), jnp.bfloat16)
+    for shift in range(4):
+        column = lax.rem(x_index + shift, 4) * 512
+        block = jnp.stack([lax.dynamic_slice(activations, (0, column + h * 2048), (tokens, 512)) for h in range(2)])
+        block = jnp.concatenate([block, extra], axis=1)
+        if shift:
+            block = lax.ppermute(block, "x", [(i, (i + shift) % 4) for i in range(4)])
+        ordered = lax.dynamic_update_slice(ordered, block[None], (lax.rem(x_index - shift + 4, 4), 0, 0, 0))
+    first, second = ordered[..., :256], ordered[..., 256:]
+    kept = jnp.where(core == 0, first, second)
+    sent = jnp.where(core == 0, second, first)
+    return kept, swap_cores(sent)
+
+
+def scaled(block, gain_part):
+    tokens = block.shape[2] - 16
+    high, middle, low = (block[:, 0, tokens + k, :tokens].astype(jnp.float32) for k in range(3))
+    inverse_rms = ((high + middle) + low)[:, None, :, None]
+    unit = block[:, :, :tokens].astype(jnp.float32) * inverse_rms
+    normed = (unit * gain_part.reshape(1, 2, 1, 256)).astype(jnp.bfloat16)
+    return normed, unit
+
+
+def code_kernel(parts_ref, coded_ref):
+    sums = (parts_ref[0] + parts_ref[1]) + (parts_ref[2] + parts_ref[3])
+    rows = sums[:, :64].reshape(16, 8, 384)
+    gains = sums[:, 64:65, :128]
+    peak = jnp.max(jnp.abs(rows), axis=1, keepdims=True)
+    step = jnp.clip(jnp.ceil(jnp.log2(peak) * STEPS), -110 * STEPS, 127 * STEPS)
+    coded = jnp.clip(jnp.round(rows * (jnp.exp2(step * (-1 / STEPS)) * FULL)), -FULL, FULL)
+    gain_peak = jnp.max(jnp.abs(gains), axis=2, keepdims=True)
+    gain_step = jnp.clip(jnp.ceil(jnp.log2(gain_peak) * STEPS), -110 * STEPS, 127 * STEPS)
+    scaled_gains = gains * (jnp.exp2(gain_step * (-1 / STEPS)) * FULL)
+    high = jnp.clip(jnp.round(scaled_gains), -FULL, FULL)
+    low = jnp.clip(jnp.round((scaled_gains - high) * FULL), -FULL, FULL)
+    shown = [jnp.broadcast_to(v[:, None], (2, 8, 1, 128)).reshape(16, 1, 128) for v in (high, low, jnp.broadcast_to(gain_step, (2, 1, 128)))]
+    extra = jnp.concatenate(
+        [step[:, :, :128], step[:, :, 128:256], step[:, :, 256:]] + shown + [jnp.zeros((16, 2, 128), jnp.float32)], axis=1
+    )
+    whole = jnp.concatenate([coded, extra], axis=2).reshape(128, 512)
+    coded_ref[...] = whole.astype(jnp.int32).astype(jnp.int16)
+
+
+def decode_kernel(coded_ref, rows_ref, gains_ref):
+    whole = coded_ref[...].astype(jnp.int32).astype(jnp.float32).reshape(16, 8, 512)
+    extra = whole[:, :, 384:]
+    step = jnp.concatenate([extra[:, 0:1], extra[:, 1:2], extra[:, 2:3]], axis=2)
+    rows_ref[...] = jnp.sum(whole[:, :, :384] * (jnp.exp2(step * (1 / STEPS)) * (1 / FULL)), axis=0)
+    scale = jnp.exp2(extra[:, 5:6] * (1 / STEPS)) * (1 / FULL)
+    gains_ref[...] = jnp.sum((extra[:, 3:4] + extra[:, 4:5] * (1 / FULL)) * scale, axis=0)
+
+
 def shards(activations, norm_gain, qkv_weight, positions, cotangent):
-    normed, inverse_rms, widened = normalize(activations, norm_gain)
-    proj_width = qkv_weight.shape[1]
-    whole_weight = lax.all_gather(qkv_weight, "local", axis=0, tiled=True)
-    projected = jnp.dot(normed, whole_weight, preferred_element_type=jnp.float32)
+    x_index = lax.axis_index("x")
+    core = lax.axis_index("core")
+    width = qkv_weight.shape[1]
+    tokens = activations.shape[0]
+    normed, inverse_rms, _ = normalize(activations, norm_gain)
+    own_weight = gather_plane(qkv_weight)
+    kept, received = redistribute(activations, inverse_rms, x_index, core)
+    gain_part = lax.dynamic_slice(norm_gain.reshape(2, 8, 256), (0, x_index * 2 + core, 0), (2, 1, 256)).reshape(512)
+    kept = scaled(kept, gain_part)
+    received = scaled(received, gain_part)
+    own_weight, normed, kept, received = lax.optimization_barrier((own_weight, normed, kept, received))
+
+    weight = join_weight(own_weight, swap_cores(own_weight), core)
+    projected = jnp.dot(normed, weight, preferred_element_type=jnp.float32)
     qkv_grads = attention_grads(projected, positions, cotangent)
-    weight_term = lax.dot_general(
-        normed, qkv_grads, (((0,), (0,)), ((), ())), preferred_element_type=jnp.float32
-    )
-    normed_grad = lax.dot_general(
-        qkv_grads, whole_weight, (((1,), (1,)), ((), ())), preferred_element_type=jnp.float32
-    )
-    gain_term = jnp.sum(normed_grad * widened * inverse_rms, axis=0)
-    island_count = lax.axis_size("island")
-    local_count = lax.axis_size("local")
-    full_rows = weight_term.shape[0]
-    row_count = full_rows // (island_count * local_count)
-    weight_parts = weight_term.reshape(island_count, local_count, row_count, proj_width)
-    gain_parts = gain_term.reshape(island_count, local_count, row_count)
-    received = (
-        lax.all_to_all(weight_parts, "local", split_axis=1, concat_axis=1, tiled=True),
-        lax.all_to_all(gain_parts, "local", split_axis=1, concat_axis=1, tiled=True),
-    )
-    weight_sums = jnp.sum(received[0], axis=1)
-    gain_sums = jnp.sum(received[1], axis=1)
-    second = (
-        lax.all_to_all(weight_sums, "island", split_axis=0, concat_axis=0, tiled=True),
-        lax.all_to_all(gain_sums, "island", split_axis=0, concat_axis=0, tiled=True),
-    )
-    qkv_share = jnp.sum(second[0], axis=0)
-    gain_share = jnp.sum(second[1], axis=0)
-    return (qkv_share, gain_share)
+    weight_rows = lax.dynamic_slice(weight.reshape(2, 8, 256, width), (0, x_index * 2 + core, 0, 0), (2, 1, 256, width)).reshape(2, 256, width)
+
+    own_grads = lax.all_to_all(broadcast_rows(qkv_grads, 4), "x", 0, 0, tiled=True)
+    other_grads = swap_cores(own_grads)
+
+    weight_term, gain_term = 0.0, 0.0
+    for (block_normed, block_unit), grads in ((kept, own_grads), (received, other_grads)):
+        grads = grads.reshape(4, tokens, width)
+        weight_term += jnp.einsum("xhtd,xtj->hdj", block_normed, grads, preferred_element_type=jnp.float32)
+        normed_grad = jnp.einsum("xtj,hdj->xhtd", grads, weight_rows, preferred_element_type=jnp.float32)
+        gain_term += jnp.sum(normed_grad * block_unit, axis=(0, 2))
+
+    parts = weight_term.reshape(2, 8, 2, 2, 8, width).transpose(0, 2, 3, 1, 4, 5).reshape(8, 64, width)
+    gains = gain_term.reshape(2, 8, 2, 2, 8).transpose(0, 2, 3, 1, 4).reshape(8, 1, 64)
+    parts = jnp.concatenate([parts, jnp.pad(gains, ((0, 0), (0, 7), (0, width - 64)))], axis=1)
+    parts = lax.all_to_all(parts, ("y_hi", "y_lo", "core"), 0, 0, tiled=True)
+    coded = pl.pallas_call(
+        code_kernel, out_shape=jax.ShapeDtypeStruct((128, 512), jnp.int16), name="code_rows"
+    )(parts.reshape(4, 2, 72, width))
+    coded = lax.all_to_all(coded, "z", 0, 0, tiled=True)
+    share, gains = pl.pallas_call(
+        decode_kernel,
+        out_shape=(jax.ShapeDtypeStruct((8, width), jnp.float32), jax.ShapeDtypeStruct((1, 128), jnp.float32)),
+        name="decode_rows",
+    )(coded)
+    place = lax.rem(lax.axis_index("z"), 8) * 8
+    return share, lax.dynamic_slice(gains, (0, place), (1, 8)).reshape(8)
 
 
 def solution(mesh):
+    fine = Mesh(mesh.devices.reshape(2, 4, 16, 2, 2), AXES)
     placed = (
-        P(("island", "local"), None),
+        P(AXES, None),
         P(),
-        P("local", None),
-        P(("island", "local")),
-        P(("island", "local"), None),
+        P(("z", "y_lo", "core"), None),
+        P(AXES),
+        P(AXES, None),
     )
     return jax.shard_map(
         shards,
-        mesh=mesh,
+        mesh=fine,
         in_specs=placed,
-        out_specs=(P(("island", "local"), None), P(("island", "local"))),
+        out_specs=(P(AXES, None), P(AXES)),
         check_vma=False,
     )

time: 496 us -> 139 us (0.28); the launches traced: 487 us -> 137 us
  waiting for transfers between devices: 428 us -> 37.8 us
  blocking collectives: 0 us -> 27.3 us
  starting transfers between devices: 24.6 us -> 49 us
  between operations: 14.2 us -> 1.23 us
    all_to_all x4 -> x3, waiting for transfers between devices: 298 us -> 34.3 us  [the longest x1 13.1 us: gather_plane(): lax.all_to_all(broadcast_rows(along_z, 16), ('y_hi', 'x', 'y_lo'), 0, 0,...]
    all_gather x1 -> x0, waiting for transfers between devices: 129 us -> none  [shards(): whole_weight = lax.all_gather(qkv_weight, 'local', axis=0, tiled=True)]
    all_to_all x0 -> x2, blocking collectives: none -> 27.3 us  [the longest x1 17 us: shards(): parts = lax.all_to_all(parts, ('y_hi', 'y_lo', 'core'), 0, 0, tiled=True)]
    ppermute x0 -> x6, starting transfers between devices: none -> 26.1 us  [the longest x3 14.7 us: swap_cores(): return lax.ppermute(array, 'core', [(0, 1), (1, 0)])]
    reduce_sum x4 -> x0, other arithmetic: 5.53 us -> none  [the longest x1 3.72 us: shards(): weight_sums = jnp.sum(received[0], axis=1)]
    all_to_all x4 -> x3, starting transfers between devices: 24.5 us -> 22.9 us  [the longest x1 14.9 us: gather_plane(): along_z = lax.all_to_all(broadcast_rows(part, 16), 'z', 0, 0, tiled=True)]
  transfers between devices with their start and end apart: 5 -> 9, of which waited for: 5 -> 6; matrix products, arithmetic and copies ran while one was open for 2% -> 5% of each run, Pallas kernels for 0% -> 0%
where the time goes in v1:
time: 139 us; the launch traced here: 137 us
  starting transfers between devices  49 us (35%)
  waiting for transfers between devices  37.8 us (27%)
  blocking collectives  27.3 us (20%)
  other arithmetic  7.38 us (5%)
  local copies, waits for them, and re-layouts  6.78 us (5%)
  matrix products  3.77 us (3%)
  Pallas kernels  3.6 us (3%)
    all_to_all x1, blocking collectives, shards(): parts = lax.all_to_all(parts, ('y_hi', 'y_lo', 'core'), 0, 0, tiled=True)  17 us
    all_to_all x1, starting transfers between devices, gather_plane(): along_z = lax.all_to_all(broadcast_rows(part, 16), 'z', 0, 0, tiled=True)  14.9 us
    ppermute x3, starting transfers between devices, swap_cores(): return lax.ppermute(array, 'core', [(0, 1), (1, 0)])  14.7 us
    all_to_all x1, waiting for transfers between devices, gather_plane(): lax.all_to_all(broadcast_rows(along_z, 16), ('y_hi', 'x', 'y_lo'), 0, 0,...  13.1 us
    all_to_all x1, waiting for transfers between devices, shards(): coded = lax.all_to_all(coded, 'z', 0, 0, tiled=True)  12 us
    ppermute x3, starting transfers between devices, redistribute(): block = lax.ppermute(block, 'x', [(i, (i + shift) % 4) for i in range(4)])  11.4 us
    all_to_all x1, blocking collectives, shards(): lax.all_to_all(broadcast_rows(qkv_grads, 4), 'x', 0, 0, tiled=True)  10.4 us
    all_to_all x1, waiting for transfers between devices, gather_plane(): along_z = lax.all_to_all(broadcast_rows(part, 16), 'z', 0, 0, tiled=True)  9.29 us
  transfers between devices with their start and end apart: 9, of which 6 were waited for; matrix products, arithmetic and copies ran while one was open for 5% of the time, Pallas kernels for 0%

profile of v1, /device:TPU:1, one launch (start us, length us, event | category | flops | bytes accessed | tf_op | source)
XLA Modules:
  0.0 136.9 jit_solution(763201471643611261)
XLA Ops:
  0.7 1.6 %fusion = f32[128]{0:T(128)S(1)} fusion(bf16[128,4096]{1,0:T(8,128)(2,1)} %param.5), kind=kLoop, calls=%fused_computation.3 | loop fusion | flops 1572736 | bytes 1049088 | tf_op jit(solution)/shard_map/reduce_sum | solution.py:35
  2.6 1.0 pad_maximum_fusion
  3.6 3.9 %collective-permute-start = (bf16[2,144,512]{2,1,0:T(8,128)(2,1)}, bf16[2,144,512]{2,1,0:T(8,128)(2,1)}, u32[]{:S(2)}, u32[]{:S(2)}) collective-permute-start(bf16[2,144,512]{2,1,0:T(8,128)(2,1)} %get-tuple-element.49), channel_id=1, source_target_pairs={{0,64},{64,128},{128,192},{192,0},{1,65},{65,129},{129,193},{193,1... | collective-permute-start | bytes 884744 | tf_op jit(solution)/shard_map/ppermute | solution.py:137
  7.5 4.4 %collective-permute-start.1 = (bf16[2,144,512]{2,1,0:T(8,128)(2,1)}, bf16[2,144,512]{2,1,0:T(8,128)(2,1)S(1)}, u32[]{:S(2)}, u32[]{:S(2)}) collective-permute-start(bf16[2,144,512]{2,1,0:T(8,128)(2,1)} %get-tuple-element.50), channel_id=1, source_target_pairs={{0,128},{64,192},{128,0},{192,64},{1,129},{65,193},{129,1},{193,65... | collective-permute-start | bytes 884744 | tf_op jit(solution)/shard_map/ppermute | solution.py:137
  11.9 3.1 %collective-permute-start.2 = (bf16[2,144,512]{2,1,0:T(8,128)(2,1)}, bf16[2,144,512]{2,1,0:T(8,128)(2,1)S(1)}, u32[]{:S(2)}, u32[]{:S(2)}) collective-permute-start(bf16[2,144,512]{2,1,0:T(8,128)(2,1)} %get-tuple-element.48), channel_id=1, source_target_pairs={{0,192},{64,0},{128,64},{192,128},{1,193},{65,1},{129,65},{193,129... | collective-permute-start | bytes 884744 | tf_op jit(solution)/shard_map/ppermute | solution.py:137
  15.0 0.7 broadcast_in_dim.21
  15.7 14.9 %all-to-all-start = ((bf16[16,8,384]{2,1,0:T(8,128)(2,1)}), bf16[16,8,384]{2,1,0:T(8,128)(2,1)S(1)}, u32[]{:S(2)}, u32[]{:S(2)}) async-start(bf16[16,8,384]{2,1,0:T(8,128)(2,1)} %broadcast_in_dim.21), calls=%async_computation | async-start | bytes 196608 | tf_op jit(solution)/shard_map/all_to_all | solution.py:108
  30.6 1.3 fusion.2
  32.1 1.0 bitcast_dynamic-update-slice_fusion.2
  33.1 9.3 %all-to-all-done = bf16[16,8,384]{2,1,0:T(8,128)(2,1)S(1)} async-done(((bf16[16,8,384]{2,1,0:T(8,128)(2,1)}), bf16[16,8,384]{2,1,0:T(8,128)(2,1)S(1)}, u32[]{:S(2)}, u32[]{:S(2)}) %all-to-all-start) | async-done | bytes 98336 | tf_op jit(solution)/shard_map/all_to_all | solution.py:108
  42.4 1.4 %broadcast_in_dim.24 = bf16[16,128,384]{2,1,0:T(8,128)(2,1)} broadcast(bf16[128,384]{1,0:T(8,128)(2,1)S(1)} %bitcast.127), dimensions={1,2} | broadcast | bytes 1671168 | tf_op jit(solution)/shard_map/broadcast_in_dim | solution.py:97
  43.8 4.3 %all-to-all-start.1 = ((bf16[16,128,384]{2,1,0:T(8,128)(2,1)}), bf16[16,128,384]{2,1,0:T(8,128)(2,1)S(1)}, u32[]{:S(2)}, u32[]{:S(2)}) async-start(bf16[16,128,384]{2,1,0:T(8,128)(2,1)} %broadcast_in_dim.24), calls=%async_computation.1 | async-start | bytes 3145728 | tf_op jit(solution)/shard_map/all_to_all | solution.py:109
  48.3 5.2 %collective-permute-start.3 = (bf16[4,2,144,256]{3,2,0,1:T(8,128)(2,1)S(1)}, bf16[4,2,144,256]{3,2,0,1:T(8,128)(2,1)S(1)}, u32[]{:S(2)}, u32[]{:S(2)}) collective-permute-start(bf16[4,2,144,256]{3,2,0,1:T(8,128)(2,1)S(1)} %get-tuple-element.22), channel_id=1, source_target_pairs={{0,1},{1,0},{2,3},{3,2},{4,5},{5,4},{6,7},{7,6},{8,9},{9,8},{10,11... | collective-permute-start | bytes 1769480 | tf_op jit(solution)/shard_map/ppermute | solution.py:101
  53.6 1.4 convert_multiply_fusion.3
  55.4 13.1 %all-to-all-done.1 = bf16[16,128,384]{2,1,0:T(8,128)(2,1)S(1)} async-done(((bf16[16,128,384]{2,1,0:T(8,128)(2,1)}), bf16[16,128,384]{2,1,0:T(8,128)(2,1)S(1)}, u32[]{:S(2)}, u32[]{:S(2)}) %all-to-all-start.1) | async-done | bytes 1572896 | tf_op jit(solution)/shard_map/all_to_all | solution.py:109
  68.4 6.4 %collective-permute-start.4 = (bf16[2048,384]{1,0:T(8,128)(2,1)S(1)}, bf16[2048,384]{1,0:T(8,128)(2,1)S(1)}, u32[]{:S(2)}, u32[]{:S(2)}) collective-permute-start(bf16[2048,384]{1,0:T(8,128)(2,1)S(1)} %bitcast.115), channel_id=1, source_target_pairs={{0,1},{1,0},{2,3},{3,2},{4,5},{5,4},{6,7},{7,6},{8,9},{9,8},{10,11... | collective-permute-start | bytes 4718600 | tf_op jit(solution)/shard_map/ppermute | solution.py:101
  74.8 3.0 %collective-permute-done.4 = bf16[2048,384]{1,0:T(8,128)(2,1)S(1)} collective-permute-done((bf16[2048,384]{1,0:T(8,128)(2,1)S(1)}, bf16[2048,384]{1,0:T(8,128)(2,1)S(1)}, u32[]{:S(2)}, u32[]{:S(2)}) %collective-permute-start.4) | collective-permute-done | bytes 1572896 | tf_op jit(solution)/shard_map/ppermute | solution.py:101
  78.5 0.6 copy.23
  79.0 0.6 copy-done.3
  79.7 0.7 fusion.48
  82.7 10.4 %all_to_all.40 = bf16[4,128,384]{2,1,0:T(8,128)(2,1)S(1)} all-to-all(bf16[4,128,384]{2,1,0:T(8,128)(2,1)S(1)} %broadcast_in_dim.60), channel_id=1, replica_groups=mesh['y_hi'=2,'x'=4,'z'=16,'y_lo'=2,'core'=2] {'x'}, dimensions={0} | all-to-all | bytes 786432 | tf_op jit(solution)/shard_map/all_to_all | solution.py:201
  93.0 3.1 %collective-permute-start.5 = (bf16[512,384]{1,0:T(8,128)(2,1)S(1)}, bf16[512,384]{1,0:T(8,128)(2,1)S(1)}, u32[]{:S(2)}, u32[]{:S(2)}) collective-permute-start(bf16[512,384]{1,0:T(8,128)(2,1)S(1)} %bitcast.120), channel_id=1, source_target_pairs={{0,1},{1,0},{2,3},{3,2},{4,5},{5,4},{6,7},{7,6},{8,9},{9,8},{10,11... | collective-permute-start | bytes 1179656 | tf_op jit(solution)/shard_map/ppermute | solution.py:101
  96.1 0.5 convolution_bitcast_fusion.3
  96.6 0.5 fusion.6
  98.0 0.5 fusion.7
  98.8 17.0 %all_to_all.41 = f32[8,72,384]{2,1,0:T(8,128)} all-to-all(f32[8,72,384]{2,1,0:T(8,128)S(1)} %select_maximum_fusion), channel_id=1, replica_groups=mesh['y_hi'=2,'x'=4,'z'=16,'y_lo'=2,'core'=2] {'y_hi','y_lo','core'}, dimensions={0} | all-to-all | bytes 1769472 | tf_op jit(solution)/shard_map/all_to_all | solution.py:214
  115.7 2.0 %code_rows.1 = s16[128,512]{1,0:T(8,128)(2,1)} custom-call(f32[4,2,72,384]{3,2,1,0:T(8,128)} %bitcast.119), custom_call_target="tpu_custom_call" | custom-call | tf_op jit(solution)/shard_map/code_rows/pallas_call | solution.py:215
  117.7 3.7 %all-to-all-start.4 = ((s16[16,8,512]{2,1,0:T(8,128)(2,1)}), s16[16,8,512]{2,1,0:T(8,128)(2,1)S(1)}, u32[]{:S(2)}, u32[]{:S(2)}) async-start(s16[16,8,512]{2,1,0:T(8,128)(2,1)} %bitcast.126), calls=%async_computation.4 | async-start | bytes 262144 | tf_op jit(solution)/shard_map/all_to_all | solution.py:218
  121.4 12.0 %all-to-all-done.4 = s16[16,8,512]{2,1,0:T(8,128)(2,1)S(1)} async-done(((s16[16,8,512]{2,1,0:T(8,128)(2,1)}), s16[16,8,512]{2,1,0:T(8,128)(2,1)S(1)}, u32[]{:S(2)}, u32[]{:S(2)}) %all-to-all-start.4) | async-done | bytes 131104 | tf_op jit(solution)/shard_map/all_to_all | solution.py:218
  133.4 0.6 copy-done.5
  134.1 1.6 %decode_rows.1 = (f32[8,384]{1,0:T(8,128)}, f32[1,128]{1,0:T(1,128)}) custom-call(s16[128,512]{1,0:T(8,128)(2,1)} %bitcast.125), custom_call_target="tpu_custom_call" | custom-call | tf_op jit(solution)/shard_map/decode_rows/pallas_call | solution.py:219
  135.6 1.3 fusion.43
  (66 shorter events, 4.9 us)
Async XLA Ops:
  0.6 14.3 %copy-start = (bf16[64,384]{1,0:T(8,128)(2,1)S(1)}, bf16[64,384]{1,0:T(8,128)(2,1)}, u32[]{:S(2)}) copy-start(bf16[64,384]{1,0:T(8,128)(2,1)} %param.7) | copy-start | bytes 147460
  0.6 1.8 %copy-start.1 = (bf16[128,4096]{1,0:T(8,128)(2,1)S(1)}, bf16[128,4096]{1,0:T(8,128)(2,1)}, u32[]{:S(2)}) copy-start(bf16[128,4096]{1,0:T(8,128)(2,1)} %param.5) | copy-start | bytes 3145732
  2.4 28.2 %copy-start.6 = (f32[4096]{0:T(1024)S(1)}, f32[4096]{0:T(1024)}, u32[]{:S(2)}) copy-start(f32[4096]{0:T(1024)} %param.6) | copy-start | bytes 49156
  3.6 28.5 %collective-permute-start = (bf16[2,144,512]{2,1,0:T(8,128)(2,1)}, bf16[2,144,512]{2,1,0:T(8,128)(2,1)}, u32[]{:S(2)}, u32[]{:S(2)}) collective-permute-start(bf16[2,144,512]{2,1,0:T(8,128)(2,1)} %get-tuple-element.49), channel_id=1, source_target_pairs={{0,64},{64,128},{128,192},{192,0},{1,65},{65,129},{129,193},{193,1... | collective-permute-start | bytes 884744 | tf_op jit(solution)/shard_map/ppermute | solution.py:137
  7.5 25.6 %collective-permute-start.1 = (bf16[2,144,512]{2,1,0:T(8,128)(2,1)}, bf16[2,144,512]{2,1,0:T(8,128)(2,1)S(1)}, u32[]{:S(2)}, u32[]{:S(2)}) collective-permute-start(bf16[2,144,512]{2,1,0:T(8,128)(2,1)} %get-tuple-element.50), channel_id=1, source_target_pairs={{0,128},{64,192},{128,0},{192,64},{1,129},{65,193},{129,1},{193,65... | collective-permute-start | bytes 884744 | tf_op jit(solution)/shard_map/ppermute | solution.py:137
  11.9 36.3 %collective-permute-start.2 = (bf16[2,144,512]{2,1,0:T(8,128)(2,1)}, bf16[2,144,512]{2,1,0:T(8,128)(2,1)S(1)}, u32[]{:S(2)}, u32[]{:S(2)}) collective-permute-start(bf16[2,144,512]{2,1,0:T(8,128)(2,1)} %get-tuple-element.48), channel_id=1, source_target_pairs={{0,192},{64,0},{128,64},{192,128},{1,193},{65,1},{129,65},{193,129... | collective-permute-start | bytes 884744 | tf_op jit(solution)/shard_map/ppermute | solution.py:137
  15.7 26.8 %all-to-all-start = ((bf16[16,8,384]{2,1,0:T(8,128)(2,1)}), bf16[16,8,384]{2,1,0:T(8,128)(2,1)S(1)}, u32[]{:S(2)}, u32[]{:S(2)}) async-start(bf16[16,8,384]{2,1,0:T(8,128)(2,1)} %broadcast_in_dim.21), calls=%async_computation | async-start | bytes 196608 | tf_op jit(solution)/shard_map/all_to_all | solution.py:108
  43.8 24.6 %all-to-all-start.1 = ((bf16[16,128,384]{2,1,0:T(8,128)(2,1)}), bf16[16,128,384]{2,1,0:T(8,128)(2,1)S(1)}, u32[]{:S(2)}, u32[]{:S(2)}) async-start(bf16[16,128,384]{2,1,0:T(8,128)(2,1)} %broadcast_in_dim.24), calls=%async_computation.1 | async-start | bytes 3145728 | tf_op jit(solution)/shard_map/all_to_all | solution.py:109
  48.3 6.9 %collective-permute-start.3 = (bf16[4,2,144,256]{3,2,0,1:T(8,128)(2,1)S(1)}, bf16[4,2,144,256]{3,2,0,1:T(8,128)(2,1)S(1)}, u32[]{:S(2)}, u32[]{:S(2)}) collective-permute-start(bf16[4,2,144,256]{3,2,0,1:T(8,128)(2,1)S(1)} %get-tuple-element.22), channel_id=1, source_target_pairs={{0,1},{1,0},{2,3},{3,2},{4,5},{5,4},{6,7},{7,6},{8,9},{9,8},{10,11... | collective-permute-start | bytes 1769480 | tf_op jit(solution)/shard_map/ppermute | solution.py:101
  54.9 19.9 %copy-start.8 = (s32[128]{0:T(128)S(1)}, s32[128]{0:T(128)}, u32[]{:S(2)}) copy-start(s32[128]{0:T(128)} %param.8) | copy-start | bytes 1540
  68.4 9.4 %collective-permute-start.4 = (bf16[2048,384]{1,0:T(8,128)(2,1)S(1)}, bf16[2048,384]{1,0:T(8,128)(2,1)S(1)}, u32[]{:S(2)}, u32[]{:S(2)}) collective-permute-start(bf16[2048,384]{1,0:T(8,128)(2,1)S(1)} %bitcast.115), channel_id=1, source_target_pairs={{0,1},{1,0},{2,3},{3,2},{4,5},{5,4},{6,7},{7,6},{8,9},{9,8},{10,11... | collective-permute-start | bytes 4718600 | tf_op jit(solution)/shard_map/ppermute | solution.py:101
  78.5 1.2 copy-start.3
  79.7 1.4 %copy-start.7 = (bf16[128,128]{1,0:T(8,128)(2,1)S(1)}, bf16[128,128]{1,0:T(8,128)(2,1)}, u32[]{:S(2)}) copy-start(bf16[128,128]{1,0:T(8,128)(2,1)} %param.9) | copy-start | bytes 98308
  81.4 14.7 %copy-start.4 = (bf16[4,2,128,256]{3,2,0,1:T(8,128)(2,1)S(1)}, bf16[4,2,128,256]{3,2,0,1:T(8,128)(2,1)}, u32[]{:S(2)}) copy-start(bf16[4,2,128,256]{3,2,0,1:T(8,128)(2,1)} %get-tuple-element.10) | copy-start | bytes 1572868
  82.6 14.0 %copy-start.2 = (f32[4,2,128,256]{3,2,0,1:T(8,128)S(1)}, f32[4,2,128,256]{3,2,0,1:T(8,128)}, u32[]{:S(2)}) copy-start(f32[4,2,128,256]{3,2,0,1:T(8,128)} %get-tuple-element.14) | copy-start | bytes 3145732
  93.0 4.4 %collective-permute-start.5 = (bf16[512,384]{1,0:T(8,128)(2,1)S(1)}, bf16[512,384]{1,0:T(8,128)(2,1)S(1)}, u32[]{:S(2)}, u32[]{:S(2)}) collective-permute-start(bf16[512,384]{1,0:T(8,128)(2,1)S(1)} %bitcast.120), channel_id=1, source_target_pairs={{0,1},{1,0},{2,3},{3,2},{4,5},{5,4},{6,7},{7,6},{8,9},{9,8},{10,11... | collective-permute-start | bytes 1179656 | tf_op jit(solution)/shard_map/ppermute | solution.py:101
  117.7 15.7 %all-to-all-start.4 = ((s16[16,8,512]{2,1,0:T(8,128)(2,1)}), s16[16,8,512]{2,1,0:T(8,128)(2,1)S(1)}, u32[]{:S(2)}, u32[]{:S(2)}) async-start(s16[16,8,512]{2,1,0:T(8,128)(2,1)} %bitcast.126), calls=%async_computation.4 | async-start | bytes 262144 | tf_op jit(solution)/shard_map/all_to_all | solution.py:218
  133.4 0.6 copy-start.5

commit v2 on v1

v2 whole, which is shorter than its diff:
```python
import jax
import jax.numpy as jnp
from jax import lax
from jax.experimental import pallas as pl
from jax.experimental.pallas import tpu as pltpu
from jax.sharding import Mesh, PartitionSpec as P

rope_base = 10000.0
norm_eps = 1e-05


def rope_tables(positions, head_size):
    half_width = head_size // 2
    exponent = jnp.arange(half_width, dtype=jnp.float32) * (-2.0 / head_size)
    frequency = jnp.power(jnp.float32(rope_base), exponent)
    angle_table = positions.astype(jnp.float32)[:, None] * frequency[None, :]
    angle_table = jnp.concatenate([angle_table, angle_table], axis=1)
    return (jnp.cos(angle_table), jnp.sin(angle_table))


def rotate(vectors, cosine_table, sine_table):
    half_width = vectors.shape[1] // 2
    turned = jnp.concatenate([-vectors[:, half_width:], vectors[:, :half_width]], axis=1)
    return vectors * cosine_table + turned * sine_table


def unrotate(gradient, cosine_table, sine_table):
    half_width = gradient.shape[1] // 2
    sined = gradient * sine_table
    turned = jnp.concatenate([sined[:, half_width:], -sined[:, :half_width]], axis=1)
    return gradient * cosine_table + turned


def normalize(activations, norm_gain):
    widened = activations.astype(jnp.float32)
    inverse_rms = lax.rsqrt(jnp.mean(widened * widened, axis=1, keepdims=True) + norm_eps)
    normed = (widened * inverse_rms * norm_gain[None, :]).astype(jnp.bfloat16)
    return (normed, inverse_rms, widened)


def attention_grads(projected, positions, cotangent):
    head_size = cotangent.shape[1]
    cosine_table, sine_table = rope_tables(positions, head_size)
    queries = rotate(projected[:, :head_size], cosine_table, sine_table).astype(jnp.bfloat16)
    keys_rot = rotate(projected[:, head_size : 2 * head_size], cosine_table, sine_table).astype(
        jnp.bfloat16
    )
    values = projected[:, 2 * head_size :].astype(jnp.bfloat16)
    score_scale = head_size ** (-0.5)
    scores = (
        lax.dot_general(
            queries, keys_rot, (((1,), (1,)), ((), ())), preferred_element_type=jnp.float32
        )
        * score_scale
    )
    token_count = positions.shape[0]
    row_index = jnp.arange(token_count, dtype=jnp.int32)[:, None]
    column_index = jnp.arange(token_count, dtype=jnp.int32)[None, :]
    visible = (column_index <= row_index) & (row_index - column_index <= positions[:, None])
    scores = jnp.where(visible, scores, -jnp.inf)
    row_peak = jnp.max(scores, axis=1, keepdims=True)
    exp_terms = jnp.exp(scores - row_peak)
    attention = exp_terms / jnp.sum(exp_terms, axis=1, keepdims=True)
    attention_low = attention.astype(jnp.bfloat16)
    prob_grad = lax.dot_general(
        cotangent, values, (((1,), (1,)), ((), ())), preferred_element_type=jnp.float32
    )
    score_grad = (
        attention
        * (prob_grad - jnp.sum(attention * prob_grad, axis=1, keepdims=True))
        * score_scale
    ).astype(jnp.bfloat16)
    query_grad = jnp.dot(score_grad, keys_rot, preferred_element_type=jnp.float32)
    key_grad = lax.dot_general(
        score_grad, queries, (((0,), (0,)), ((), ())), preferred_element_type=jnp.float32
    )
    value_grad = lax.dot_general(
        attention_low, cotangent, (((0,), (0,)), ((), ())), preferred_element_type=jnp.float32
    )
    joined = jnp.concatenate(
        [
            unrotate(query_grad, cosine_table, sine_table),
            unrotate(key_grad, cosine_table, sine_table),
            value_grad,
        ],
        axis=1,
    )
    return joined.astype(jnp.bfloat16)


AXES = ("y_hi", "x", "z", "y_lo", "core")
STEPS = 64.0
SMALL = pltpu.CompilerParams(vmem_limit_bytes=8 * 2**20)
FULL = 32767.0


def broadcast_rows(block, count):
    rows, width = block.shape
    return jnp.broadcast_to(block[None], (count, rows, width)).reshape(count * rows, width)


def swap_cores(array):
    return lax.ppermute(array, "core", [(0, 1), (1, 0)])


def gather_plane(qkv_weight):
    width = qkv_weight.shape[1]
    member = lax.axis_index("y_hi") * 4 + lax.axis_index("x")
    part = lax.dynamic_slice(qkv_weight, (member * 8, 0), (8, width))
    along_z = lax.all_to_all(broadcast_rows(part, 16), "z", 0, 0, tiled=True)
    return along_z, lax.all_to_all(broadcast_rows(along_z, 16), ("y_hi", "x", "y_lo"), 0, 0, tiled=True)


def join_weight(own, core):
    width = own.shape[1]
    other = swap_cores(own)
    weight = jnp.zeros((16, 2, 2, 8, 8, width), own.dtype)
    for block, side in ((own, core), (other, 1 - core)):
        block = block.reshape(8, 2, 16, 8, width).transpose(2, 1, 0, 3, 4)
        weight = lax.dynamic_update_slice(weight, block[:, :, None], (0, 0, side, 0, 0, 0))
    return weight.reshape(4096, width)


def split_exact(row):
    high = lax.reduce_precision(row, 8, 7)
    rest = row - high
    middle = lax.reduce_precision(rest, 8, 7)
    return jnp.concatenate([high, middle, rest - middle]).astype(jnp.bfloat16)


def redistribute(activations, inverse_rms, x_index, core, after):
    tokens = activations.shape[0]
    extra = split_exact(inverse_rms.reshape(1, tokens))
    extra = jnp.tile(jnp.pad(extra, ((0, 13), (0, 0))), (1, 4))[None]
    extra = jnp.concatenate([extra, extra])
    blocks = []
    for shift in range(4):
        column = lax.rem(x_index + shift, 4) * 512
        block = jnp.stack([lax.dynamic_slice(activations, (0, column + h * 2048), (tokens, 512)) for h in range(2)])
        block = jnp.concatenate([block, extra], axis=1)
        if shift:
            block = lax.ppermute(block, "x", [(i, (i + shift) % 4) for i in range(4)])
        blocks.append(block)
    ordered = jnp.broadcast_to(after[:1, :1].reshape(1, 1, 1, 1), (4, 2, tokens + 16, 512))
    for shift, block in enumerate(blocks):
        ordered = lax.dynamic_update_slice(ordered, block[None], (lax.rem(x_index - shift + 4, 4), 0, 0, 0))
    first, second = ordered[..., :256], ordered[..., 256:]
    kept = jnp.where(core == 0, first, second)
    sent = jnp.where(core == 0, second, first)
    return kept, swap_cores(sent)


def prepare_kernel(block_ref, gain_ref, normed_ref, unit_ref):
    for x in range(4):
        for half in range(2):
            block = block_ref[x, half].astype(jnp.float32)
            inverse_rms = (block[128:129, :128] + block[129:130, :128]) + block[130:131, :128]
            unit = block[:128].T * inverse_rms
            place = (pl.ds(half * 256, 256), pl.ds(x * 128, 128))
            unit_ref[place] = unit
            normed_ref[place] = (unit * gain_ref[pl.ds(half * 256, 256), :]).astype(jnp.bfloat16)


def prepared(block, gain_part):
    return pl.pallas_call(
        prepare_kernel,
        out_shape=(jax.ShapeDtypeStruct((512, 512), jnp.bfloat16), jax.ShapeDtypeStruct((512, 512), jnp.float32)),
        name="prepare_columns",
        compiler_params=pltpu.CompilerParams(vmem_limit_bytes=16 * 2**20),
    )(block, gain_part.reshape(512, 1))


def step_of(values, axis):
    peak = jnp.max(jnp.abs(values), axis=axis, keepdims=True)
    return jnp.clip(jnp.ceil(jnp.log2(peak) * STEPS), -110 * STEPS, 127 * STEPS)


def coded_values(values, step):
    return jnp.clip(jnp.round(values * (jnp.exp2(step * (-1 / STEPS)) * FULL)), -FULL, FULL)


def decoded_scale(step):
    return jnp.exp2(step * (1 / STEPS)) * (1 / FULL)


def coded_gain(gains):
    step = step_of(gains, -1)
    exact = gains * (jnp.exp2(step * (-1 / STEPS)) * FULL)
    high = jnp.clip(jnp.round(exact), -FULL, FULL)
    low = jnp.clip(jnp.round((exact - high) * FULL), -FULL, FULL)
    return high, low, jnp.broadcast_to(step, gains.shape)


def narrow(values):
    return values.astype(jnp.int32).astype(jnp.int16)


def wide(codes):
    return codes.astype(jnp.int32).astype(jnp.float32)


def grads_kernel(kept_ref, kept_unit_ref, received_ref, received_unit_ref, own_ref, other_ref, rows_ref, coded_ref, term_ref):
    term_ref[...] = jnp.dot(kept_ref[...], own_ref[...], preferred_element_type=jnp.float32) + jnp.dot(
        received_ref[...], other_ref[...], preferred_element_type=jnp.float32
    )
    gain = 0.0
    for unit_ref, grads_ref in ((kept_unit_ref, own_ref), (received_unit_ref, other_ref)):
        normed_grad = lax.dot_general(
            rows_ref[...], grads_ref[...], (((1,), (1,)), ((), ())), preferred_element_type=jnp.float32
        )
        gain += jnp.sum(normed_grad * unit_ref[...], axis=1, keepdims=True)
    lanes = lax.broadcasted_iota(jnp.int32, (64, 128), 1)
    table = jnp.zeros((64, 128), jnp.float32)
    for chunk in range(8):
        first = chunk // 4 * 256 + chunk % 4 * 8
        column = jnp.concatenate([gain[first + z * 32 : first + z * 32 + 8] for z in range(8)])
        table = jnp.where(lanes == chunk, column, table)
    table = jnp.concatenate([table, jnp.zeros((64, 128), jnp.float32)]).T
    gains = coded_gain(table[:8])
    for chunk in range(8):
        first = chunk // 4 * 256 + chunk % 4 * 8
        rows = jnp.concatenate([term_ref[pl.ds(first + z * 32, 8), :] for z in range(8)])
        step = step_of(rows, 0)
        shown = [jnp.pad(part[chunk : chunk + 1], ((0, 0), (0, 256))) for part in gains]
        whole = [coded_values(rows, step), step] + shown + [jnp.zeros((4, 384), jnp.float32)]
        coded_ref[chunk] = narrow(jnp.concatenate(whole))


def code_z_kernel(parts_ref, coded_ref):
    rows, gains = [], []
    for core in range(2):
        row_sum, gain_sum = 0.0, 0.0
        for y in range(4):
            part = wide(parts_ref[y * 2 + core])
            extra = part[64:]
            row_sum += part[:64] * decoded_scale(extra[0:1])
            gain_sum += (extra[1:2, :128] + extra[2:3, :128] * (1 / FULL)) * decoded_scale(extra[3:4, :128])
        rows.append(row_sum)
        gains.append(gain_sum)
    rows = jnp.concatenate(rows).reshape(16, 8, 384)
    step = step_of(rows, 1)
    shown = jnp.concatenate(coded_gain(jnp.concatenate(gains)) + (jnp.zeros((2, 128), jnp.float32),))
    extra = []
    for z in range(16):
        moved = shown if z % 8 == 0 else pltpu.roll(shown, 128 - z % 8 * 8, 1)
        core = z // 8
        extra.append(jnp.concatenate(
            [step[z, :, k * 128 : (k + 1) * 128] for k in range(3)]
            + [moved[k + core : k + core + 1] for k in (0, 2, 4)]
            + [jnp.zeros((2, 128), jnp.float32)]
        ))
    whole = jnp.concatenate([coded_values(rows, step).reshape(128, 384), jnp.concatenate(extra)], axis=1)
    coded_ref[...] = narrow(whole)


def decode_kernel(coded_ref, rows_ref, gains_ref):
    whole = wide(coded_ref[...]).reshape(16, 8, 512)
    extra = whole[:, :, 384:]
    step = jnp.concatenate([extra[:, 0:1], extra[:, 1:2], extra[:, 2:3]], axis=2)
    rows_ref[...] = jnp.sum(whole[:, :, :384] * decoded_scale(step), axis=0)
    gains = (extra[:, 3:4] + extra[:, 4:5] * (1 / FULL)) * decoded_scale(extra[:, 5:6])
    gains_ref[...] = jnp.sum(gains, axis=0)[:, :8]


def shards(activations, norm_gain, qkv_weight, positions, cotangent):
    x_index = lax.axis_index("x")
    core = lax.axis_index("core")
    width = qkv_weight.shape[1]
    tokens = activations.shape[0]
    normed, inverse_rms, _ = normalize(activations, norm_gain)
    along_z, own_weight = gather_plane(qkv_weight)
    kept, received = redistribute(activations, inverse_rms, x_index, core, along_z)
    gain_part = lax.dynamic_slice(norm_gain.reshape(2, 8, 256), (0, x_index * 2 + core, 0), (2, 1, 256)).reshape(512)
    kept = prepared(kept, gain_part)
    received = prepared(received, gain_part)
    own_weight, normed, kept, received = lax.optimization_barrier((own_weight, normed, kept, received))

    weight = join_weight(own_weight, core)
    projected = jnp.dot(normed, weight, preferred_element_type=jnp.float32)
    qkv_grads = attention_grads(projected, positions, cotangent)
    weight_rows = lax.dynamic_slice(weight.reshape(2, 8, 256, width), (0, x_index * 2 + core, 0, 0), (2, 1, 256, width)).reshape(512, width)

    own_grads = lax.all_to_all(broadcast_rows(qkv_grads, 4), "x", 0, 0, tiled=True)
    other_grads = swap_cores(own_grads)

    parts = pl.pallas_call(
        grads_kernel,
        out_shape=jax.ShapeDtypeStruct((8, 72, width), jnp.int16),
        scratch_shapes=[pltpu.VMEM((512, width), jnp.float32)],
        name="code_y",
        compiler_params=pltpu.CompilerParams(vmem_limit_bytes=16 * 2**20),
    )(*kept, *received, own_grads, other_grads, weight_rows)
    parts = lax.all_to_all(parts, ("y_hi", "y_lo", "core"), 0, 0, tiled=True)
    coded = pl.pallas_call(
        code_z_kernel, out_shape=jax.ShapeDtypeStruct((128, 512), jnp.int16), name="code_z", compiler_params=SMALL
    )(parts)
    coded = lax.all_to_all(coded, "z", 0, 0, tiled=True)
    share, gains = pl.pallas_call(
        decode_kernel,
        out_shape=(jax.ShapeDtypeStruct((8, width), jnp.float32), jax.ShapeDtypeStruct((1, 8), jnp.float32)),
        name="decode_rows", compiler_params=SMALL,
    )(coded)
    return share, gains.reshape(8)


def solution(mesh):
    fine = Mesh(mesh.devices.reshape(2, 4, 16, 2, 2), AXES)
    placed = (
        P(AXES, None),
        P(),
        P(("z", "y_lo", "core"), None),
        P(AXES),
        P(AXES, None),
    )
    return jax.shard_map(
        shards,
        mesh=fine,
        in_specs=placed,
        out_specs=(P(AXES, None), P(AXES)),
        check_vma=False,
    )
```

time: 139 us -> 127 us (0.914)
  waiting for transfers between devices: 37.8 us -> 15.1 us
  blocking collectives: 27.3 us -> 44.1 us
  other arithmetic: 7.38 us -> 4.07 us
  starting transfers between devices: 49 us -> 45.8 us
  local copies, waits for them, and re-layouts: 6.78 us -> 8.8 us
  matrix products: 3.77 us -> 1.92 us
    all_to_all x0 -> x1, blocking collectives: none -> 22.5 us  [shards(): coded = lax.all_to_all(coded, 'z', 0, 0, tiled=True)]
    all_to_all x1 -> x0, waiting for transfers between devices: 12 us -> none  [shards(): coded = lax.all_to_all(coded, 'z', 0, 0, tiled=True)]
    all_to_all x1, waiting for transfers between devices: 9.29 us -> 0.01 us  [gather_plane(): along_z = lax.all_to_all(broadcast_rows(part, 16), 'z', 0, 0, tiled=True)]
    all_to_all x1, blocking collectives: 17 us -> 11.3 us  [shards(): parts = lax.all_to_all(parts, ('y_hi', 'y_lo', 'core'), 0, 0, tiled=True)]
    dynamic_update_slice x0 -> x2, local copies, waits for them, and re-layouts: none -> 3.77 us  [join_weight(): lax.dynamic_update_slice(weight, block[:, :, None], (0, 0, side, 0, 0, 0))]
    all_to_all x1 -> x0, starting transfers between devices: 3.67 us -> none  [shards(): coded = lax.all_to_all(coded, 'z', 0, 0, tiled=True)]
    dot_general x4 -> x0, matrix products: 1.92 us -> none  [the longest x2 0.97 us: shards(): jnp.einsum('xtj,hdj->xhtd', grads, weight_rows, preferred_element_type=jn...]
    all_to_all x1, starting transfers between devices: 4.32 us -> 5.94 us  [gather_plane(): lax.all_to_all(broadcast_rows(along_z, 16), ('y_hi', 'x', 'y_lo'), 0, 0,...]
  transfers between devices with their start and end apart: 9 -> 8, of which waited for: 6 -> 3; matrix products, arithmetic and copies ran while one was open for 5% -> 7% of each run, Pallas kernels for 0% -> 1%
where the time goes in v2:
time: 127 us; the launch traced here: 125 us
  starting transfers between devices  45.8 us (36%)
  blocking collectives  44.1 us (35%)
  waiting for transfers between devices  15.1 us (12%)
  local copies, waits for them, and re-layouts  8.8 us (7%)
  other arithmetic  4.07 us (3%)
  Pallas kernels  3.85 us (3%)
  matrix products  1.92 us (2%)
    all_to_all x1, blocking collectives, shards(): coded = lax.all_to_all(coded, 'z', 0, 0, tiled=True)  22.5 us
    all_to_all x1, starting transfers between devices, gather_plane(): along_z = lax.all_to_all(broadcast_rows(part, 16), 'z', 0, 0, tiled=True)  15.7 us
    ppermute x3, starting transfers between devices, swap_cores(): return lax.ppermute(array, 'core', [(0, 1), (1, 0)])  13.6 us
    all_to_all x1, waiting for transfers between devices, gather_plane(): lax.all_to_all(broadcast_rows(along_z, 16), ('y_hi', 'x', 'y_lo'), 0, 0,...  12.8 us
    all_to_all x1, blocking collectives, shards(): parts = lax.all_to_all(parts, ('y_hi', 'y_lo', 'core'), 0, 0, tiled=True)  11.3 us
    ppermute x3, starting transfers between devices, redistribute(): block = lax.ppermute(block, 'x', [(i, (i + shift) % 4) for i in range(4)])  10.5 us
    all_to_all x1, blocking collectives, shards(): lax.all_to_all(broadcast_rows(qkv_grads, 4), 'x', 0, 0, tiled=True)  10.2 us
    all_to_all x1, starting transfers between devices, gather_plane(): lax.all_to_all(broadcast_rows(along_z, 16), ('y_hi', 'x', 'y_lo'), 0, 0,...  5.94 us
  transfers between devices with their start and end apart: 8, of which 3 were waited for; matrix products, arithmetic and copies ran while one was open for 7% of the time, Pallas kernels for 1%

profile of v2, /device:TPU:1, one launch (start us, length us, event | category | flops | bytes accessed | tf_op | source)
XLA Modules:
  0.0 124.8 jit_solution(15891032657542474340)
XLA Ops:
  0.7 0.8 copy-done
  1.4 0.7 broadcast_in_dim.30
  2.1 15.7 %all-to-all-start = ((bf16[16,8,384]{2,1,0:T(8,128)(2,1)}), bf16[16,8,384]{2,1,0:T(8,128)(2,1)S(1)}, u32[]{:S(2)}, u32[]{:S(2)}) async-start(bf16[16,8,384]{2,1,0:T(8,128)(2,1)} %broadcast_in_dim.30), calls=%async_computation | async-start | bytes 196608 | tf_op jit(solution)/shard_map/all_to_all | solution.py:110
  17.9 1.5 %fusion = f32[128]{0:T(128)S(1)} fusion(bf16[128,4096]{1,0:T(8,128)(2,1)} %param.5), kind=kLoop, calls=%fused_computation.2 | loop fusion | flops 1572736 | bytes 1049088 | tf_op jit(solution)/shard_map/reduce_sum | solution.py:36
  19.7 3.1 %collective-permute-start = (bf16[2,144,512]{2,1,0:T(8,128)(2,1)S(1)}, bf16[2,144,512]{2,1,0:T(8,128)(2,1)S(1)}, u32[]{:S(2)}, u32[]{:S(2)}) collective-permute-start(bf16[2,144,512]{2,1,0:T(8,128)(2,1)S(1)} %get-tuple-element.51), channel_id=1, source_target_pairs={{0,64},{64,128},{128,192},{192,0},{1,65},{65,129},{129,193},{193,1... | collective-permute-start | bytes 884744 | tf_op jit(solution)/shard_map/ppermute | solution.py:142
  22.9 4.4 %collective-permute-start.1 = (bf16[2,144,512]{2,1,0:T(8,128)(2,1)S(1)}, bf16[2,144,512]{2,1,0:T(8,128)(2,1)S(1)}, u32[]{:S(2)}, u32[]{:S(2)}) collective-permute-start(bf16[2,144,512]{2,1,0:T(8,128)(2,1)S(1)} %get-tuple-element.52), channel_id=1, source_target_pairs={{0,128},{64,192},{128,0},{192,64},{1,129},{65,193},{129,1},{193,65... | collective-permute-start | bytes 884744 | tf_op jit(solution)/shard_map/ppermute | solution.py:142
  27.2 3.1 %collective-permute-start.2 = (bf16[2,144,512]{2,1,0:T(8,128)(2,1)S(1)}, bf16[2,144,512]{2,1,0:T(8,128)(2,1)S(1)}, u32[]{:S(2)}, u32[]{:S(2)}) collective-permute-start(bf16[2,144,512]{2,1,0:T(8,128)(2,1)S(1)} %get-tuple-element.50), channel_id=1, source_target_pairs={{0,192},{64,0},{128,64},{192,128},{1,193},{65,1},{129,65},{193,129... | collective-permute-start | bytes 884744 | tf_op jit(solution)/shard_map/ppermute | solution.py:142
  30.6 0.5 slice.61
  31.1 1.3 %broadcast_in_dim.32 = bf16[16,128,384]{2,1,0:T(8,128)(2,1)} broadcast(bf16[128,384]{1,0:T(8,128)(2,1)S(1)} %bitcast.74), dimensions={1,2} | broadcast | bytes 1671168 | tf_op jit(solution)/shard_map/broadcast_in_dim | solution.py:99
  32.4 5.9 %all-to-all-start.1 = ((bf16[16,128,384]{2,1,0:T(8,128)(2,1)}), bf16[16,128,384]{2,1,0:T(8,128)(2,1)}, u32[]{:S(2)}, u32[]{:S(2)}) async-start(bf16[16,128,384]{2,1,0:T(8,128)(2,1)} %broadcast_in_dim.32), calls=%async_computation.1 | async-start | bytes 3145728 | tf_op jit(solution)/shard_map/all_to_all | solution.py:111
  38.4 0.7 broadcast_in_dim.66
  39.4 4.8 %collective-permute-start.3 = (bf16[4,2,144,256]{3,2,1,0:T(8,128)(2,1)S(1)}, bf16[4,2,144,256]{3,2,1,0:T(8,128)(2,1)S(1)}, u32[]{:S(2)}, u32[]{:S(2)}) collective-permute-start(bf16[4,2,144,256]{3,2,1,0:T(8,128)(2,1)S(1)} %get-tuple-element.28), channel_id=1, source_target_pairs={{0,1},{1,0},{2,3},{3,2},{4,5},{5,4},{6,7},{7,6},{8,9},{9,8},{10,11... | collective-permute-start | bytes 1769480 | tf_op jit(solution)/shard_map/ppermute | solution.py:103
  44.2 1.3 %fusion.2 = bf16[128,4096]{1,0:T(8,128)(2,1)} fusion(bf16[128,4096]{1,0:T(8,128)(2,1)S(1)} %copy-done.1, f32[4096]{0:T(1024)S(1)} %copy-done.3, f32[128]{0:T(128)S(1)} %get-tuple-element.27), kind=kLoop, calls=%fused_computation.4 | loop fusion | flops 2097152 | bytes 2114048 | tf_op jit(solution)/shard_map/convert_element_type | solution.py:37
  45.6 0.5 prepare_columns.2
  46.1 0.5 prepare_columns.3
  46.6 12.8 %all-to-all-done.1 = bf16[16,128,384]{2,1,0:T(8,128)(2,1)} async-done(((bf16[16,128,384]{2,1,0:T(8,128)(2,1)}), bf16[16,128,384]{2,1,0:T(8,128)(2,1)}, u32[]{:S(2)}, u32[]{:S(2)}) %all-to-all-start.1) | async-done | bytes 1572896 | tf_op jit(solution)/shard_map/all_to_all | solution.py:111
  59.4 5.6 %collective-permute-start.4 = (bf16[2048,384]{1,0:T(8,128)(2,1)}, bf16[2048,384]{1,0:T(8,128)(2,1)}, u32[]{:S(2)}, u32[]{:S(2)}) collective-permute-start(bf16[2048,384]{1,0:T(8,128)(2,1)} %bitcast.1), channel_id=1, source_target_pairs={{0,1},{1,0},{2,3},{3,2},{4,5},{5,4},{6,7},{7,6},{8,9},{9,8},{10,11... | collective-permute-start | bytes 4718600 | tf_op jit(solution)/shard_map/ppermute | solution.py:103
  65.1 0.5 broadcast_in_dim.71
  65.6 1.8 %copy_dynamic-update-slice_fusion.1 = bf16[16,2,2,8,8,384]{5,4,3,2,1,0:T(8,128)(2,1)S(1)} fusion(bf16[16,2,2,8,8,384]{5,4,3,2,1,0:T(8,128)(2,1)S(1)} %broadcast_in_dim.71, s32[]{:T(128)S(6)} %select_n.82, bf16[16,2,1,8,8,384]{5,4,0,1,3,2:T(8,128)(2,1)} %bitcast.19), kind=kLoop, calls=%fused_computation.6 | loop fusion | bytes 3145732 | tf_op jit(solution)/shard_map/dynamic_update_slice | solution.py:120
  67.5 1.0 collective-permute-done.4
  68.4 1.9 %copy_dynamic-update-slice_fusion = bf16[16,2,2,8,8,384]{5,4,3,2,1,0:T(8,128)(2,1)S(1)} fusion(bf16[16,2,2,8,8,384]{5,4,3,2,1,0:T(8,128)(2,1)S(1)} %copy_dynamic-update-slice_fusion.1, s32[]{:T(128)S(6)} %select_n.83, bf16[16,2,1,8,8,384]{5,4,0,1,3,2:T(8,128)(2,1)} %bitcast.22), kind=kLoop, calls=%fused_computation.5 | loop fusion | bytes 3145732 | tf_op jit(solution)/shard_map/dynamic_update_slice | solution.py:120
  70.4 0.8 fusion.30
  71.3 0.3 fusion.7
  72.6 0.3 fusion.10
  73.4 10.2 %all_to_all.39 = bf16[4,128,384]{2,1,0:T(8,128)(2,1)S(1)} all-to-all(bf16[4,128,384]{2,1,0:T(8,128)(2,1)S(1)} %broadcast_in_dim.75), channel_id=1, replica_groups=mesh['y_hi'=2,'x'=4,'z'=16,'y_lo'=2,'core'=2] {'x'}, dimensions={0} | all-to-all | bytes 786432 | tf_op jit(solution)/shard_map/all_to_all | solution.py:283
  83.6 3.1 %collective-permute-start.5 = (bf16[512,384]{1,0:T(8,128)(2,1)S(1)}, bf16[512,384]{1,0:T(8,128)(2,1)S(1)}, u32[]{:S(2)}, u32[]{:S(2)}) collective-permute-start(bf16[512,384]{1,0:T(8,128)(2,1)S(1)} %bitcast.66), channel_id=1, source_target_pairs={{0,1},{1,0},{2,3},{3,2},{4,5},{5,4},{6,7},{7,6},{8,9},{9,8},{10,11... | collective-permute-start | bytes 1179656 | tf_op jit(solution)/shard_map/ppermute | solution.py:103
  86.8 1.3 %collective-permute-done.5.other_ref = bf16[512,384]{1,0:T(8,128)(2,1)S(1)} collective-permute-done((bf16[512,384]{1,0:T(8,128)(2,1)S(1)}, bf16[512,384]{1,0:T(8,128)(2,1)S(1)}, u32[]{:S(2)}, u32[]{:S(2)}) %collective-permute-start.5) | collective-permute-done | bytes 393248 | tf_op jit(solution)/shard_map/ppermute | solution.py:103
  88.1 1.8 %code_y.1 = s16[8,72,384]{2,1,0:T(8,128)(2,1)S(1)} custom-call(bf16[512,512]{1,0:T(8,128)(2,1)S(1)} %get-tuple-element.18.kept_ref, f32[512,512]{1,0:T(8,128)S(1)} %get-tuple-element.19.kept_unit_ref, bf16[512,512]{1,0:T(8,128)(2,1)S(1)} %get-tuple-element.20.received_ref, f32[512,512]{1,0:T(8,128)S(1)} %get-tuple-element.21.received_unit_ref, ...), custom_call_target="tpu_custom_call" | custom-call | tf_op jit(solution)/shard_map/code_y/pallas_call | solution.py:286
  89.9 11.3 %all_to_all.40.parts_ref = s16[8,72,384]{2,1,0:T(8,128)(2,1)S(1)} all-to-all(s16[8,72,384]{2,1,0:T(8,128)(2,1)S(1)} %code_y.1), channel_id=1, replica_groups=mesh['y_hi'=2,'x'=4,'z'=16,'y_lo'=2,'core'=2] {'y_hi','y_lo','core'}, dimensions={0} | all-to-all | bytes 884736 | tf_op jit(solution)/shard_map/all_to_all | solution.py:293
  101.2 0.3 code_z.1
  101.6 22.5 %all_to_all.41 = s16[16,8,512]{2,1,0:T(8,128)(2,1)S(1)} all-to-all(s16[16,8,512]{2,1,0:T(8,128)(2,1)S(1)} %bitcast.70), channel_id=1, replica_groups=mesh['y_hi'=2,'x'=4,'z'=16,'y_lo'=2,'core'=2] {'z'}, dimensions={0} | all-to-all | bytes 262144 | tf_op jit(solution)/shard_map/all_to_all | solution.py:297
  124.1 0.7 decode_rows.1
  (49 shorter events, 2.2 us)
Async XLA Ops:
  0.6 0.8 copy-start
  0.6 18.8 %copy-start.1 = (bf16[128,4096]{1,0:T(8,128)(2,1)S(1)}, bf16[128,4096]{1,0:T(8,128)(2,1)}, u32[]{:S(2)}) copy-start(bf16[128,4096]{1,0:T(8,128)(2,1)} %param.5) | copy-start | bytes 3145732
  2.1 28.5 %all-to-all-start = ((bf16[16,8,384]{2,1,0:T(8,128)(2,1)}), bf16[16,8,384]{2,1,0:T(8,128)(2,1)S(1)}, u32[]{:S(2)}, u32[]{:S(2)}) async-start(bf16[16,8,384]{2,1,0:T(8,128)(2,1)} %broadcast_in_dim.30), calls=%async_computation | async-start | bytes 196608 | tf_op jit(solution)/shard_map/all_to_all | solution.py:110
  19.5 10.8 %copy-start.3 = (f32[4096]{0:T(1024)S(1)}, f32[4096]{0:T(1024)}, u32[]{:S(2)}) copy-start(f32[4096]{0:T(1024)} %param.6) | copy-start | bytes 49156
  19.7 19.4 %collective-permute-start = (bf16[2,144,512]{2,1,0:T(8,128)(2,1)S(1)}, bf16[2,144,512]{2,1,0:T(8,128)(2,1)S(1)}, u32[]{:S(2)}, u32[]{:S(2)}) collective-permute-start(bf16[2,144,512]{2,1,0:T(8,128)(2,1)S(1)} %get-tuple-element.51), channel_id=1, source_target_pairs={{0,64},{64,128},{128,192},{192,0},{1,65},{65,129},{129,193},{193,1... | collective-permute-start | bytes 884744 | tf_op jit(solution)/shard_map/ppermute | solution.py:142
  22.9 16.3 %collective-permute-start.1 = (bf16[2,144,512]{2,1,0:T(8,128)(2,1)S(1)}, bf16[2,144,512]{2,1,0:T(8,128)(2,1)S(1)}, u32[]{:S(2)}, u32[]{:S(2)}) collective-permute-start(bf16[2,144,512]{2,1,0:T(8,128)(2,1)S(1)} %get-tuple-element.52), channel_id=1, source_target_pairs={{0,128},{64,192},{128,0},{192,64},{1,129},{65,193},{129,1},{193,65... | collective-permute-start | bytes 884744 | tf_op jit(solution)/shard_map/ppermute | solution.py:142
  27.2 12.0 %collective-permute-start.2 = (bf16[2,144,512]{2,1,0:T(8,128)(2,1)S(1)}, bf16[2,144,512]{2,1,0:T(8,128)(2,1)S(1)}, u32[]{:S(2)}, u32[]{:S(2)}) collective-permute-start(bf16[2,144,512]{2,1,0:T(8,128)(2,1)S(1)} %get-tuple-element.50), channel_id=1, source_target_pairs={{0,192},{64,0},{128,64},{192,128},{1,193},{65,1},{129,65},{193,129... | collective-permute-start | bytes 884744 | tf_op jit(solution)/shard_map/ppermute | solution.py:142
  32.4 27.0 %all-to-all-start.1 = ((bf16[16,128,384]{2,1,0:T(8,128)(2,1)}), bf16[16,128,384]{2,1,0:T(8,128)(2,1)}, u32[]{:S(2)}, u32[]{:S(2)}) async-start(bf16[16,128,384]{2,1,0:T(8,128)(2,1)} %broadcast_in_dim.32), calls=%async_computation.1 | async-start | bytes 3145728 | tf_op jit(solution)/shard_map/all_to_all | solution.py:111
  39.4 25.7 %copy-start.5 = (s32[128]{0:T(128)S(1)}, s32[128]{0:T(128)}, u32[]{:S(2)}) copy-start(s32[128]{0:T(128)} %param.8) | copy-start | bytes 1540
  39.4 6.7 %collective-permute-start.3 = (bf16[4,2,144,256]{3,2,1,0:T(8,128)(2,1)S(1)}, bf16[4,2,144,256]{3,2,1,0:T(8,128)(2,1)S(1)}, u32[]{:S(2)}, u32[]{:S(2)}) collective-permute-start(bf16[4,2,144,256]{3,2,1,0:T(8,128)(2,1)S(1)} %get-tuple-element.28), channel_id=1, source_target_pairs={{0,1},{1,0},{2,3},{3,2},{4,5},{5,4},{6,7},{7,6},{8,9},{9,8},{10,11... | collective-permute-start | bytes 1769480 | tf_op jit(solution)/shard_map/ppermute | solution.py:103
  59.4 9.0 %collective-permute-start.4 = (bf16[2048,384]{1,0:T(8,128)(2,1)}, bf16[2048,384]{1,0:T(8,128)(2,1)}, u32[]{:S(2)}, u32[]{:S(2)}) collective-permute-start(bf16[2048,384]{1,0:T(8,128)(2,1)} %bitcast.1), channel_id=1, source_target_pairs={{0,1},{1,0},{2,3},{3,2},{4,5},{5,4},{6,7},{7,6},{8,9},{9,8},{10,11... | collective-permute-start | bytes 4718600 | tf_op jit(solution)/shard_map/ppermute | solution.py:103
  68.4 1.9 %copy-start.2 = (bf16[128,4096]{1,0:T(8,128)(2,1)S(1)}, bf16[128,4096]{1,0:T(8,128)(2,1)}, u32[]{:S(2)}) copy-start(bf16[128,4096]{1,0:T(8,128)(2,1)} %fusion.2) | copy-start | bytes 3145732
  70.4 1.5 %copy-start.4 = (bf16[128,128]{1,0:T(8,128)(2,1)S(1)}, bf16[128,128]{1,0:T(8,128)(2,1)}, u32[]{:S(2)}) copy-start(bf16[128,128]{1,0:T(8,128)(2,1)} %param.9) | copy-start | bytes 98308
  83.6 4.5 %collective-permute-start.5 = (bf16[512,384]{1,0:T(8,128)(2,1)S(1)}, bf16[512,384]{1,0:T(8,128)(2,1)S(1)}, u32[]{:S(2)}, u32[]{:S(2)}) collective-permute-start(bf16[512,384]{1,0:T(8,128)(2,1)S(1)} %bitcast.66), channel_id=1, source_target_pairs={{0,1},{1,0},{2,3},{3,2},{4,5},{5,4},{6,7},{7,6},{8,9},{9,8},{10,11... | collective-permute-start | bytes 1179656 | tf_op jit(solution)/shard_map/ppermute | solution.py:103

commit v3 on v2

v3 whole, which is shorter than its diff:
```python
import jax
import jax.numpy as jnp
from jax import lax
from jax.experimental import pallas as pl
from jax.experimental.pallas import tpu as pltpu
from jax.sharding import Mesh, PartitionSpec as P

rope_base = 10000.0
norm_eps = 1e-05


def angle_kernel(positions_ref, frequency_ref, after_ref, angles_ref):
    angles_ref[...] = positions_ref[...].astype(jnp.float32) * frequency_ref[...]


def rope_tables(positions, head_size, after):
    half_width = head_size // 2
    exponent = jnp.arange(half_width, dtype=jnp.float32) * (-2.0 / head_size)
    frequency = jnp.power(jnp.float32(rope_base), exponent)
    frequency = jnp.concatenate([frequency, frequency])[None]
    vmem = pl.BlockSpec(memory_space=pltpu.VMEM)
    angle_table = pl.pallas_call(
        angle_kernel,
        out_shape=jax.ShapeDtypeStruct((positions.shape[0], head_size), jnp.float32),
        in_specs=[vmem, vmem, pl.BlockSpec(memory_space=pl.ANY)],
        out_specs=vmem,
        name="angles",
        compiler_params=SMALL,
        cost_estimate=BRIEF,
    )(positions, frequency, after)
    return (jnp.cos(angle_table), jnp.sin(angle_table))


def normalize(activations, norm_gain):
    widened = activations.astype(jnp.float32)
    inverse_rms = lax.rsqrt(jnp.mean(widened * widened, axis=1, keepdims=True) + norm_eps)
    return (widened * inverse_rms * norm_gain[None, :]).astype(jnp.bfloat16)


def attention_kernel(
    core_ref, own_ref, other_ref, normed_ref, cosine_ref, sine_ref, positions_ref, cotangent_ref, grads_ref, rows_ref, weight_ref
):
    projected = project(core_ref, own_ref, other_ref, normed_ref, weight_ref, rows_ref)
    cosine, sine = cosine_ref[...], sine_ref[...]
    lower = lax.broadcasted_iota(jnp.int32, (128, 128), 1) < 64
    turned_sine = jnp.where(lower, -sine, sine)

    def rotate(part):
        return (part * cosine + pltpu.roll(part, 64, 1) * turned_sine).astype(jnp.bfloat16)

    def unrotate(part):
        return part * cosine + pltpu.roll(part * turned_sine, 64, 1)

    def product(left, right, over):
        return lax.dot_general(left, right, (((over[0],), (over[1],)), ((), ())), preferred_element_type=jnp.float32)

    queries, keys_rot = rotate(projected[:, :128]), rotate(projected[:, 128:256])
    values = projected[:, 256:].astype(jnp.bfloat16)
    cotangent = cotangent_ref[...]
    score_scale = 128 ** (-0.5)
    scores = product(queries, keys_rot, (1, 1)) * score_scale
    row_index = lax.broadcasted_iota(jnp.int32, (128, 128), 0)
    column_index = lax.broadcasted_iota(jnp.int32, (128, 128), 1)
    visible = (column_index <= row_index) & (row_index - column_index <= positions_ref[...])
    scores = jnp.where(visible, scores, -jnp.inf)
    exp_terms = jnp.exp(scores - jnp.max(scores, axis=1, keepdims=True))
    attention = exp_terms / jnp.sum(exp_terms, axis=1, keepdims=True)
    attention_low = attention.astype(jnp.bfloat16)
    prob_grad = product(cotangent, values, (1, 1))
    score_grad = (
        attention * (prob_grad - jnp.sum(attention * prob_grad, axis=1, keepdims=True)) * score_scale
    ).astype(jnp.bfloat16)
    grads = jnp.concatenate(
        [
            unrotate(product(score_grad, keys_rot, (1, 0))),
            unrotate(product(score_grad, queries, (0, 0))),
            product(attention_low, cotangent, (0, 0)),
        ],
        axis=1,
    ).astype(jnp.bfloat16)
    for copy in range(4):
        grads_ref[copy] = grads


def attention_grads(place, own, normed, tables, positions, cotangent):
    tokens, width = normed.shape[0], own.shape[1]
    raw = own.reshape(8, 2, 16, 8, width)
    ordered = pl.pallas_call(
        order_kernel,
        out_shape=jax.ShapeDtypeStruct((16, 2, 64, width), own.dtype),
        name="order_rows",
        compiler_params=SMALL,
        cost_estimate=BRIEF,
    )(raw)
    vmem = pl.BlockSpec(memory_space=pltpu.VMEM)
    grads, rows = pl.pallas_call(
        attention_kernel,
        out_shape=(
            jax.ShapeDtypeStruct((4, tokens, width), jnp.bfloat16),
            jax.ShapeDtypeStruct((512, width), jnp.bfloat16),
        ),
        in_specs=[pl.BlockSpec(memory_space=pltpu.SMEM)] + [vmem] * 7,
        out_specs=(vmem, vmem),
        scratch_shapes=[pltpu.VMEM((4096, width), jnp.bfloat16)],
        name="attention_grads",
        compiler_params=pltpu.CompilerParams(vmem_limit_bytes=20 * 2**20),
    )(place, ordered, swap_cores(own).reshape(raw.shape), normed, *tables, positions, cotangent)
    return grads.reshape(4 * tokens, width), rows


AXES = ("y_hi", "x", "z", "y_lo", "core")
STEPS = 64.0
BRIEF = pl.CostEstimate(flops=2**20, bytes_accessed=2**18, transcendentals=0)
SMALL = pltpu.CompilerParams(vmem_limit_bytes=8 * 2**20)
FULL = 32767.0


def broadcast_rows(block, count):
    rows, width = block.shape
    return jnp.broadcast_to(block[None], (count, rows, width)).reshape(count * rows, width)


def swap_cores(array):
    return lax.ppermute(array, "core", [(0, 1), (1, 0)])


def copy_kernel(part_ref, copies_ref, seed_ref):
    for copy in range(16):
        copies_ref[copy] = part_ref[...]
    seed_ref[...] = jnp.zeros_like(seed_ref)


def gather_plane(qkv_weight):
    width = qkv_weight.shape[1]
    member = lax.axis_index("y_hi") * 4 + lax.axis_index("x")
    part = lax.dynamic_slice(qkv_weight, (member * 8, 0), (8, width))
    along_z = lax.all_to_all(broadcast_rows(part, 16), "z", 0, 0, tiled=True)
    copies, seed = pl.pallas_call(
        copy_kernel,
        out_shape=(jax.ShapeDtypeStruct((16, 128, width), jnp.bfloat16), jax.ShapeDtypeStruct((1, 512), jnp.bfloat16)),
        name="copy_rows",
        compiler_params=SMALL,
    )(along_z)
    plane = lax.all_to_all(copies.reshape(2048, width), ("y_hi", "x", "y_lo"), 0, 0, tiled=True)
    return seed, plane


def order_kernel(raw_ref, ordered_ref):
    for z in range(16):
        for y in range(2):
            rows = [raw_ref[eighth, y, z].astype(jnp.float32) for eighth in range(8)]
            ordered_ref[z, y] = jnp.concatenate(rows).astype(jnp.bfloat16)


def project(core_ref, own_ref, other_ref, normed_ref, weight_ref, rows_ref):
    core, column = core_ref[0], core_ref[1]
    for z in range(16):
        for y in range(2):
            rows = [other_ref[eighth, y, z].astype(jnp.float32) for eighth in range(8)]
            place = z * 256 + y * 128
            weight_ref[pl.ds(pl.multiple_of(place + core * 64, 64), 64), :] = own_ref[z, y]
            weight_ref[pl.ds(pl.multiple_of(place + (1 - core) * 64, 64), 64), :] = jnp.concatenate(rows).astype(jnp.bfloat16)
    for half in range(2):
        start = pl.multiple_of(half * 2048 + column * 256, 256)
        rows_ref[pl.ds(half * 256, 256), :] = weight_ref[pl.ds(start, 256), :]
    return jnp.dot(normed_ref[...], weight_ref[...], preferred_element_type=jnp.float32)


def blocks_kernel(x_ref, activations_ref, *block_refs):
    squares = 0.0
    for part in range(4):
        widened = activations_ref[:, part * 1024 : (part + 1) * 1024].astype(jnp.float32)
        squares += jnp.sum(widened * widened, axis=1, keepdims=True)
    inverse_rms = jnp.broadcast_to(lax.rsqrt(squares / 4096 + norm_eps), (128, 128)).T
    high = inverse_rms.astype(jnp.bfloat16).astype(jnp.float32)
    rest = inverse_rms - high
    middle = rest.astype(jnp.bfloat16).astype(jnp.float32)
    row = lax.broadcasted_iota(jnp.int32, (128, 128), 0)
    extra = jnp.where(row == 0, high, jnp.where(row == 1, middle, jnp.where(row == 2, rest - middle, 0.0)))
    extra = jnp.concatenate([extra[:16]] * 4, axis=1).astype(jnp.bfloat16)
    for shift, block_ref in enumerate(block_refs):
        target = lax.rem(x_ref[0] + shift, 4)
        for half in range(2):
            start = pl.multiple_of(half * 2048 + target * 512, 512)
            block_ref[half, pl.ds(0, 128), :] = activations_ref[:, pl.ds(start, 512)]
            block_ref[half, pl.ds(128, 16), :] = extra


def redistribute(activations, x_index, core, seed):
    tokens = activations.shape[0]
    vmem = pl.BlockSpec(memory_space=pltpu.VMEM)
    blocks = pl.pallas_call(
        blocks_kernel,
        out_shape=[jax.ShapeDtypeStruct((2, tokens + 16, 512), jnp.bfloat16)] * 4,
        in_specs=[pl.BlockSpec(memory_space=pltpu.SMEM), vmem],
        out_specs=[vmem] * 4,
        name="cut_blocks",
        compiler_params=SMALL,
        cost_estimate=BRIEF,
    )(x_index.reshape(1), activations)
    ordered = jnp.broadcast_to(seed.reshape(1, 1, 1, 512), (4, 2, tokens + 16, 512))
    for shift, block in enumerate(blocks):
        if shift:
            block = lax.ppermute(block, "x", [(i, (i + shift) % 4) for i in range(4)])
        ordered = lax.dynamic_update_slice(ordered, block[None], (lax.rem(x_index - shift + 4, 4), 0, 0, 0))
    first, second = ordered[..., :256], ordered[..., 256:]
    kept = jnp.where(core == 0, first, second)
    sent = jnp.where(core == 0, second, first)
    return kept, swap_cores(sent)


def prepare_kernel(block_ref, gain_ref, normed_ref, unit_ref):
    for x in range(4):
        for half in range(2):
            block = block_ref[x, half].astype(jnp.float32)
            inverse_rms = (block[128:129, :128] + block[129:130, :128]) + block[130:131, :128]
            unit = block[:128].T * inverse_rms
            place = (pl.ds(half * 256, 256), pl.ds(x * 128, 128))
            unit_ref[place] = unit
            normed_ref[place] = (unit * gain_ref[pl.ds(half * 256, 256), :]).astype(jnp.bfloat16)


def prepared(block, gain_part):
    return pl.pallas_call(
        prepare_kernel,
        out_shape=(jax.ShapeDtypeStruct((512, 512), jnp.bfloat16), jax.ShapeDtypeStruct((512, 512), jnp.float32)),
        name="prepare_columns",
        compiler_params=pltpu.CompilerParams(vmem_limit_bytes=16 * 2**20),
    )(block, gain_part.reshape(512, 1))


def step_of(values, axis):
    peak = jnp.max(jnp.abs(values), axis=axis, keepdims=True)
    return jnp.clip(jnp.ceil(jnp.log2(peak) * STEPS), -110 * STEPS, 127 * STEPS)


def coded_values(values, step):
    return jnp.clip(jnp.round(values * (jnp.exp2(step * (-1 / STEPS)) * FULL)), -FULL, FULL)


def decoded_scale(step):
    return jnp.exp2(step * (1 / STEPS)) * (1 / FULL)


def coded_gain(gains):
    step = step_of(gains, -1)
    exact = gains * (jnp.exp2(step * (-1 / STEPS)) * FULL)
    high = jnp.clip(jnp.round(exact), -FULL, FULL)
    low = jnp.clip(jnp.round((exact - high) * FULL), -FULL, FULL)
    return high, low, jnp.broadcast_to(step, gains.shape)


def narrow(values):
    return values.astype(jnp.int32).astype(jnp.int16)


def wide(codes):
    return codes.astype(jnp.int32).astype(jnp.float32)


def half_grads(normed_ref, unit_ref, grads_ref, rows_ref):
    term = jnp.dot(normed_ref[...], grads_ref[...], preferred_element_type=jnp.float32)
    normed_grad = lax.dot_general(
        rows_ref[...], grads_ref[...], (((1,), (1,)), ((), ())), preferred_element_type=jnp.float32
    )
    return term, jnp.sum(normed_grad * unit_ref[...], axis=1, keepdims=True)


def first_grads_kernel(normed_ref, unit_ref, grads_ref, rows_ref, term_ref, gain_ref):
    term_ref[...], gain_ref[...] = half_grads(normed_ref, unit_ref, grads_ref, rows_ref)


def grads_kernel(first_ref, first_gain_ref, normed_ref, unit_ref, grads_ref, rows_ref, coded_ref, term_ref):
    term, gain = half_grads(normed_ref, unit_ref, grads_ref, rows_ref)
    term_ref[...] = first_ref[...] + term
    gain = first_gain_ref[...] + gain
    lanes = lax.broadcasted_iota(jnp.int32, (64, 128), 1)
    table = jnp.zeros((64, 128), jnp.float32)
    for chunk in range(8):
        first = chunk // 4 * 256 + chunk % 4 * 8
        column = jnp.concatenate([gain[first + z * 32 : first + z * 32 + 8] for z in range(8)])
        table = jnp.where(lanes == chunk, column, table)
    table = jnp.concatenate([table, jnp.zeros((64, 128), jnp.float32)]).T
    gains = coded_gain(table[:8])
    for chunk in range(8):
        first = chunk // 4 * 256 + chunk % 4 * 8
        rows = jnp.concatenate([term_ref[pl.ds(first + z * 32, 8), :] for z in range(8)])
        step = step_of(rows, 0)
        shown = [jnp.pad(part[chunk : chunk + 1], ((0, 0), (0, 256))) for part in gains]
        whole = [coded_values(rows, step), step] + shown + [jnp.zeros((4, 384), jnp.float32)]
        coded_ref[chunk] = narrow(jnp.concatenate(whole))


def code_z_kernel(parts_ref, coded_ref):
    rows, gains = [], []
    for core in range(2):
        row_sum, gain_sum = 0.0, 0.0
        for y in range(4):
            part = wide(parts_ref[y * 2 + core])
            extra = part[64:]
            row_sum += part[:64] * decoded_scale(extra[0:1])
            gain_sum += (extra[1:2, :128] + extra[2:3, :128] * (1 / FULL)) * decoded_scale(extra[3:4, :128])
        rows.append(row_sum)
        gains.append(gain_sum)
    rows = jnp.concatenate(rows).reshape(16, 8, 384)
    step = step_of(rows, 1)
    shown = jnp.concatenate(coded_gain(jnp.concatenate(gains)) + (jnp.zeros((2, 128), jnp.float32),))
    extra = []
    for z in range(16):
        moved = shown if z % 8 == 0 else pltpu.roll(shown, 128 - z % 8 * 8, 1)
        core = z // 8
        extra.append(jnp.concatenate(
            [step[z, :, k * 128 : (k + 1) * 128] for k in range(3)]
            + [moved[k + core : k + core + 1] for k in (0, 2, 4)]
            + [jnp.zeros((2, 128), jnp.float32)]
        ))
    whole = jnp.concatenate([coded_values(rows, step).reshape(128, 384), jnp.concatenate(extra)], axis=1)
    coded_ref[...] = narrow(whole)


def decode_kernel(coded_ref, rows_ref, gains_ref):
    whole = wide(coded_ref[...]).reshape(16, 8, 512)
    extra = whole[:, :, 384:]
    step = jnp.concatenate([extra[:, 0:1], extra[:, 1:2], extra[:, 2:3]], axis=2)
    rows_ref[...] = jnp.sum(whole[:, :, :384] * decoded_scale(step), axis=0)
    gains = (extra[:, 3:4] + extra[:, 4:5] * (1 / FULL)) * decoded_scale(extra[:, 5:6])
    gains_ref[...] = jnp.sum(gains, axis=0)[:, :8]


def shards(activations, norm_gain, qkv_weight, positions, cotangent):
    x_index = lax.axis_index("x")
    core = lax.axis_index("core")
    width = qkv_weight.shape[1]
    tokens = activations.shape[0]
    seed, own_weight = gather_plane(qkv_weight)
    normed = normalize(activations + jnp.tile(seed, (1, 8)), norm_gain)
    kept, received = redistribute(activations, x_index, core, seed)
    gain_part = lax.dynamic_slice(norm_gain.reshape(2, 8, 256), (0, x_index * 2 + core, 0), (2, 1, 256)).reshape(512)
    kept = prepared(kept, gain_part)
    received = prepared(received, gain_part)
    own_weight, normed, kept, received = lax.optimization_barrier((own_weight, normed, kept, received))
    positions = positions.reshape(tokens, 1)
    tables = rope_tables(positions, cotangent.shape[1], own_weight)

    place = jnp.stack([core, x_index * 2 + core])
    qkv_grads, weight_rows = attention_grads(place, own_weight, normed, tables, positions, cotangent)

    own_grads = lax.all_to_all(qkv_grads, "x", 0, 0, tiled=True)
    other_grads = swap_cores(own_grads)

    first = pl.pallas_call(
        first_grads_kernel,
        out_shape=(jax.ShapeDtypeStruct((512, width), jnp.float32), jax.ShapeDtypeStruct((512, 1), jnp.float32)),
        name="first_grads",
        compiler_params=pltpu.CompilerParams(vmem_limit_bytes=16 * 2**20),
        cost_estimate=BRIEF,
    )(*kept, own_grads, weight_rows)
    parts = pl.pallas_call(
        grads_kernel,
        out_shape=jax.ShapeDtypeStruct((8, 72, width), jnp.int16),
        scratch_shapes=[pltpu.VMEM((512, width), jnp.float32)],
        name="code_y",
        compiler_params=pltpu.CompilerParams(vmem_limit_bytes=16 * 2**20),
    )(*first, *received, other_grads, weight_rows)
    parts = lax.all_to_all(parts, ("y_hi", "y_lo", "core"), 0, 0, tiled=True)
    coded = pl.pallas_call(
        code_z_kernel, out_shape=jax.ShapeDtypeStruct((128, 512), jnp.int16), name="code_z", compiler_params=SMALL
    )(parts)
    coded = lax.all_to_all(coded, "z", 0, 0, tiled=True)
    share, gains = pl.pallas_call(
        decode_kernel,
        out_shape=(jax.ShapeDtypeStruct((8, width), jnp.float32), jax.ShapeDtypeStruct((1, 8), jnp.float32)),
        name="decode_rows", compiler_params=SMALL,
    )(coded)
    return share, gains.reshape(8)


def solution(mesh):
    fine = Mesh(mesh.devices.reshape(2, 4, 16, 2, 2), AXES)
    placed = (
        P(AXES, None),
        P(),
        P(("z", "y_lo", "core"), None),
        P(AXES),
        P(AXES, None),
    )
    return jax.shard_map(
        shards,
        mesh=fine,
        in_specs=placed,
        out_specs=(P(AXES, None), P(AXES)),
        check_vma=False,
    )
```

time: 127 us -> 124 us (0.976)
  Pallas kernels: 3.85 us -> 9.24 us
  other arithmetic: 4.07 us -> 0.98 us
  waiting for transfers between devices: 15.1 us -> 12.8 us
  matrix products: 1.92 us -> 0 us
  local copies, waits for them, and re-layouts: 8.8 us -> 7.34 us
    pallas_call x0 -> x6, Pallas kernels: none -> 5.88 us  [the longest x1 3.23 us: attention_grads(): pl.pallas_call(attention_kernel, out_shape=(jax.ShapeDtypeStruct((4, toke...]
    dynamic_update_slice x2 -> x0, local copies, waits for them, and re-layouts: 3.77 us -> none  [join_weight(): lax.dynamic_update_slice(weight, block[:, :, None], (0, 0, side, 0, 0, 0))]
    unnamed x13 -> x26, local copies, waits for them, and re-layouts: 0.81 us -> 4.05 us
    all_to_all x1, waiting for transfers between devices: 12.8 us -> 9.78 us  [gather_plane(): lax.all_to_all(copies.reshape(2048, width), ('y_hi', 'x', 'y_lo'), 0, 0,...]
    dynamic_update_slice x3 -> x4, local copies, waits for them, and re-layouts: 0.08 us -> 2.03 us  [redistribute(): lax.dynamic_update_slice(ordered, block[None], (lax.rem(x_index - shift +...]
    dot_general x6 -> x0, matrix products: 1.92 us -> none  [the longest x1 0.77 us: shards(): projected = jnp.dot(normed, weight, preferred_element_type=jnp.float32)]
    broadcast_in_dim x3 -> x1, local copies, waits for them, and re-layouts: 2.03 us -> 0.65 us  [broadcast_rows(): jnp.broadcast_to(block[None], (count, rows, width))]
    convert_element_type x4 -> x1, other arithmetic: 1.69 us -> 0.34 us  [normalize(): return (widened * inverse_rms * norm_gain[None, :]).astype(jnp.bfloat16)]
  transfers between devices with their start and end apart: 8 -> 8, of which waited for: 3 -> 4; matrix products, arithmetic and copies ran while one was open for 7% -> 3% of each run, Pallas kernels for 1% -> 3%
where the time goes in v3:
time: 124 us; the launch traced here: 122 us
  starting transfers between devices  46.2 us (37%)
  blocking collectives  44.1 us (36%)
  waiting for transfers between devices  12.8 us (10%)
  Pallas kernels  9.24 us (7%)
  local copies, waits for them, and re-layouts  7.34 us (6%)
    all_to_all x1, blocking collectives, shards(): coded = lax.all_to_all(coded, 'z', 0, 0, tiled=True)  22.6 us
    all_to_all x1, starting transfers between devices, gather_plane(): along_z = lax.all_to_all(broadcast_rows(part, 16), 'z', 0, 0, tiled=True)  15.7 us
    ppermute x3, starting transfers between devices, swap_cores(): return lax.ppermute(array, 'core', [(0, 1), (1, 0)])  13.7 us
    all_to_all x1, blocking collectives, shards(): parts = lax.all_to_all(parts, ('y_hi', 'y_lo', 'core'), 0, 0, tiled=True)  11.3 us
    ppermute x3, starting transfers between devices, redistribute(): block = lax.ppermute(block, 'x', [(i, (i + shift) % 4) for i in range(4)])  10.5 us
    all_to_all x1, blocking collectives, shards(): own_grads = lax.all_to_all(qkv_grads, 'x', 0, 0, tiled=True)  10.2 us
    all_to_all x1, waiting for transfers between devices, gather_plane(): lax.all_to_all(copies.reshape(2048, width), ('y_hi', 'x', 'y_lo'), 0, 0,...  9.78 us
    all_to_all x1, starting transfers between devices, gather_plane(): lax.all_to_all(copies.reshape(2048, width), ('y_hi', 'x', 'y_lo'), 0, 0,...  6.21 us
  transfers between devices with their start and end apart: 8, of which 4 were waited for; matrix products, arithmetic and copies ran while one was open for 3% of the time, Pallas kernels for 3%

profile of v3, /device:TPU:1, one launch (start us, length us, event | category | flops | bytes accessed | tf_op | source)
XLA Modules:
  0.0 121.7 jit_solution(6671221546341387786)
XLA Ops:
  0.7 0.8 copy-done
  1.4 0.6 broadcast_in_dim.28
  2.1 15.7 %all-to-all-start = ((bf16[16,8,384]{2,1,0:T(8,128)(2,1)}), bf16[16,8,384]{2,1,0:T(8,128)(2,1)S(1)}, u32[]{:S(2)}, u32[]{:S(2)}) async-start(bf16[16,8,384]{2,1,0:T(8,128)(2,1)} %broadcast_in_dim.28), calls=%async_computation | async-start | bytes 196608 | tf_op jit(solution)/shard_map/all_to_all | solution.py:137
  17.8 1.2 copy-done.1
  19.1 0.3 cut_blocks.1
  19.4 3.1 %collective-permute-start = (bf16[2,144,512]{2,1,0:T(8,128)(2,1)S(1)}, bf16[2,144,512]{2,1,0:T(8,128)(2,1)}, u32[]{:S(2)}, u32[]{:S(2)}) collective-permute-start(bf16[2,144,512]{2,1,0:T(8,128)(2,1)S(1)} %get-tuple-element.27), channel_id=1, source_target_pairs={{0,64},{64,128},{128,192},{192,0},{1,65},{65,129},{129,193},{193,1... | collective-permute-start | bytes 884744 | tf_op jit(solution)/shard_map/ppermute | solution.py:204
  22.5 4.4 %collective-permute-start.1 = (bf16[2,144,512]{2,1,0:T(8,128)(2,1)S(1)}, bf16[2,144,512]{2,1,0:T(8,128)(2,1)}, u32[]{:S(2)}, u32[]{:S(2)}) collective-permute-start(bf16[2,144,512]{2,1,0:T(8,128)(2,1)S(1)} %get-tuple-element.28), channel_id=1, source_target_pairs={{0,128},{64,192},{128,0},{192,64},{1,129},{65,193},{129,1},{193,65... | collective-permute-start | bytes 884744 | tf_op jit(solution)/shard_map/ppermute | solution.py:204
  26.9 3.1 %collective-permute-start.2 = (bf16[2,144,512]{2,1,0:T(8,128)(2,1)S(1)}, bf16[2,144,512]{2,1,0:T(8,128)(2,1)S(1)}, u32[]{:S(2)}, u32[]{:S(2)}) collective-permute-start(bf16[2,144,512]{2,1,0:T(8,128)(2,1)S(1)} %get-tuple-element.29), channel_id=1, source_target_pairs={{0,192},{64,0},{128,64},{192,128},{1,193},{65,1},{129,65},{193,129... | collective-permute-start | bytes 884744 | tf_op jit(solution)/shard_map/ppermute | solution.py:204
  30.2 1.3 %copy_rows.1 = (bf16[16,128,384]{2,1,0:T(8,128)(2,1)}, bf16[1,512]{1,0:T(2,128)(2,1)S(1)}) custom-call(bf16[128,384]{1,0:T(8,128)(2,1)S(1)} %bitcast.33), custom_call_target="tpu_custom_call" | custom-call | tf_op jit(solution)/shard_map/copy_rows/pallas_call | solution.py:138
  31.5 6.2 %all-to-all-start.1 = ((bf16[16,128,384]{2,1,0:T(8,128)(2,1)}), bf16[16,128,384]{2,1,0:T(8,128)(2,1)S(1)}, u32[]{:S(2)}, u32[]{:S(2)}) async-start(bf16[16,128,384]{2,1,0:T(8,128)(2,1)} %get-tuple-element.24), calls=%async_computation.1 | async-start | bytes 3145728 | tf_op jit(solution)/shard_map/all_to_all | solution.py:144
  37.9 1.0 bitcast_dynamic-update-slice_fusion.2
  38.9 1.0 bitcast_dynamic-update-slice_fusion.1
  40.1 5.0 %collective-permute-start.3 = (bf16[4,2,144,256]{3,2,1,0:T(8,128)(2,1)S(1)}, bf16[4,2,144,256]{3,2,1,0:T(8,128)(2,1)S(1)}, u32[]{:S(2)}, u32[]{:S(2)}) collective-permute-start(bf16[4,2,144,256]{3,2,1,0:T(8,128)(2,1)S(1)} %get-tuple-element.46), channel_id=1, source_target_pairs={{0,1},{1,0},{2,3},{3,2},{4,5},{5,4},{6,7},{7,6},{8,9},{9,8},{10,11... | collective-permute-start | bytes 1769480 | tf_op jit(solution)/shard_map/ppermute | solution.py:124
  45.1 0.5 prepare_columns.2
  45.6 0.4 fusion
  46.0 0.3 fusion.2.normed_ref
  46.7 0.5 prepare_columns.3
  47.2 1.0 copy-done.5
  48.2 0.8 copy-done.7
  49.0 9.8 %all-to-all-done.1 = bf16[16,128,384]{2,1,0:T(8,128)(2,1)S(1)} async-done(((bf16[16,128,384]{2,1,0:T(8,128)(2,1)}), bf16[16,128,384]{2,1,0:T(8,128)(2,1)S(1)}, u32[]{:S(2)}, u32[]{:S(2)}) %all-to-all-start.1) | async-done | bytes 1572896 | tf_op jit(solution)/shard_map/all_to_all | solution.py:144
  58.8 5.6 %collective-permute-start.4 = (bf16[2048,384]{1,0:T(8,128)(2,1)S(1)}, bf16[2048,384]{1,0:T(8,128)(2,1)}, u32[]{:S(2)}, u32[]{:S(2)}) collective-permute-start(bf16[2048,384]{1,0:T(8,128)(2,1)S(1)} %bitcast.26), channel_id=1, source_target_pairs={{0,1},{1,0},{2,3},{3,2},{4,5},{5,4},{6,7},{7,6},{8,9},{9,8},{10,11... | collective-permute-start | bytes 4718600 | tf_op jit(solution)/shard_map/ppermute | solution.py:124
  65.2 2.4 %collective-permute-done.4 = bf16[2048,384]{1,0:T(8,128)(2,1)} collective-permute-done((bf16[2048,384]{1,0:T(8,128)(2,1)S(1)}, bf16[2048,384]{1,0:T(8,128)(2,1)}, u32[]{:S(2)}, u32[]{:S(2)}) %collective-permute-start.4) | collective-permute-done | bytes 1572896 | tf_op jit(solution)/shard_map/ppermute | solution.py:124
  67.6 3.2 %attention_grads.1 = (bf16[4,128,384]{2,1,0:T(8,128)(2,1)S(1)}, bf16[512,384]{1,0:T(8,128)(2,1)S(1)}) custom-call(s32[2]{0:T(128)S(1)} %pad_add_fusion.core_ref, bf16[16,2,64,384]{3,2,1,0:T(8,128)(2,1)S(1)} %order_rows.1.own_ref, bf16[8,2,16,8,384]{4,3,2,1,0:T(8,128)(2,1)} %bitcast.11.other_ref, bf16[128,4096]{1,0:T(8,128)(2,1)S(1)} %fusion.2.normed_ref, ...), custom_call_target="tpu_custom_call" | custom-call | tf_op jit(solution)/shard_map/attention_grads/pallas_call | solution.py:96
  70.8 10.2 %all_to_all.41 = bf16[4,128,384]{2,1,0:T(8,128)(2,1)S(1)} all-to-all(bf16[4,128,384]{2,1,0:T(8,128)(2,1)S(1)} %get-tuple-element.38), channel_id=1, replica_groups=mesh['y_hi'=2,'x'=4,'z'=16,'y_lo'=2,'core'=2] {'x'}, dimensions={0} | all-to-all | bytes 786432 | tf_op jit(solution)/shard_map/all_to_all | solution.py:348
  81.0 3.1 %collective-permute-start.5 = (bf16[512,384]{1,0:T(8,128)(2,1)S(1)}, bf16[512,384]{1,0:T(8,128)(2,1)S(1)}, u32[]{:S(2)}, u32[]{:S(2)}) collective-permute-start(bf16[512,384]{1,0:T(8,128)(2,1)S(1)} %bitcast.29), channel_id=1, source_target_pairs={{0,1},{1,0},{2,3},{3,2},{4,5},{5,4},{6,7},{7,6},{8,9},{9,8},{10,11... | collective-permute-start | bytes 1179656 | tf_op jit(solution)/shard_map/ppermute | solution.py:124
  84.2 0.8 first_grads.1
  84.9 0.5 collective-permute-done.5.grads_ref
  85.5 1.3 %code_y.1 = s16[8,72,384]{2,1,0:T(8,128)(2,1)S(1)} custom-call(f32[512,384]{1,0:T(8,128)S(1)} %get-tuple-element.40.first_ref, f32[512,1]{1,0:T(8,128)S(1)} %get-tuple-element.41.first_gain_ref, bf16[512,512]{1,0:T(8,128)(2,1)S(1)} %copy-done.8, f32[512,512]{1,0:T(8,128)S(1)} %copy-done.6, bf16[512,384]{1,0:T(8,128)(2,1)S(1)} %collective-permute-done.5.grads_ref, ...), custom_call_target="tpu_custom_call" | custom-call | tf_op jit(solution)/shard_map/code_y/pallas_call | solution.py:358
  86.8 11.3 %all_to_all.42.parts_ref = s16[8,72,384]{2,1,0:T(8,128)(2,1)S(1)} all-to-all(s16[8,72,384]{2,1,0:T(8,128)(2,1)S(1)} %code_y.1), channel_id=1, replica_groups=mesh['y_hi'=2,'x'=4,'z'=16,'y_lo'=2,'core'=2] {'y_hi','y_lo','core'}, dimensions={0} | all-to-all | bytes 884736 | tf_op jit(solution)/shard_map/all_to_all | solution.py:365
  98.1 0.3 code_z.1
  98.5 22.6 %all_to_all.43 = s16[16,8,512]{2,1,0:T(8,128)(2,1)S(1)} all-to-all(s16[16,8,512]{2,1,0:T(8,128)(2,1)S(1)} %bitcast.32), channel_id=1, replica_groups=mesh['y_hi'=2,'x'=4,'z'=16,'y_lo'=2,'core'=2] {'z'}, dimensions={0} | all-to-all | bytes 262144 | tf_op jit(solution)/shard_map/all_to_all | solution.py:369
  121.0 0.7 decode_rows.1
  (44 shorter events, 1.6 us)
Async XLA Ops:
  0.6 0.8 copy-start
  0.6 29.3 %copy-start.10 = (f32[4096]{0:T(1024)S(1)}, f32[4096]{0:T(1024)}, u32[]{:S(2)}) copy-start(f32[4096]{0:T(1024)} %param.6) | copy-start | bytes 49156
  2.1 28.1 %all-to-all-start = ((bf16[16,8,384]{2,1,0:T(8,128)(2,1)}), bf16[16,8,384]{2,1,0:T(8,128)(2,1)S(1)}, u32[]{:S(2)}, u32[]{:S(2)}) async-start(bf16[16,8,384]{2,1,0:T(8,128)(2,1)} %broadcast_in_dim.28), calls=%async_computation | async-start | bytes 196608 | tf_op jit(solution)/shard_map/all_to_all | solution.py:137
  17.8 1.2 %copy-start.1 = (bf16[128,4096]{1,0:T(8,128)(2,1)S(1)}, bf16[128,4096]{1,0:T(8,128)(2,1)}, u32[]{:S(2)}) copy-start(bf16[128,4096]{1,0:T(8,128)(2,1)} %activations_ref.1) | copy-start | bytes 3145732
  19.4 18.5 %collective-permute-start = (bf16[2,144,512]{2,1,0:T(8,128)(2,1)S(1)}, bf16[2,144,512]{2,1,0:T(8,128)(2,1)}, u32[]{:S(2)}, u32[]{:S(2)}) collective-permute-start(bf16[2,144,512]{2,1,0:T(8,128)(2,1)S(1)} %get-tuple-element.27), channel_id=1, source_target_pairs={{0,64},{64,128},{128,192},{192,0},{1,65},{65,129},{129,193},{193,1... | collective-permute-start | bytes 884744 | tf_op jit(solution)/shard_map/ppermute | solution.py:204
  22.5 16.4 %collective-permute-start.1 = (bf16[2,144,512]{2,1,0:T(8,128)(2,1)S(1)}, bf16[2,144,512]{2,1,0:T(8,128)(2,1)}, u32[]{:S(2)}, u32[]{:S(2)}) collective-permute-start(bf16[2,144,512]{2,1,0:T(8,128)(2,1)S(1)} %get-tuple-element.28), channel_id=1, source_target_pairs={{0,128},{64,192},{128,0},{192,64},{1,129},{65,193},{129,1},{193,65... | collective-permute-start | bytes 884744 | tf_op jit(solution)/shard_map/ppermute | solution.py:204
  26.9 13.0 %collective-permute-start.2 = (bf16[2,144,512]{2,1,0:T(8,128)(2,1)S(1)}, bf16[2,144,512]{2,1,0:T(8,128)(2,1)S(1)}, u32[]{:S(2)}, u32[]{:S(2)}) collective-permute-start(bf16[2,144,512]{2,1,0:T(8,128)(2,1)S(1)} %get-tuple-element.29), channel_id=1, source_target_pairs={{0,192},{64,0},{128,64},{192,128},{1,193},{65,1},{129,65},{193,129... | collective-permute-start | bytes 884744 | tf_op jit(solution)/shard_map/ppermute | solution.py:204
  31.5 27.2 %all-to-all-start.1 = ((bf16[16,128,384]{2,1,0:T(8,128)(2,1)}), bf16[16,128,384]{2,1,0:T(8,128)(2,1)S(1)}, u32[]{:S(2)}, u32[]{:S(2)}) async-start(bf16[16,128,384]{2,1,0:T(8,128)(2,1)} %get-tuple-element.24), calls=%async_computation.1 | async-start | bytes 3145728 | tf_op jit(solution)/shard_map/all_to_all | solution.py:144
  40.0 5.7 %copy-start.2 = (bf16[128,4096]{1,0:T(8,128)(2,1)S(1)}, bf16[128,4096]{1,0:T(8,128)(2,1)}, u32[]{:S(2)}) copy-start(bf16[128,4096]{1,0:T(8,128)(2,1)} %activations_ref.1) | copy-start | bytes 3145732
  40.1 6.6 %collective-permute-start.3 = (bf16[4,2,144,256]{3,2,1,0:T(8,128)(2,1)S(1)}, bf16[4,2,144,256]{3,2,1,0:T(8,128)(2,1)S(1)}, u32[]{:S(2)}, u32[]{:S(2)}) collective-permute-start(bf16[4,2,144,256]{3,2,1,0:T(8,128)(2,1)S(1)} %get-tuple-element.46), channel_id=1, source_target_pairs={{0,1},{1,0},{2,3},{3,2},{4,5},{5,4},{6,7},{7,6},{8,9},{9,8},{10,11... | collective-permute-start | bytes 1769480 | tf_op jit(solution)/shard_map/ppermute | solution.py:124
  45.6 1.0 copy-start.3
  46.0 18.4 %copy-start.11 = (s32[128]{0:T(128)S(1)}, s32[128]{0:T(128)}, u32[]{:S(2)}) copy-start(s32[128]{0:T(128)} %param.8) | copy-start | bytes 1540
  47.2 1.0 copy-start.5
  48.2 0.8 copy-start.7
  58.8 8.8 %collective-permute-start.4 = (bf16[2048,384]{1,0:T(8,128)(2,1)S(1)}, bf16[2048,384]{1,0:T(8,128)(2,1)}, u32[]{:S(2)}, u32[]{:S(2)}) collective-permute-start(bf16[2048,384]{1,0:T(8,128)(2,1)S(1)} %bitcast.26), channel_id=1, source_target_pairs={{0,1},{1,0},{2,3},{3,2},{4,5},{5,4},{6,7},{7,6},{8,9},{9,8},{10,11... | collective-permute-start | bytes 4718600 | tf_op jit(solution)/shard_map/ppermute | solution.py:124
  64.8 2.7 %copy-start.9 = (bf16[128,128]{1,0:T(8,128)(2,1)S(1)}, bf16[128,128]{1,0:T(8,128)(2,1)}, u32[]{:S(2)}) copy-start(bf16[128,128]{1,0:T(8,128)(2,1)} %cotangent_ref.1) | copy-start | bytes 98308
  67.6 16.6 %copy-start.4 = (f32[512,512]{1,0:T(8,128)S(1)}, f32[512,512]{1,0:T(8,128)}, u32[]{:S(2)}) copy-start(f32[512,512]{1,0:T(8,128)} %copy-done.3) | copy-start | bytes 3145732
  81.0 4.4 %collective-permute-start.5 = (bf16[512,384]{1,0:T(8,128)(2,1)S(1)}, bf16[512,384]{1,0:T(8,128)(2,1)S(1)}, u32[]{:S(2)}, u32[]{:S(2)}) collective-permute-start(bf16[512,384]{1,0:T(8,128)(2,1)S(1)} %bitcast.29), channel_id=1, source_target_pairs={{0,1},{1,0},{2,3},{3,2},{4,5},{5,4},{6,7},{7,6},{8,9},{9,8},{10,11... | collective-permute-start | bytes 1179656 | tf_op jit(solution)/shard_map/ppermute | solution.py:124
  84.1 1.3 %copy-start.6 = (f32[512,512]{1,0:T(8,128)S(1)}, f32[512,512]{1,0:T(8,128)}, u32[]{:S(2)}) copy-start(f32[512,512]{1,0:T(8,128)} %copy-done.5) | copy-start | bytes 3145732
  84.1 1.3 %copy-start.8 = (bf16[512,512]{1,0:T(8,128)(2,1)S(1)}, bf16[512,512]{1,0:T(8,128)(2,1)}, u32[]{:S(2)}) copy-start(bf16[512,512]{1,0:T(8,128)(2,1)} %copy-done.7) | copy-start | bytes 1572868

commit v4 on v3

--- a/solution.py
+++ b/solution.py
@@ -109,6 +109,7 @@
 
 
 AXES = ("y_hi", "x", "z", "y_lo", "core")
+Z_ORDER = [[(place + 8) % 16 for place in range(16)]]
 STEPS = 64.0
 BRIEF = pl.CostEstimate(flops=2**20, bytes_accessed=2**18, transcendentals=0)
 SMALL = pltpu.CompilerParams(vmem_limit_bytes=8 * 2**20)
@@ -126,7 +127,8 @@
 
 def copy_kernel(part_ref, copies_ref, seed_ref):
     for copy in range(16):
-        copies_ref[copy] = part_ref[...]
+        copies_ref[copy, pl.ds(0, 64), :] = part_ref[pl.ds(64, 64), :]
+        copies_ref[copy, pl.ds(64, 64), :] = part_ref[pl.ds(0, 64), :]
     seed_ref[...] = jnp.zeros_like(seed_ref)
 
 
@@ -134,7 +136,7 @@
     width = qkv_weight.shape[1]
     member = lax.axis_index("y_hi") * 4 + lax.axis_index("x")
     part = lax.dynamic_slice(qkv_weight, (member * 8, 0), (8, width))
-    along_z = lax.all_to_all(broadcast_rows(part, 16), "z", 0, 0, tiled=True)
+    along_z = lax.all_to_all(broadcast_rows(part, 16), "z", 0, 0, axis_index_groups=Z_ORDER, tiled=True)
     copies, seed = pl.pallas_call(
         copy_kernel,
         out_shape=(jax.ShapeDtypeStruct((16, 128, width), jnp.bfloat16), jax.ShapeDtypeStruct((1, 512), jnp.bfloat16)),
@@ -315,7 +317,7 @@
             + [jnp.zeros((2, 128), jnp.float32)]
         ))
     whole = jnp.concatenate([coded_values(rows, step).reshape(128, 384), jnp.concatenate(extra)], axis=1)
-    coded_ref[...] = narrow(whole)
+    coded_ref[...] = narrow(jnp.concatenate([whole[64:], whole[:64]]))
 
 
 def decode_kernel(coded_ref, rows_ref, gains_ref):
@@ -366,7 +368,7 @@
     coded = pl.pallas_call(
         code_z_kernel, out_shape=jax.ShapeDtypeStruct((128, 512), jnp.int16), name="code_z", compiler_params=SMALL
     )(parts)
-    coded = lax.all_to_all(coded, "z", 0, 0, tiled=True)
+    coded = lax.all_to_all(coded, "z", 0, 0, axis_index_groups=Z_ORDER, tiled=True)
     share, gains = pl.pallas_call(
         decode_kernel,
         out_shape=(jax.ShapeDtypeStruct((8, width), jnp.float32), jax.ShapeDtypeStruct((1, 8), jnp.float32)),

time: 124 us -> 120 us (0.968); the launches traced: 122 us -> 119 us
  blocking collectives: 44.1 us -> 38.7 us
  starting transfers between devices: 46.2 us -> 49.4 us
    all_to_all x1, blocking collectives: 22.6 us -> 17.3 us  [shards(): lax.all_to_all(coded, 'z', 0, 0, axis_index_groups=Z_ORDER, tiled=True)]
    all_to_all x1, starting transfers between devices: 15.7 us -> 19.1 us  [gather_plane(): lax.all_to_all(broadcast_rows(part, 16), 'z', 0, 0, axis_index_groups=Z_O...]
    all_to_all x1, starting transfers between devices: 6.21 us -> 4.32 us  [gather_plane(): lax.all_to_all(copies.reshape(2048, width), ('y_hi', 'x', 'y_lo'), 0, 0,...]
    ppermute x3, starting transfers between devices: 13.7 us -> 15.4 us  [swap_cores(): return lax.ppermute(array, 'core', [(0, 1), (1, 0)])]
  transfers between devices with their start and end apart: 8 -> 8, of which waited for: 4 -> 6; matrix products, arithmetic and copies ran while one was open for 3% -> 3% of each run, Pallas kernels for 3% -> 3%
where the time goes in v4:
time: 120 us; the launch traced here: 119 us
  starting transfers between devices  49.4 us (41%)
  blocking collectives  38.7 us (32%)
  waiting for transfers between devices  12.5 us (10%)
  Pallas kernels  9.25 us (8%)
  local copies, waits for them, and re-layouts  7.33 us (6%)
    all_to_all x1, starting transfers between devices, gather_plane(): lax.all_to_all(broadcast_rows(part, 16), 'z', 0, 0, axis_index_groups=Z_O...  19.1 us
    all_to_all x1, blocking collectives, shards(): lax.all_to_all(coded, 'z', 0, 0, axis_index_groups=Z_ORDER, tiled=True)  17.3 us
    ppermute x3, starting transfers between devices, swap_cores(): return lax.ppermute(array, 'core', [(0, 1), (1, 0)])  15.4 us
    all_to_all x1, blocking collectives, shards(): parts = lax.all_to_all(parts, ('y_hi', 'y_lo', 'core'), 0, 0, tiled=True)  11.3 us
    ppermute x3, starting transfers between devices, redistribute(): block = lax.ppermute(block, 'x', [(i, (i + shift) % 4) for i in range(4)])  10.5 us
    all_to_all x1, blocking collectives, shards(): own_grads = lax.all_to_all(qkv_grads, 'x', 0, 0, tiled=True)  10.1 us
    all_to_all x1, waiting for transfers between devices, gather_plane(): lax.all_to_all(copies.reshape(2048, width), ('y_hi', 'x', 'y_lo'), 0, 0,...  8.95 us
    all_to_all x1, starting transfers between devices, gather_plane(): lax.all_to_all(copies.reshape(2048, width), ('y_hi', 'x', 'y_lo'), 0, 0,...  4.32 us
  transfers between devices with their start and end apart: 8, of which 6 were waited for; matrix products, arithmetic and copies ran while one was open for 3% of the time, Pallas kernels for 3%

profile of v4, /device:TPU:1, one launch (start us, length us, event | category | flops | bytes accessed | tf_op | source)
XLA Modules:
  0.0 119.2 jit_solution(5607415798624065676)
XLA Ops:
  0.7 0.8 copy-done
  1.4 0.6 broadcast_in_dim.28
  2.1 19.1 %all-to-all-start = ((bf16[16,8,384]{2,1,0:T(8,128)(2,1)}), bf16[16,8,384]{2,1,0:T(8,128)(2,1)S(1)}, u32[]{:S(2)}, u32[]{:S(2)}) async-start(bf16[16,8,384]{2,1,0:T(8,128)(2,1)} %broadcast_in_dim.28), calls=%async_computation | async-start | bytes 196608 | tf_op jit(solution)/shard_map/all_to_all | solution.py:139
  21.2 1.2 %copy-done.1 = bf16[128,4096]{1,0:T(8,128)(2,1)S(1)} copy-done((bf16[128,4096]{1,0:T(8,128)(2,1)S(1)}, bf16[128,4096]{1,0:T(8,128)(2,1)}, u32[]{:S(2)}) %copy-start.1) | copy-done | bytes 1048600
  22.4 0.3 cut_blocks.1
  22.8 3.1 %collective-permute-start = (bf16[2,144,512]{2,1,0:T(8,128)(2,1)S(1)}, bf16[2,144,512]{2,1,0:T(8,128)(2,1)}, u32[]{:S(2)}, u32[]{:S(2)}) collective-permute-start(bf16[2,144,512]{2,1,0:T(8,128)(2,1)S(1)} %get-tuple-element.27), channel_id=1, source_target_pairs={{0,64},{64,128},{128,192},{192,0},{1,65},{65,129},{129,193},{193,1... | collective-permute-start | bytes 884744 | tf_op jit(solution)/shard_map/ppermute | solution.py:206
  25.9 4.4 %collective-permute-start.1 = (bf16[2,144,512]{2,1,0:T(8,128)(2,1)S(1)}, bf16[2,144,512]{2,1,0:T(8,128)(2,1)}, u32[]{:S(2)}, u32[]{:S(2)}) collective-permute-start(bf16[2,144,512]{2,1,0:T(8,128)(2,1)S(1)} %get-tuple-element.28), channel_id=1, source_target_pairs={{0,128},{64,192},{128,0},{192,64},{1,129},{65,193},{129,1},{193,65... | collective-permute-start | bytes 884744 | tf_op jit(solution)/shard_map/ppermute | solution.py:206
  30.3 3.1 %collective-permute-start.2 = (bf16[2,144,512]{2,1,0:T(8,128)(2,1)S(1)}, bf16[2,144,512]{2,1,0:T(8,128)(2,1)S(1)}, u32[]{:S(2)}, u32[]{:S(2)}) collective-permute-start(bf16[2,144,512]{2,1,0:T(8,128)(2,1)S(1)} %get-tuple-element.29), channel_id=1, source_target_pairs={{0,192},{64,0},{128,64},{192,128},{1,193},{65,1},{129,65},{193,129... | collective-permute-start | bytes 884744 | tf_op jit(solution)/shard_map/ppermute | solution.py:206
  33.6 1.3 %copy_rows.1 = (bf16[16,128,384]{2,1,0:T(8,128)(2,1)}, bf16[1,512]{1,0:T(2,128)(2,1)S(1)}) custom-call(bf16[128,384]{1,0:T(8,128)(2,1)S(1)} %bitcast.33), custom_call_target="tpu_custom_call" | custom-call | tf_op jit(solution)/shard_map/copy_rows/pallas_call | solution.py:140
  34.9 4.3 %all-to-all-start.1 = ((bf16[16,128,384]{2,1,0:T(8,128)(2,1)}), bf16[16,128,384]{2,1,0:T(8,128)(2,1)S(1)}, u32[]{:S(2)}, u32[]{:S(2)}) async-start(bf16[16,128,384]{2,1,0:T(8,128)(2,1)} %get-tuple-element.24), calls=%async_computation.1 | async-start | bytes 3145728 | tf_op jit(solution)/shard_map/all_to_all | solution.py:146
  39.4 1.0 bitcast_dynamic-update-slice_fusion.2
  40.5 1.0 bitcast_dynamic-update-slice_fusion.1
  41.5 0.4 collective-permute-done.2
  42.1 5.8 %collective-permute-start.3 = (bf16[4,2,144,256]{3,2,1,0:T(8,128)(2,1)S(1)}, bf16[4,2,144,256]{3,2,1,0:T(8,128)(2,1)S(1)}, u32[]{:S(2)}, u32[]{:S(2)}) collective-permute-start(bf16[4,2,144,256]{3,2,1,0:T(8,128)(2,1)S(1)} %get-tuple-element.46), channel_id=1, source_target_pairs={{0,1},{1,0},{2,3},{3,2},{4,5},{5,4},{6,7},{7,6},{8,9},{9,8},{10,11... | collective-permute-start | bytes 1769480 | tf_op jit(solution)/shard_map/ppermute | solution.py:125
  47.9 0.5 prepare_columns.2
  48.5 0.4 fusion
  48.9 0.3 fusion.2.normed_ref
  49.5 0.5 prepare_columns.3
  50.0 1.0 copy-done.5
  51.0 0.8 copy-done.7
  51.8 8.9 %all-to-all-done.1 = bf16[16,128,384]{2,1,0:T(8,128)(2,1)S(1)} async-done(((bf16[16,128,384]{2,1,0:T(8,128)(2,1)}), bf16[16,128,384]{2,1,0:T(8,128)(2,1)S(1)}, u32[]{:S(2)}, u32[]{:S(2)}) %all-to-all-start.1) | async-done | bytes 1572896 | tf_op jit(solution)/shard_map/all_to_all | solution.py:146
  60.8 5.8 %collective-permute-start.4 = (bf16[2048,384]{1,0:T(8,128)(2,1)S(1)}, bf16[2048,384]{1,0:T(8,128)(2,1)}, u32[]{:S(2)}, u32[]{:S(2)}) collective-permute-start(bf16[2048,384]{1,0:T(8,128)(2,1)S(1)} %bitcast.26), channel_id=1, source_target_pairs={{0,1},{1,0},{2,3},{3,2},{4,5},{5,4},{6,7},{7,6},{8,9},{9,8},{10,11... | collective-permute-start | bytes 4718600 | tf_op jit(solution)/shard_map/ppermute | solution.py:125
  67.4 2.4 %collective-permute-done.4 = bf16[2048,384]{1,0:T(8,128)(2,1)} collective-permute-done((bf16[2048,384]{1,0:T(8,128)(2,1)S(1)}, bf16[2048,384]{1,0:T(8,128)(2,1)}, u32[]{:S(2)}, u32[]{:S(2)}) %collective-permute-start.4) | collective-permute-done | bytes 1572896 | tf_op jit(solution)/shard_map/ppermute | solution.py:125
  69.7 3.2 %attention_grads.1 = (bf16[4,128,384]{2,1,0:T(8,128)(2,1)S(1)}, bf16[512,384]{1,0:T(8,128)(2,1)S(1)}) custom-call(s32[2]{0:T(128)S(1)} %pad_add_fusion.core_ref, bf16[16,2,64,384]{3,2,1,0:T(8,128)(2,1)S(1)} %order_rows.1.own_ref, bf16[8,2,16,8,384]{4,3,2,1,0:T(8,128)(2,1)} %bitcast.11.other_ref, bf16[128,4096]{1,0:T(8,128)(2,1)S(1)} %fusion.2.normed_ref, ...), custom_call_target="tpu_custom_call" | custom-call | tf_op jit(solution)/shard_map/attention_grads/pallas_call | solution.py:96
  73.0 10.1 %all_to_all.41 = bf16[4,128,384]{2,1,0:T(8,128)(2,1)S(1)} all-to-all(bf16[4,128,384]{2,1,0:T(8,128)(2,1)S(1)} %get-tuple-element.38), channel_id=1, replica_groups=mesh['y_hi'=2,'x'=4,'z'=16,'y_lo'=2,'core'=2] {'x'}, dimensions={0} | all-to-all | bytes 786432 | tf_op jit(solution)/shard_map/all_to_all | solution.py:350
  83.1 3.7 %collective-permute-start.5 = (bf16[512,384]{1,0:T(8,128)(2,1)S(1)}, bf16[512,384]{1,0:T(8,128)(2,1)S(1)}, u32[]{:S(2)}, u32[]{:S(2)}) collective-permute-start(bf16[512,384]{1,0:T(8,128)(2,1)S(1)} %bitcast.29), channel_id=1, source_target_pairs={{0,1},{1,0},{2,3},{3,2},{4,5},{5,4},{6,7},{7,6},{8,9},{9,8},{10,11... | collective-permute-start | bytes 1179656 | tf_op jit(solution)/shard_map/ppermute | solution.py:125
  86.8 0.8 first_grads.1
  87.6 0.5 collective-permute-done.5.grads_ref
  88.2 1.3 %code_y.1 = s16[8,72,384]{2,1,0:T(8,128)(2,1)S(1)} custom-call(f32[512,384]{1,0:T(8,128)S(1)} %get-tuple-element.40.first_ref, f32[512,1]{1,0:T(8,128)S(1)} %get-tuple-element.41.first_gain_ref, bf16[512,512]{1,0:T(8,128)(2,1)S(1)} %copy-done.8, f32[512,512]{1,0:T(8,128)S(1)} %copy-done.6, bf16[512,384]{1,0:T(8,128)(2,1)S(1)} %collective-permute-done.5.grads_ref, ...), custom_call_target="tpu_custom_call" | custom-call | tf_op jit(solution)/shard_map/code_y/pallas_call | solution.py:360
  89.5 11.3 %all_to_all.42.parts_ref = s16[8,72,384]{2,1,0:T(8,128)(2,1)S(1)} all-to-all(s16[8,72,384]{2,1,0:T(8,128)(2,1)S(1)} %code_y.1), channel_id=1, replica_groups=mesh['y_hi'=2,'x'=4,'z'=16,'y_lo'=2,'core'=2] {'y_hi','y_lo','core'}, dimensions={0} | all-to-all | bytes 884736 | tf_op jit(solution)/shard_map/all_to_all | solution.py:367
  101.2 17.3 %all_to_all.43 = s16[16,8,512]{2,1,0:T(8,128)(2,1)S(1)} all-to-all(s16[16,8,512]{2,1,0:T(8,128)(2,1)S(1)} %bitcast.32), channel_id=1, replica_groups={{32,36,40,44,48,52,56,60,0,4,8,12,16,20,24,28},{33,37,41,45,49,53,57,61..., dimensions={0} | all-to-all | bytes 262144 | tf_op jit(solution)/shard_map/all_to_all | solution.py:371
  118.5 0.7 decode_rows.1
  (44 shorter events, 2.0 us)
Async XLA Ops:
  0.6 0.8 copy-start
  0.6 32.7 %copy-start.10 = (f32[4096]{0:T(1024)S(1)}, f32[4096]{0:T(1024)}, u32[]{:S(2)}) copy-start(f32[4096]{0:T(1024)} %param.6) | copy-start | bytes 49156
  2.1 31.5 %all-to-all-start = ((bf16[16,8,384]{2,1,0:T(8,128)(2,1)}), bf16[16,8,384]{2,1,0:T(8,128)(2,1)S(1)}, u32[]{:S(2)}, u32[]{:S(2)}) async-start(bf16[16,8,384]{2,1,0:T(8,128)(2,1)} %broadcast_in_dim.28), calls=%async_computation | async-start | bytes 196608 | tf_op jit(solution)/shard_map/all_to_all | solution.py:139
  21.2 1.2 %copy-start.1 = (bf16[128,4096]{1,0:T(8,128)(2,1)S(1)}, bf16[128,4096]{1,0:T(8,128)(2,1)}, u32[]{:S(2)}) copy-start(bf16[128,4096]{1,0:T(8,128)(2,1)} %activations_ref.1) | copy-start | bytes 3145732
  22.8 16.6 %collective-permute-start = (bf16[2,144,512]{2,1,0:T(8,128)(2,1)S(1)}, bf16[2,144,512]{2,1,0:T(8,128)(2,1)}, u32[]{:S(2)}, u32[]{:S(2)}) collective-permute-start(bf16[2,144,512]{2,1,0:T(8,128)(2,1)S(1)} %get-tuple-element.27), channel_id=1, source_target_pairs={{0,64},{64,128},{128,192},{192,0},{1,65},{65,129},{129,193},{193,1... | collective-permute-start | bytes 884744 | tf_op jit(solution)/shard_map/ppermute | solution.py:206
  25.9 14.6 %collective-permute-start.1 = (bf16[2,144,512]{2,1,0:T(8,128)(2,1)S(1)}, bf16[2,144,512]{2,1,0:T(8,128)(2,1)}, u32[]{:S(2)}, u32[]{:S(2)}) collective-permute-start(bf16[2,144,512]{2,1,0:T(8,128)(2,1)S(1)} %get-tuple-element.28), channel_id=1, source_target_pairs={{0,128},{64,192},{128,0},{192,64},{1,129},{65,193},{129,1},{193,65... | collective-permute-start | bytes 884744 | tf_op jit(solution)/shard_map/ppermute | solution.py:206
  30.3 11.7 %collective-permute-start.2 = (bf16[2,144,512]{2,1,0:T(8,128)(2,1)S(1)}, bf16[2,144,512]{2,1,0:T(8,128)(2,1)S(1)}, u32[]{:S(2)}, u32[]{:S(2)}) collective-permute-start(bf16[2,144,512]{2,1,0:T(8,128)(2,1)S(1)} %get-tuple-element.29), channel_id=1, source_target_pairs={{0,192},{64,0},{128,64},{192,128},{1,193},{65,1},{129,65},{193,129... | collective-permute-start | bytes 884744 | tf_op jit(solution)/shard_map/ppermute | solution.py:206
  34.9 25.8 %all-to-all-start.1 = ((bf16[16,128,384]{2,1,0:T(8,128)(2,1)}), bf16[16,128,384]{2,1,0:T(8,128)(2,1)S(1)}, u32[]{:S(2)}, u32[]{:S(2)}) async-start(bf16[16,128,384]{2,1,0:T(8,128)(2,1)} %get-tuple-element.24), calls=%async_computation.1 | async-start | bytes 3145728 | tf_op jit(solution)/shard_map/all_to_all | solution.py:146
  42.0 6.5 %copy-start.2 = (bf16[128,4096]{1,0:T(8,128)(2,1)S(1)}, bf16[128,4096]{1,0:T(8,128)(2,1)}, u32[]{:S(2)}) copy-start(bf16[128,4096]{1,0:T(8,128)(2,1)} %activations_ref.1) | copy-start | bytes 3145732
  42.1 7.4 %collective-permute-start.3 = (bf16[4,2,144,256]{3,2,1,0:T(8,128)(2,1)S(1)}, bf16[4,2,144,256]{3,2,1,0:T(8,128)(2,1)S(1)}, u32[]{:S(2)}, u32[]{:S(2)}) collective-permute-start(bf16[4,2,144,256]{3,2,1,0:T(8,128)(2,1)S(1)} %get-tuple-element.46), channel_id=1, source_target_pairs={{0,1},{1,0},{2,3},{3,2},{4,5},{5,4},{6,7},{7,6},{8,9},{9,8},{10,11... | collective-permute-start | bytes 1769480 | tf_op jit(solution)/shard_map/ppermute | solution.py:125
  48.4 1.0 copy-start.3
  48.8 17.7 %copy-start.11 = (s32[128]{0:T(128)S(1)}, s32[128]{0:T(128)}, u32[]{:S(2)}) copy-start(s32[128]{0:T(128)} %param.8) | copy-start | bytes 1540
  50.0 1.0 copy-start.5
  51.0 0.8 copy-start.7
  60.8 9.0 %collective-permute-start.4 = (bf16[2048,384]{1,0:T(8,128)(2,1)S(1)}, bf16[2048,384]{1,0:T(8,128)(2,1)}, u32[]{:S(2)}, u32[]{:S(2)}) collective-permute-start(bf16[2048,384]{1,0:T(8,128)(2,1)S(1)} %bitcast.26), channel_id=1, source_target_pairs={{0,1},{1,0},{2,3},{3,2},{4,5},{5,4},{6,7},{7,6},{8,9},{9,8},{10,11... | collective-permute-start | bytes 4718600 | tf_op jit(solution)/shard_map/ppermute | solution.py:125
  67.0 2.7 %copy-start.9 = (bf16[128,128]{1,0:T(8,128)(2,1)S(1)}, bf16[128,128]{1,0:T(8,128)(2,1)}, u32[]{:S(2)}) copy-start(bf16[128,128]{1,0:T(8,128)(2,1)} %cotangent_ref.1) | copy-start | bytes 98308
  69.7 17.1 %copy-start.4 = (f32[512,512]{1,0:T(8,128)S(1)}, f32[512,512]{1,0:T(8,128)}, u32[]{:S(2)}) copy-start(f32[512,512]{1,0:T(8,128)} %copy-done.3) | copy-start | bytes 3145732
  83.1 5.1 %collective-permute-start.5 = (bf16[512,384]{1,0:T(8,128)(2,1)S(1)}, bf16[512,384]{1,0:T(8,128)(2,1)S(1)}, u32[]{:S(2)}, u32[]{:S(2)}) collective-permute-start(bf16[512,384]{1,0:T(8,128)(2,1)S(1)} %bitcast.29), channel_id=1, source_target_pairs={{0,1},{1,0},{2,3},{3,2},{4,5},{5,4},{6,7},{7,6},{8,9},{9,8},{10,11... | collective-permute-start | bytes 1179656 | tf_op jit(solution)/shard_map/ppermute | solution.py:125
  86.8 1.3 %copy-start.6 = (f32[512,512]{1,0:T(8,128)S(1)}, f32[512,512]{1,0:T(8,128)}, u32[]{:S(2)}) copy-start(f32[512,512]{1,0:T(8,128)} %copy-done.5) | copy-start | bytes 3145732
  86.8 1.3 %copy-start.8 = (bf16[512,512]{1,0:T(8,128)(2,1)S(1)}, bf16[512,512]{1,0:T(8,128)(2,1)}, u32[]{:S(2)}) copy-start(bf16[512,512]{1,0:T(8,128)(2,1)} %copy-done.7) | copy-start | bytes 1572868

commit v5 on v3

--- a/solution.py
+++ b/solution.py
@@ -109,6 +109,8 @@
 
 
 AXES = ("y_hi", "x", "z", "y_lo", "core")
+FIRST_Z, LAST_Z = 12, 4
+FIRST_ORDER, LAST_ORDER = ([[(place + start) % 16 for place in range(16)]] for start in (FIRST_Z, LAST_Z))
 STEPS = 64.0
 BRIEF = pl.CostEstimate(flops=2**20, bytes_accessed=2**18, transcendentals=0)
 SMALL = pltpu.CompilerParams(vmem_limit_bytes=8 * 2**20)
@@ -125,8 +127,10 @@
 
 
 def copy_kernel(part_ref, copies_ref, seed_ref):
+    late = FIRST_Z * 8
     for copy in range(16):
-        copies_ref[copy] = part_ref[...]
+        copies_ref[copy, pl.ds(0, late), :] = part_ref[pl.ds(128 - late, late), :]
+        copies_ref[copy, pl.ds(late, 128 - late), :] = part_ref[pl.ds(0, 128 - late), :]
     seed_ref[...] = jnp.zeros_like(seed_ref)
 
 
@@ -134,7 +138,7 @@
     width = qkv_weight.shape[1]
     member = lax.axis_index("y_hi") * 4 + lax.axis_index("x")
     part = lax.dynamic_slice(qkv_weight, (member * 8, 0), (8, width))
-    along_z = lax.all_to_all(broadcast_rows(part, 16), "z", 0, 0, tiled=True)
+    along_z = lax.all_to_all(broadcast_rows(part, 16), "z", 0, 0, axis_index_groups=FIRST_ORDER, tiled=True)
     copies, seed = pl.pallas_call(
         copy_kernel,
         out_shape=(jax.ShapeDtypeStruct((16, 128, width), jnp.bfloat16), jax.ShapeDtypeStruct((1, 512), jnp.bfloat16)),
@@ -315,7 +319,7 @@
             + [jnp.zeros((2, 128), jnp.float32)]
         ))
     whole = jnp.concatenate([coded_values(rows, step).reshape(128, 384), jnp.concatenate(extra)], axis=1)
-    coded_ref[...] = narrow(whole)
+    coded_ref[...] = narrow(jnp.concatenate([whole[LAST_Z * 8 :], whole[: LAST_Z * 8]]))
 
 
 def decode_kernel(coded_ref, rows_ref, gains_ref):
@@ -366,7 +370,7 @@
     coded = pl.pallas_call(
         code_z_kernel, out_shape=jax.ShapeDtypeStruct((128, 512), jnp.int16), name="code_z", compiler_params=SMALL
     )(parts)
-    coded = lax.all_to_all(coded, "z", 0, 0, tiled=True)
+    coded = lax.all_to_all(coded, "z", 0, 0, axis_index_groups=LAST_ORDER, tiled=True)
     share, gains = pl.pallas_call(
         decode_kernel,
         out_shape=(jax.ShapeDtypeStruct((8, width), jnp.float32), jax.ShapeDtypeStruct((1, 8), jnp.float32)),

time: 124 us -> 117 us (0.944); the launches traced: 122 us -> 117 us
  blocking collectives: 44.1 us -> 39.4 us
    all_to_all x1, blocking collectives: 22.6 us -> 17.9 us  [shards(): lax.all_to_all(coded, 'z', 0, 0, axis_index_groups=LAST_ORDER, tiled=True)]
    all_to_all x1, starting transfers between devices: 6.21 us -> 4.32 us  [gather_plane(): lax.all_to_all(copies.reshape(2048, width), ('y_hi', 'x', 'y_lo'), 0, 0,...]
    ppermute x3, starting transfers between devices: 13.7 us -> 15.4 us  [swap_cores(): return lax.ppermute(array, 'core', [(0, 1), (1, 0)])]
  transfers between devices with their start and end apart: 8 -> 8, of which waited for: 4 -> 6; matrix products, arithmetic and copies ran while one was open for 3% -> 3% of each run, Pallas kernels for 3% -> 3%
where the time goes in v5:
time: 117 us
  starting transfers between devices  46.2 us (39%)
  blocking collectives  39.4 us (34%)
  waiting for transfers between devices  12.5 us (11%)
  Pallas kernels  9.24 us (8%)
  local copies, waits for them, and re-layouts  7.33 us (6%)
    all_to_all x1, blocking collectives, shards(): lax.all_to_all(coded, 'z', 0, 0, axis_index_groups=LAST_ORDER, tiled=True)  17.9 us
    all_to_all x1, starting transfers between devices, gather_plane(): lax.all_to_all(broadcast_rows(part, 16), 'z', 0, 0, axis_index_groups=FIR...  15.9 us
    ppermute x3, starting transfers between devices, swap_cores(): return lax.ppermute(array, 'core', [(0, 1), (1, 0)])  15.4 us
    all_to_all x1, blocking collectives, shards(): parts = lax.all_to_all(parts, ('y_hi', 'y_lo', 'core'), 0, 0, tiled=True)  11.3 us
    ppermute x3, starting transfers between devices, redistribute(): block = lax.ppermute(block, 'x', [(i, (i + shift) % 4) for i in range(4)])  10.5 us
    all_to_all x1, blocking collectives, shards(): own_grads = lax.all_to_all(qkv_grads, 'x', 0, 0, tiled=True)  10.1 us
    all_to_all x1, waiting for transfers between devices, gather_plane(): lax.all_to_all(copies.reshape(2048, width), ('y_hi', 'x', 'y_lo'), 0, 0,...  8.95 us
    all_to_all x1, starting transfers between devices, gather_plane(): lax.all_to_all(copies.reshape(2048, width), ('y_hi', 'x', 'y_lo'), 0, 0,...  4.32 us
  transfers between devices with their start and end apart: 8, of which 6 were waited for; matrix products, arithmetic and copies ran while one was open for 3% of the time, Pallas kernels for 3%

profile of v5, /device:TPU:1, one launch (start us, length us, event | category | flops | bytes accessed | tf_op | source)
XLA Modules:
  0.0 116.6 jit_solution(2442078280209782218)
XLA Ops:
  0.7 0.8 copy-done
  1.4 0.6 broadcast_in_dim.28
  2.1 15.9 %all-to-all-start = ((bf16[16,8,384]{2,1,0:T(8,128)(2,1)}), bf16[16,8,384]{2,1,0:T(8,128)(2,1)S(1)}, u32[]{:S(2)}, u32[]{:S(2)}) async-start(bf16[16,8,384]{2,1,0:T(8,128)(2,1)} %broadcast_in_dim.28), calls=%async_computation | async-start | bytes 196608 | tf_op jit(solution)/shard_map/all_to_all | solution.py:141
  18.0 1.2 %copy-done.1 = bf16[128,4096]{1,0:T(8,128)(2,1)S(1)} copy-done((bf16[128,4096]{1,0:T(8,128)(2,1)S(1)}, bf16[128,4096]{1,0:T(8,128)(2,1)}, u32[]{:S(2)}) %copy-start.1) | copy-done | bytes 1048600
  19.2 0.3 cut_blocks.1
  19.6 3.1 %collective-permute-start = (bf16[2,144,512]{2,1,0:T(8,128)(2,1)S(1)}, bf16[2,144,512]{2,1,0:T(8,128)(2,1)}, u32[]{:S(2)}, u32[]{:S(2)}) collective-permute-start(bf16[2,144,512]{2,1,0:T(8,128)(2,1)S(1)} %get-tuple-element.27), channel_id=1, source_target_pairs={{0,64},{64,128},{128,192},{192,0},{1,65},{65,129},{129,193},{193,1... | collective-permute-start | bytes 884744 | tf_op jit(solution)/shard_map/ppermute | solution.py:208
  22.7 4.4 %collective-permute-start.1 = (bf16[2,144,512]{2,1,0:T(8,128)(2,1)S(1)}, bf16[2,144,512]{2,1,0:T(8,128)(2,1)}, u32[]{:S(2)}, u32[]{:S(2)}) collective-permute-start(bf16[2,144,512]{2,1,0:T(8,128)(2,1)S(1)} %get-tuple-element.28), channel_id=1, source_target_pairs={{0,128},{64,192},{128,0},{192,64},{1,129},{65,193},{129,1},{193,65... | collective-permute-start | bytes 884744 | tf_op jit(solution)/shard_map/ppermute | solution.py:208
  27.1 3.1 %collective-permute-start.2 = (bf16[2,144,512]{2,1,0:T(8,128)(2,1)S(1)}, bf16[2,144,512]{2,1,0:T(8,128)(2,1)S(1)}, u32[]{:S(2)}, u32[]{:S(2)}) collective-permute-start(bf16[2,144,512]{2,1,0:T(8,128)(2,1)S(1)} %get-tuple-element.29), channel_id=1, source_target_pairs={{0,192},{64,0},{128,64},{192,128},{1,193},{65,1},{129,65},{193,129... | collective-permute-start | bytes 884744 | tf_op jit(solution)/shard_map/ppermute | solution.py:208
  30.4 1.3 %copy_rows.1 = (bf16[16,128,384]{2,1,0:T(8,128)(2,1)}, bf16[1,512]{1,0:T(2,128)(2,1)S(1)}) custom-call(bf16[128,384]{1,0:T(8,128)(2,1)S(1)} %bitcast.33), custom_call_target="tpu_custom_call" | custom-call | tf_op jit(solution)/shard_map/copy_rows/pallas_call | solution.py:142
  31.7 4.3 %all-to-all-start.1 = ((bf16[16,128,384]{2,1,0:T(8,128)(2,1)}), bf16[16,128,384]{2,1,0:T(8,128)(2,1)S(1)}, u32[]{:S(2)}, u32[]{:S(2)}) async-start(bf16[16,128,384]{2,1,0:T(8,128)(2,1)} %get-tuple-element.24), calls=%async_computation.1 | async-start | bytes 3145728 | tf_op jit(solution)/shard_map/all_to_all | solution.py:148
  36.2 1.0 bitcast_dynamic-update-slice_fusion.2
  37.4 1.0 bitcast_dynamic-update-slice_fusion.1
  38.3 0.4 collective-permute-done.2
  38.9 5.8 %collective-permute-start.3 = (bf16[4,2,144,256]{3,2,1,0:T(8,128)(2,1)S(1)}, bf16[4,2,144,256]{3,2,1,0:T(8,128)(2,1)S(1)}, u32[]{:S(2)}, u32[]{:S(2)}) collective-permute-start(bf16[4,2,144,256]{3,2,1,0:T(8,128)(2,1)S(1)} %get-tuple-element.46), channel_id=1, source_target_pairs={{0,1},{1,0},{2,3},{3,2},{4,5},{5,4},{6,7},{7,6},{8,9},{9,8},{10,11... | collective-permute-start | bytes 1769480 | tf_op jit(solution)/shard_map/ppermute | solution.py:126
  44.7 0.5 prepare_columns.2
  45.3 0.4 fusion
  45.7 0.3 fusion.2.normed_ref
  46.3 0.5 prepare_columns.3
  46.9 1.0 copy-done.5
  47.8 0.8 copy-done.7
  48.6 8.9 %all-to-all-done.1 = bf16[16,128,384]{2,1,0:T(8,128)(2,1)S(1)} async-done(((bf16[16,128,384]{2,1,0:T(8,128)(2,1)}), bf16[16,128,384]{2,1,0:T(8,128)(2,1)S(1)}, u32[]{:S(2)}, u32[]{:S(2)}) %all-to-all-start.1) | async-done | bytes 1572896 | tf_op jit(solution)/shard_map/all_to_all | solution.py:148
  57.6 5.8 %collective-permute-start.4 = (bf16[2048,384]{1,0:T(8,128)(2,1)S(1)}, bf16[2048,384]{1,0:T(8,128)(2,1)}, u32[]{:S(2)}, u32[]{:S(2)}) collective-permute-start(bf16[2048,384]{1,0:T(8,128)(2,1)S(1)} %bitcast.26), channel_id=1, source_target_pairs={{0,1},{1,0},{2,3},{3,2},{4,5},{5,4},{6,7},{7,6},{8,9},{9,8},{10,11... | collective-permute-start | bytes 4718600 | tf_op jit(solution)/shard_map/ppermute | solution.py:126
  64.2 2.4 %collective-permute-done.4 = bf16[2048,384]{1,0:T(8,128)(2,1)} collective-permute-done((bf16[2048,384]{1,0:T(8,128)(2,1)S(1)}, bf16[2048,384]{1,0:T(8,128)(2,1)}, u32[]{:S(2)}, u32[]{:S(2)}) %collective-permute-start.4) | collective-permute-done | bytes 1572896 | tf_op jit(solution)/shard_map/ppermute | solution.py:126
  66.6 3.2 %attention_grads.1 = (bf16[4,128,384]{2,1,0:T(8,128)(2,1)S(1)}, bf16[512,384]{1,0:T(8,128)(2,1)S(1)}) custom-call(s32[2]{0:T(128)S(1)} %pad_add_fusion.core_ref, bf16[16,2,64,384]{3,2,1,0:T(8,128)(2,1)S(1)} %order_rows.1.own_ref, bf16[8,2,16,8,384]{4,3,2,1,0:T(8,128)(2,1)} %bitcast.11.other_ref, bf16[128,4096]{1,0:T(8,128)(2,1)S(1)} %fusion.2.normed_ref, ...), custom_call_target="tpu_custom_call" | custom-call | tf_op jit(solution)/shard_map/attention_grads/pallas_call | solution.py:96
  69.8 10.1 %all_to_all.41 = bf16[4,128,384]{2,1,0:T(8,128)(2,1)S(1)} all-to-all(bf16[4,128,384]{2,1,0:T(8,128)(2,1)S(1)} %get-tuple-element.38), channel_id=1, replica_groups=mesh['y_hi'=2,'x'=4,'z'=16,'y_lo'=2,'core'=2] {'x'}, dimensions={0} | all-to-all | bytes 786432 | tf_op jit(solution)/shard_map/all_to_all | solution.py:352
  79.9 3.7 %collective-permute-start.5 = (bf16[512,384]{1,0:T(8,128)(2,1)S(1)}, bf16[512,384]{1,0:T(8,128)(2,1)S(1)}, u32[]{:S(2)}, u32[]{:S(2)}) collective-permute-start(bf16[512,384]{1,0:T(8,128)(2,1)S(1)} %bitcast.29), channel_id=1, source_target_pairs={{0,1},{1,0},{2,3},{3,2},{4,5},{5,4},{6,7},{7,6},{8,9},{9,8},{10,11... | collective-permute-start | bytes 1179656 | tf_op jit(solution)/shard_map/ppermute | solution.py:126
  83.6 0.8 first_grads.1
  84.4 0.5 collective-permute-done.5.grads_ref
  85.0 1.3 %code_y.1 = s16[8,72,384]{2,1,0:T(8,128)(2,1)S(1)} custom-call(f32[512,384]{1,0:T(8,128)S(1)} %get-tuple-element.40.first_ref, f32[512,1]{1,0:T(8,128)S(1)} %get-tuple-element.41.first_gain_ref, bf16[512,512]{1,0:T(8,128)(2,1)S(1)} %copy-done.8, f32[512,512]{1,0:T(8,128)S(1)} %copy-done.6, bf16[512,384]{1,0:T(8,128)(2,1)S(1)} %collective-permute-done.5.grads_ref, ...), custom_call_target="tpu_custom_call" | custom-call | tf_op jit(solution)/shard_map/code_y/pallas_call | solution.py:362
  86.3 11.3 %all_to_all.42.parts_ref = s16[8,72,384]{2,1,0:T(8,128)(2,1)S(1)} all-to-all(s16[8,72,384]{2,1,0:T(8,128)(2,1)S(1)} %code_y.1), channel_id=1, replica_groups=mesh['y_hi'=2,'x'=4,'z'=16,'y_lo'=2,'core'=2] {'y_hi','y_lo','core'}, dimensions={0} | all-to-all | bytes 884736 | tf_op jit(solution)/shard_map/all_to_all | solution.py:369
  98.0 17.9 %all_to_all.43 = s16[16,8,512]{2,1,0:T(8,128)(2,1)S(1)} all-to-all(s16[16,8,512]{2,1,0:T(8,128)(2,1)S(1)} %bitcast.32), channel_id=1, replica_groups={{16,20,24,28,32,36,40,44,48,52,56,60,0,4,8,12},{17,21,25,29,33,37,41,45..., dimensions={0} | all-to-all | bytes 262144 | tf_op jit(solution)/shard_map/all_to_all | solution.py:373
  115.9 0.7 decode_rows.1
  (44 shorter events, 2.0 us)
Async XLA Ops:
  0.6 0.8 copy-start
  0.6 29.5 %copy-start.10 = (f32[4096]{0:T(1024)S(1)}, f32[4096]{0:T(1024)}, u32[]{:S(2)}) copy-start(f32[4096]{0:T(1024)} %param.6) | copy-start | bytes 49156
  2.1 28.3 %all-to-all-start = ((bf16[16,8,384]{2,1,0:T(8,128)(2,1)}), bf16[16,8,384]{2,1,0:T(8,128)(2,1)S(1)}, u32[]{:S(2)}, u32[]{:S(2)}) async-start(bf16[16,8,384]{2,1,0:T(8,128)(2,1)} %broadcast_in_dim.28), calls=%async_computation | async-start | bytes 196608 | tf_op jit(solution)/shard_map/all_to_all | solution.py:141
  18.0 1.2 %copy-start.1 = (bf16[128,4096]{1,0:T(8,128)(2,1)S(1)}, bf16[128,4096]{1,0:T(8,128)(2,1)}, u32[]{:S(2)}) copy-start(bf16[128,4096]{1,0:T(8,128)(2,1)} %activations_ref.1) | copy-start | bytes 3145732
  19.6 16.6 %collective-permute-start = (bf16[2,144,512]{2,1,0:T(8,128)(2,1)S(1)}, bf16[2,144,512]{2,1,0:T(8,128)(2,1)}, u32[]{:S(2)}, u32[]{:S(2)}) collective-permute-start(bf16[2,144,512]{2,1,0:T(8,128)(2,1)S(1)} %get-tuple-element.27), channel_id=1, source_target_pairs={{0,64},{64,128},{128,192},{192,0},{1,65},{65,129},{129,193},{193,1... | collective-permute-start | bytes 884744 | tf_op jit(solution)/shard_map/ppermute | solution.py:208
  22.7 14.6 %collective-permute-start.1 = (bf16[2,144,512]{2,1,0:T(8,128)(2,1)S(1)}, bf16[2,144,512]{2,1,0:T(8,128)(2,1)}, u32[]{:S(2)}, u32[]{:S(2)}) collective-permute-start(bf16[2,144,512]{2,1,0:T(8,128)(2,1)S(1)} %get-tuple-element.28), channel_id=1, source_target_pairs={{0,128},{64,192},{128,0},{192,64},{1,129},{65,193},{129,1},{193,65... | collective-permute-start | bytes 884744 | tf_op jit(solution)/shard_map/ppermute | solution.py:208
  27.1 11.7 %collective-permute-start.2 = (bf16[2,144,512]{2,1,0:T(8,128)(2,1)S(1)}, bf16[2,144,512]{2,1,0:T(8,128)(2,1)S(1)}, u32[]{:S(2)}, u32[]{:S(2)}) collective-permute-start(bf16[2,144,512]{2,1,0:T(8,128)(2,1)S(1)} %get-tuple-element.29), channel_id=1, source_target_pairs={{0,192},{64,0},{128,64},{192,128},{1,193},{65,1},{129,65},{193,129... | collective-permute-start | bytes 884744 | tf_op jit(solution)/shard_map/ppermute | solution.py:208
  31.7 25.8 %all-to-all-start.1 = ((bf16[16,128,384]{2,1,0:T(8,128)(2,1)}), bf16[16,128,384]{2,1,0:T(8,128)(2,1)S(1)}, u32[]{:S(2)}, u32[]{:S(2)}) async-start(bf16[16,128,384]{2,1,0:T(8,128)(2,1)} %get-tuple-element.24), calls=%async_computation.1 | async-start | bytes 3145728 | tf_op jit(solution)/shard_map/all_to_all | solution.py:148
  38.8 6.5 %copy-start.2 = (bf16[128,4096]{1,0:T(8,128)(2,1)S(1)}, bf16[128,4096]{1,0:T(8,128)(2,1)}, u32[]{:S(2)}) copy-start(bf16[128,4096]{1,0:T(8,128)(2,1)} %activations_ref.1) | copy-start | bytes 3145732
  38.9 7.4 %collective-permute-start.3 = (bf16[4,2,144,256]{3,2,1,0:T(8,128)(2,1)S(1)}, bf16[4,2,144,256]{3,2,1,0:T(8,128)(2,1)S(1)}, u32[]{:S(2)}, u32[]{:S(2)}) collective-permute-start(bf16[4,2,144,256]{3,2,1,0:T(8,128)(2,1)S(1)} %get-tuple-element.46), channel_id=1, source_target_pairs={{0,1},{1,0},{2,3},{3,2},{4,5},{5,4},{6,7},{7,6},{8,9},{9,8},{10,11... | collective-permute-start | bytes 1769480 | tf_op jit(solution)/shard_map/ppermute | solution.py:126
  45.3 1.0 copy-start.3
  45.7 17.7 %copy-start.11 = (s32[128]{0:T(128)S(1)}, s32[128]{0:T(128)}, u32[]{:S(2)}) copy-start(s32[128]{0:T(128)} %param.8) | copy-start | bytes 1540
  46.9 1.0 copy-start.5
  47.8 0.8 copy-start.7
  57.6 9.0 %collective-permute-start.4 = (bf16[2048,384]{1,0:T(8,128)(2,1)S(1)}, bf16[2048,384]{1,0:T(8,128)(2,1)}, u32[]{:S(2)}, u32[]{:S(2)}) collective-permute-start(bf16[2048,384]{1,0:T(8,128)(2,1)S(1)} %bitcast.26), channel_id=1, source_target_pairs={{0,1},{1,0},{2,3},{3,2},{4,5},{5,4},{6,7},{7,6},{8,9},{9,8},{10,11... | collective-permute-start | bytes 4718600 | tf_op jit(solution)/shard_map/ppermute | solution.py:126
  63.8 2.7 %copy-start.9 = (bf16[128,128]{1,0:T(8,128)(2,1)S(1)}, bf16[128,128]{1,0:T(8,128)(2,1)}, u32[]{:S(2)}) copy-start(bf16[128,128]{1,0:T(8,128)(2,1)} %cotangent_ref.1) | copy-start | bytes 98308
  66.6 17.1 %copy-start.4 = (f32[512,512]{1,0:T(8,128)S(1)}, f32[512,512]{1,0:T(8,128)}, u32[]{:S(2)}) copy-start(f32[512,512]{1,0:T(8,128)} %copy-done.3) | copy-start | bytes 3145732
  79.9 5.0 %collective-permute-start.5 = (bf16[512,384]{1,0:T(8,128)(2,1)S(1)}, bf16[512,384]{1,0:T(8,128)(2,1)S(1)}, u32[]{:S(2)}, u32[]{:S(2)}) collective-permute-start(bf16[512,384]{1,0:T(8,128)(2,1)S(1)} %bitcast.29), channel_id=1, source_target_pairs={{0,1},{1,0},{2,3},{3,2},{4,5},{5,4},{6,7},{7,6},{8,9},{9,8},{10,11... | collective-permute-start | bytes 1179656 | tf_op jit(solution)/shard_map/ppermute | solution.py:126
  83.6 1.3 %copy-start.6 = (f32[512,512]{1,0:T(8,128)S(1)}, f32[512,512]{1,0:T(8,128)}, u32[]{:S(2)}) copy-start(f32[512,512]{1,0:T(8,128)} %copy-done.5) | copy-start | bytes 3145732
  83.6 1.3 %copy-start.8 = (bf16[512,512]{1,0:T(8,128)(2,1)S(1)}, bf16[512,512]{1,0:T(8,128)(2,1)}, u32[]{:S(2)}) copy-start(bf16[512,512]{1,0:T(8,128)(2,1)} %copy-done.7) | copy-start | bytes 1572868

commit v6 on v5

--- a/solution.py
+++ b/solution.py
@@ -104,7 +104,7 @@
         scratch_shapes=[pltpu.VMEM((4096, width), jnp.bfloat16)],
         name="attention_grads",
         compiler_params=pltpu.CompilerParams(vmem_limit_bytes=20 * 2**20),
-    )(place, ordered, swap_cores(own).reshape(raw.shape), normed, *tables, positions, cotangent)
+    )(place, ordered, swap_cores(ordered), normed, *tables, positions, cotangent)
     return grads.reshape(4 * tokens, width), rows
 
 
@@ -160,10 +160,9 @@
     core, column = core_ref[0], core_ref[1]
     for z in range(16):
         for y in range(2):
-            rows = [other_ref[eighth, y, z].astype(jnp.float32) for eighth in range(8)]
             place = z * 256 + y * 128
             weight_ref[pl.ds(pl.multiple_of(place + core * 64, 64), 64), :] = own_ref[z, y]
-            weight_ref[pl.ds(pl.multiple_of(place + (1 - core) * 64, 64), 64), :] = jnp.concatenate(rows).astype(jnp.bfloat16)
+            weight_ref[pl.ds(pl.multiple_of(place + (1 - core) * 64, 64), 64), :] = other_ref[z, y]
     for half in range(2):
         start = pl.multiple_of(half * 2048 + column * 256, 256)
         rows_ref[pl.ds(half * 256, 256), :] = weight_ref[pl.ds(start, 256), :]
@@ -203,7 +202,8 @@
         cost_estimate=BRIEF,
     )(x_index.reshape(1), activations)
     ordered = jnp.broadcast_to(seed.reshape(1, 1, 1, 512), (4, 2, tokens + 16, 512))
-    for shift, block in enumerate(blocks):
+    for shift in (0, 2, 1, 3):
+        block = blocks[shift]
         if shift:
             block = lax.ppermute(block, "x", [(i, (i + shift) % 4) for i in range(4)])
         ordered = lax.dynamic_update_slice(ordered, block[None], (lax.rem(x_index - shift + 4, 4), 0, 0, 0))

time: 117 us -> 117 us (level)
  starting transfers between devices: 46.2 us -> 45 us
    ppermute x3, starting transfers between devices: 15.4 us -> 13.6 us  [swap_cores(): return lax.ppermute(array, 'core', [(0, 1), (1, 0)])]
    unnamed x26 -> x32, local copies, waits for them, and re-layouts: 4.05 us -> 4.67 us
  transfers between devices with their start and end apart: 8 -> 8, of which waited for: 6 -> 3; matrix products, arithmetic and copies ran while one was open for 3% -> 4% of each run, Pallas kernels for 3% -> 3%
where the time goes in v6:
time: 117 us; the launch traced here: 116 us
  starting transfers between devices  45 us (38%)
  blocking collectives  38.8 us (33%)
  waiting for transfers between devices  11.4 us (10%)
  Pallas kernels  9.3 us (8%)
  local copies, waits for them, and re-layouts  7.98 us (7%)
  other arithmetic  1.97 us (2%)
    all_to_all x1, blocking collectives, shards(): lax.all_to_all(coded, 'z', 0, 0, axis_index_groups=LAST_ORDER, tiled=True)  17.3 us
    all_to_all x1, starting transfers between devices, gather_plane(): lax.all_to_all(broadcast_rows(part, 16), 'z', 0, 0, axis_index_groups=FIR...  15.9 us
    ppermute x3, starting transfers between devices, swap_cores(): return lax.ppermute(array, 'core', [(0, 1), (1, 0)])  13.6 us
    all_to_all x1, blocking collectives, shards(): parts = lax.all_to_all(parts, ('y_hi', 'y_lo', 'core'), 0, 0, tiled=True)  11.3 us
    ppermute x3, starting transfers between devices, redistribute(): block = lax.ppermute(block, 'x', [(i, (i + shift) % 4) for i in range(4)])  11.1 us
    all_to_all x1, blocking collectives, shards(): own_grads = lax.all_to_all(qkv_grads, 'x', 0, 0, tiled=True)  10.2 us
    all_to_all x1, waiting for transfers between devices, gather_plane(): lax.all_to_all(copies.reshape(2048, width), ('y_hi', 'x', 'y_lo'), 0, 0,...  8.41 us
    unnamed x32, local copies, waits for them, and re-layouts  4.67 us
  transfers between devices with their start and end apart: 8, of which 3 were waited for; matrix products, arithmetic and copies ran while one was open for 4% of the time, Pallas kernels for 3%

profile of v6, /device:TPU:1, one launch (start us, length us, event | category | flops | bytes accessed | tf_op | source)
XLA Modules:
  0.0 115.5 jit_solution(10374997334498746901)
XLA Ops:
  0.7 0.8 copy-done
  1.4 0.7 broadcast_in_dim.28
  2.1 15.9 %all-to-all-start = ((bf16[16,8,384]{2,1,0:T(8,128)(2,1)}), bf16[16,8,384]{2,1,0:T(8,128)(2,1)S(1)}, u32[]{:S(2)}, u32[]{:S(2)}) async-start(bf16[16,8,384]{2,1,0:T(8,128)(2,1)} %broadcast_in_dim.28), calls=%async_computation | async-start | bytes 196608 | tf_op jit(solution)/shard_map/all_to_all | solution.py:141
  18.0 1.2 %copy-done.1 = bf16[128,4096]{1,0:T(8,128)(2,1)S(1)} copy-done((bf16[128,4096]{1,0:T(8,128)(2,1)S(1)}, bf16[128,4096]{1,0:T(8,128)(2,1)}, u32[]{:S(2)}) %copy-start.1) | copy-done | bytes 1048600
  19.3 0.3 cut_blocks.1
  19.6 4.7 %collective-permute-start = (bf16[2,144,512]{2,1,0:T(8,128)(2,1)S(1)}, bf16[2,144,512]{2,1,0:T(8,128)(2,1)}, u32[]{:S(2)}, u32[]{:S(2)}) collective-permute-start(bf16[2,144,512]{2,1,0:T(8,128)(2,1)S(1)} %get-tuple-element.27), channel_id=1, source_target_pairs={{0,128},{64,192},{128,0},{192,64},{1,129},{65,193},{129,1},{193,65... | collective-permute-start | bytes 884744 | tf_op jit(solution)/shard_map/ppermute | solution.py:208
  24.3 2.2 %collective-permute-start.1 = (bf16[2,144,512]{2,1,0:T(8,128)(2,1)S(1)}, bf16[2,144,512]{2,1,0:T(8,128)(2,1)}, u32[]{:S(2)}, u32[]{:S(2)}) collective-permute-start(bf16[2,144,512]{2,1,0:T(8,128)(2,1)S(1)} %get-tuple-element.28), channel_id=1, source_target_pairs={{0,64},{64,128},{128,192},{192,0},{1,65},{65,129},{129,193},{193,1... | collective-permute-start | bytes 884744 | tf_op jit(solution)/shard_map/ppermute | solution.py:208
  26.5 4.3 %collective-permute-start.2 = (bf16[2,144,512]{2,1,0:T(8,128)(2,1)S(1)}, bf16[2,144,512]{2,1,0:T(8,128)(2,1)S(1)}, u32[]{:S(2)}, u32[]{:S(2)}) collective-permute-start(bf16[2,144,512]{2,1,0:T(8,128)(2,1)S(1)} %get-tuple-element.29), channel_id=1, source_target_pairs={{0,192},{64,0},{128,64},{192,128},{1,193},{65,1},{129,65},{193,129... | collective-permute-start | bytes 884744 | tf_op jit(solution)/shard_map/ppermute | solution.py:208
  31.0 1.3 %copy_rows.1 = (bf16[16,128,384]{2,1,0:T(8,128)(2,1)}, bf16[1,512]{1,0:T(2,128)(2,1)S(1)}) custom-call(bf16[128,384]{1,0:T(8,128)(2,1)S(1)} %bitcast.31), custom_call_target="tpu_custom_call" | custom-call | tf_op jit(solution)/shard_map/copy_rows/pallas_call | solution.py:142
  32.3 4.3 %all-to-all-start.1 = ((bf16[16,128,384]{2,1,0:T(8,128)(2,1)}), bf16[16,128,384]{2,1,0:T(8,128)(2,1)S(1)}, u32[]{:S(2)}, u32[]{:S(2)}) async-start(bf16[16,128,384]{2,1,0:T(8,128)(2,1)} %get-tuple-element.24), calls=%async_computation.1 | async-start | bytes 3145728 | tf_op jit(solution)/shard_map/all_to_all | solution.py:148
  36.8 1.0 bitcast_dynamic-update-slice_fusion.2
  37.8 1.0 bitcast_dynamic-update-slice_fusion.1
  39.0 4.4 %collective-permute-start.3 = (bf16[4,2,144,256]{3,2,1,0:T(8,128)(2,1)S(1)}, bf16[4,2,144,256]{3,2,1,0:T(8,128)(2,1)S(1)}, u32[]{:S(2)}, u32[]{:S(2)}) collective-permute-start(bf16[4,2,144,256]{3,2,1,0:T(8,128)(2,1)S(1)} %get-tuple-element.46), channel_id=1, source_target_pairs={{0,1},{1,0},{2,3},{3,2},{4,5},{5,4},{6,7},{7,6},{8,9},{9,8},{10,11... | collective-permute-start | bytes 1769480 | tf_op jit(solution)/shard_map/ppermute | solution.py:126
  43.4 0.5 prepare_columns.2
  43.9 0.8 copy-done.8
  44.7 0.4 fusion
  45.1 1.3 %fusion.2.normed_ref = bf16[128,4096]{1,0:T(8,128)(2,1)} fusion(f32[4096]{0:T(1024)S(1)} %copy-done.13, f32[128]{0:T(128)S(1)} %add_rsqrt_fusion, bf16[128,4096]{1,0:T(8,128)(2,1)S(1)} %copy-done.2, bf16[4096]{0:T(1024)(128)(2,1)S(1)} %bitcast.33), kind=kLoop, calls=%fused_computation.4 | loop fusion | flops 2621440 | bytes 2122240 | tf_op jit(solution)/shard_map/convert_element_type | solution.py:37
  46.4 0.5 prepare_columns.3
  47.0 1.0 copy-done.6
  47.9 0.8 copy-done.10
  48.8 8.4 %all-to-all-done.1 = bf16[16,128,384]{2,1,0:T(8,128)(2,1)S(1)} async-done(((bf16[16,128,384]{2,1,0:T(8,128)(2,1)}), bf16[16,128,384]{2,1,0:T(8,128)(2,1)S(1)}, u32[]{:S(2)}, u32[]{:S(2)}) %all-to-all-start.1) | async-done | bytes 1572896 | tf_op jit(solution)/shard_map/all_to_all | solution.py:148
  57.3 6.1 %collective-permute-start.4 = (bf16[16,2,64,384]{3,2,1,0:T(8,128)(2,1)S(1)}, bf16[16,2,64,384]{3,2,1,0:T(8,128)(2,1)}, u32[]{:S(2)}, u32[]{:S(2)}) collective-permute-start(bf16[16,2,64,384]{3,2,1,0:T(8,128)(2,1)S(1)} %order_rows.1.own_ref), channel_id=1, source_target_pairs={{0,1},{1,0},{2,3},{3,2},{4,5},{5,4},{6,7},{7,6},{8,9},{9,8},{10,11... | collective-permute-start | bytes 4718600 | tf_op jit(solution)/shard_map/ppermute | solution.py:126
  64.1 2.5 %collective-permute-done.4.other_ref = bf16[16,2,64,384]{3,2,1,0:T(8,128)(2,1)} collective-permute-done((bf16[16,2,64,384]{3,2,1,0:T(8,128)(2,1)S(1)}, bf16[16,2,64,384]{3,2,1,0:T(8,128)(2,1)}, u32[]{:S(2)}, u32[]{:S(2)}) %collective-permute-start.4) | collective-permute-done | bytes 1572896 | tf_op jit(solution)/shard_map/ppermute | solution.py:126
  66.6 3.3 %attention_grads.1 = (bf16[4,128,384]{2,1,0:T(8,128)(2,1)S(1)}, bf16[512,384]{1,0:T(8,128)(2,1)S(1)}) custom-call(s32[2]{0:T(128)S(1)} %pad_add_fusion.core_ref, bf16[16,2,64,384]{3,2,1,0:T(8,128)(2,1)S(1)} %order_rows.1.own_ref, bf16[16,2,64,384]{3,2,1,0:T(8,128)(2,1)} %collective-permute-done.4.other_ref, bf16[128,4096]{1,0:T(8,128)(2,1)S(1)} %copy-done.3, ...), custom_call_target="tpu_custom_call" | custom-call | tf_op jit(solution)/shard_map/attention_grads/pallas_call | solution.py:96
  69.9 10.2 %all_to_all.41 = bf16[4,128,384]{2,1,0:T(8,128)(2,1)S(1)} all-to-all(bf16[4,128,384]{2,1,0:T(8,128)(2,1)S(1)} %get-tuple-element.38), channel_id=1, replica_groups=mesh['y_hi'=2,'x'=4,'z'=16,'y_lo'=2,'core'=2] {'x'}, dimensions={0} | all-to-all | bytes 786432 | tf_op jit(solution)/shard_map/all_to_all | solution.py:352
  80.1 3.1 %collective-permute-start.5 = (bf16[512,384]{1,0:T(8,128)(2,1)S(1)}, bf16[512,384]{1,0:T(8,128)(2,1)S(1)}, u32[]{:S(2)}, u32[]{:S(2)}) collective-permute-start(bf16[512,384]{1,0:T(8,128)(2,1)S(1)} %bitcast.27), channel_id=1, source_target_pairs={{0,1},{1,0},{2,3},{3,2},{4,5},{5,4},{6,7},{7,6},{8,9},{9,8},{10,11... | collective-permute-start | bytes 1179656 | tf_op jit(solution)/shard_map/ppermute | solution.py:126
  83.3 0.8 first_grads.1
  84.1 0.5 collective-permute-done.5.grads_ref
  84.6 1.3 %code_y.1 = s16[8,72,384]{2,1,0:T(8,128)(2,1)S(1)} custom-call(f32[512,384]{1,0:T(8,128)S(1)} %get-tuple-element.40.first_ref, f32[512,1]{1,0:T(8,128)S(1)} %get-tuple-element.41.first_gain_ref, bf16[512,512]{1,0:T(8,128)(2,1)S(1)} %copy-done.11, f32[512,512]{1,0:T(8,128)S(1)} %copy-done.7, bf16[512,384]{1,0:T(8,128)(2,1)S(1)} %collective-permute-done.5.grads_ref, ...), custom_call_target="tpu_custom_call" | custom-call | tf_op jit(solution)/shard_map/code_y/pallas_call | solution.py:362
  86.0 11.3 %all_to_all.42.parts_ref = s16[8,72,384]{2,1,0:T(8,128)(2,1)S(1)} all-to-all(s16[8,72,384]{2,1,0:T(8,128)(2,1)S(1)} %code_y.1), channel_id=1, replica_groups=mesh['y_hi'=2,'x'=4,'z'=16,'y_lo'=2,'core'=2] {'y_hi','y_lo','core'}, dimensions={0} | all-to-all | bytes 884736 | tf_op jit(solution)/shard_map/all_to_all | solution.py:369
  97.6 17.3 %all_to_all.43 = s16[16,8,512]{2,1,0:T(8,128)(2,1)S(1)} all-to-all(s16[16,8,512]{2,1,0:T(8,128)(2,1)S(1)} %bitcast.30), channel_id=1, replica_groups={{16,20,24,28,32,36,40,44,48,52,56,60,0,4,8,12},{17,21,25,29,33,37,41,45..., dimensions={0} | all-to-all | bytes 262144 | tf_op jit(solution)/shard_map/all_to_all | solution.py:373
  114.8 0.7 decode_rows.1
  (50 shorter events, 1.6 us)
Async XLA Ops:
  0.6 0.8 copy-start
  0.6 30.1 %copy-start.13 = (f32[4096]{0:T(1024)S(1)}, f32[4096]{0:T(1024)}, u32[]{:S(2)}) copy-start(f32[4096]{0:T(1024)} %param.6) | copy-start | bytes 49156
  2.1 28.9 %all-to-all-start = ((bf16[16,8,384]{2,1,0:T(8,128)(2,1)}), bf16[16,8,384]{2,1,0:T(8,128)(2,1)S(1)}, u32[]{:S(2)}, u32[]{:S(2)}) async-start(bf16[16,8,384]{2,1,0:T(8,128)(2,1)} %broadcast_in_dim.28), calls=%async_computation | async-start | bytes 196608 | tf_op jit(solution)/shard_map/all_to_all | solution.py:141
  18.0 1.2 %copy-start.1 = (bf16[128,4096]{1,0:T(8,128)(2,1)S(1)}, bf16[128,4096]{1,0:T(8,128)(2,1)}, u32[]{:S(2)}) copy-start(bf16[128,4096]{1,0:T(8,128)(2,1)} %activations_ref.1) | copy-start | bytes 3145732
  19.6 17.2 %collective-permute-start = (bf16[2,144,512]{2,1,0:T(8,128)(2,1)S(1)}, bf16[2,144,512]{2,1,0:T(8,128)(2,1)}, u32[]{:S(2)}, u32[]{:S(2)}) collective-permute-start(bf16[2,144,512]{2,1,0:T(8,128)(2,1)S(1)} %get-tuple-element.27), channel_id=1, source_target_pairs={{0,128},{64,192},{128,0},{192,64},{1,129},{65,193},{129,1},{193,65... | collective-permute-start | bytes 884744 | tf_op jit(solution)/shard_map/ppermute | solution.py:208
  24.3 13.6 %collective-permute-start.1 = (bf16[2,144,512]{2,1,0:T(8,128)(2,1)S(1)}, bf16[2,144,512]{2,1,0:T(8,128)(2,1)}, u32[]{:S(2)}, u32[]{:S(2)}) collective-permute-start(bf16[2,144,512]{2,1,0:T(8,128)(2,1)S(1)} %get-tuple-element.28), channel_id=1, source_target_pairs={{0,64},{64,128},{128,192},{192,0},{1,65},{65,129},{129,193},{193,1... | collective-permute-start | bytes 884744 | tf_op jit(solution)/shard_map/ppermute | solution.py:208
  26.5 12.3 %collective-permute-start.2 = (bf16[2,144,512]{2,1,0:T(8,128)(2,1)S(1)}, bf16[2,144,512]{2,1,0:T(8,128)(2,1)S(1)}, u32[]{:S(2)}, u32[]{:S(2)}) collective-permute-start(bf16[2,144,512]{2,1,0:T(8,128)(2,1)S(1)} %get-tuple-element.29), channel_id=1, source_target_pairs={{0,192},{64,0},{128,64},{192,128},{1,193},{65,1},{129,65},{193,129... | collective-permute-start | bytes 884744 | tf_op jit(solution)/shard_map/ppermute | solution.py:208
  32.3 24.8 %all-to-all-start.1 = ((bf16[16,128,384]{2,1,0:T(8,128)(2,1)}), bf16[16,128,384]{2,1,0:T(8,128)(2,1)S(1)}, u32[]{:S(2)}, u32[]{:S(2)}) async-start(bf16[16,128,384]{2,1,0:T(8,128)(2,1)} %get-tuple-element.24), calls=%async_computation.1 | async-start | bytes 3145728 | tf_op jit(solution)/shard_map/all_to_all | solution.py:148
  38.9 5.9 %copy-start.2 = (bf16[128,4096]{1,0:T(8,128)(2,1)S(1)}, bf16[128,4096]{1,0:T(8,128)(2,1)}, u32[]{:S(2)}) copy-start(bf16[128,4096]{1,0:T(8,128)(2,1)} %activations_ref.1) | copy-start | bytes 3145732
  39.0 7.4 %collective-permute-start.3 = (bf16[4,2,144,256]{3,2,1,0:T(8,128)(2,1)S(1)}, bf16[4,2,144,256]{3,2,1,0:T(8,128)(2,1)S(1)}, u32[]{:S(2)}, u32[]{:S(2)}) collective-permute-start(bf16[4,2,144,256]{3,2,1,0:T(8,128)(2,1)S(1)} %get-tuple-element.46), channel_id=1, source_target_pairs={{0,1},{1,0},{2,3},{3,2},{4,5},{5,4},{6,7},{7,6},{8,9},{9,8},{10,11... | collective-permute-start | bytes 1769480 | tf_op jit(solution)/shard_map/ppermute | solution.py:126
  43.9 0.8 copy-start.8
  44.7 1.7 %copy-start.4 = (f32[512,512]{1,0:T(8,128)}, f32[512,512]{1,0:T(8,128)S(1)}, u32[]{:S(2)}) copy-start(f32[512,512]{1,0:T(8,128)S(1)} %get-tuple-element.35.unit_ref) | copy-start | bytes 3145732
  47.0 1.0 copy-start.6
  47.9 0.8 copy-start.10
  57.2 6.3 %copy-start.14 = (s32[128]{0:T(128)S(1)}, s32[128]{0:T(128)}, u32[]{:S(2)}) copy-start(s32[128]{0:T(128)} %param.8) | copy-start | bytes 1540
  57.3 9.3 %copy-start.12 = (bf16[128,128]{1,0:T(8,128)(2,1)S(1)}, bf16[128,128]{1,0:T(8,128)(2,1)}, u32[]{:S(2)}) copy-start(bf16[128,128]{1,0:T(8,128)(2,1)} %cotangent_ref.1) | copy-start | bytes 98308
  57.3 9.3 %collective-permute-start.4 = (bf16[16,2,64,384]{3,2,1,0:T(8,128)(2,1)S(1)}, bf16[16,2,64,384]{3,2,1,0:T(8,128)(2,1)}, u32[]{:S(2)}, u32[]{:S(2)}) collective-permute-start(bf16[16,2,64,384]{3,2,1,0:T(8,128)(2,1)S(1)} %order_rows.1.own_ref), channel_id=1, source_target_pairs={{0,1},{1,0},{2,3},{3,2},{4,5},{5,4},{6,7},{7,6},{8,9},{9,8},{10,11... | collective-permute-start | bytes 4718600 | tf_op jit(solution)/shard_map/ppermute | solution.py:126
  63.6 3.0 %copy-start.3 = (bf16[128,4096]{1,0:T(8,128)(2,1)S(1)}, bf16[128,4096]{1,0:T(8,128)(2,1)}, u32[]{:S(2)}) copy-start(bf16[128,4096]{1,0:T(8,128)(2,1)} %fusion.2.normed_ref) | copy-start | bytes 3145732
  66.6 16.6 %copy-start.5 = (f32[512,512]{1,0:T(8,128)S(1)}, f32[512,512]{1,0:T(8,128)}, u32[]{:S(2)}) copy-start(f32[512,512]{1,0:T(8,128)} %copy-done.4) | copy-start | bytes 3145732
  66.6 16.6 %copy-start.9 = (bf16[512,512]{1,0:T(8,128)(2,1)S(1)}, bf16[512,512]{1,0:T(8,128)(2,1)}, u32[]{:S(2)}) copy-start(bf16[512,512]{1,0:T(8,128)(2,1)} %copy-done.8) | copy-start | bytes 1572868
  80.1 4.4 %collective-permute-start.5 = (bf16[512,384]{1,0:T(8,128)(2,1)S(1)}, bf16[512,384]{1,0:T(8,128)(2,1)S(1)}, u32[]{:S(2)}, u32[]{:S(2)}) collective-permute-start(bf16[512,384]{1,0:T(8,128)(2,1)S(1)} %bitcast.27), channel_id=1, source_target_pairs={{0,1},{1,0},{2,3},{3,2},{4,5},{5,4},{6,7},{7,6},{8,9},{9,8},{10,11... | collective-permute-start | bytes 1179656 | tf_op jit(solution)/shard_map/ppermute | solution.py:126
  83.3 1.3 %copy-start.7 = (f32[512,512]{1,0:T(8,128)S(1)}, f32[512,512]{1,0:T(8,128)}, u32[]{:S(2)}) copy-start(f32[512,512]{1,0:T(8,128)} %copy-done.6) | copy-start | bytes 3145732
  83.3 1.3 %copy-start.11 = (bf16[512,512]{1,0:T(8,128)(2,1)S(1)}, bf16[512,512]{1,0:T(8,128)(2,1)}, u32[]{:S(2)}) copy-start(bf16[512,512]{1,0:T(8,128)(2,1)} %copy-done.10) | copy-start | bytes 1572868

commit v7 on v6

--- a/solution.py
+++ b/solution.py
@@ -126,6 +126,13 @@
     return lax.ppermute(array, "core", [(0, 1), (1, 0)])
 
 
+def part_kernel(member_ref, weight_ref, parts_ref, wide_ref):
+    wide_ref[...] = weight_ref[...].astype(jnp.float32)
+    rows = wide_ref[pl.ds(pl.multiple_of(member_ref[0] * 8, 8), 8), :].astype(jnp.bfloat16)
+    for copy in range(16):
+        parts_ref[copy] = rows
+
+
 def copy_kernel(part_ref, copies_ref, seed_ref):
     late = FIRST_Z * 8
     for copy in range(16):
@@ -137,8 +144,17 @@
 def gather_plane(qkv_weight):
     width = qkv_weight.shape[1]
     member = lax.axis_index("y_hi") * 4 + lax.axis_index("x")
-    part = lax.dynamic_slice(qkv_weight, (member * 8, 0), (8, width))
-    along_z = lax.all_to_all(broadcast_rows(part, 16), "z", 0, 0, axis_index_groups=FIRST_ORDER, tiled=True)
+    parts = pl.pallas_call(
+        part_kernel,
+        out_shape=jax.ShapeDtypeStruct((16, 8, width), jnp.bfloat16),
+        in_specs=[pl.BlockSpec(memory_space=pltpu.SMEM), pl.BlockSpec(memory_space=pltpu.VMEM)],
+        out_specs=pl.BlockSpec(memory_space=pltpu.VMEM),
+        scratch_shapes=[pltpu.VMEM((64, width), jnp.float32)],
+        name="part_rows",
+        compiler_params=SMALL,
+        cost_estimate=BRIEF,
+    )(member.reshape(1), qkv_weight)
+    along_z = lax.all_to_all(parts.reshape(128, width), "z", 0, 0, axis_index_groups=FIRST_ORDER, tiled=True)
     copies, seed = pl.pallas_call(
         copy_kernel,
         out_shape=(jax.ShapeDtypeStruct((16, 128, width), jnp.bfloat16), jax.ShapeDtypeStruct((1, 512), jnp.bfloat16)),

time: 117 us -> 117 us (level)
  no operation moved by 1% of the time
where the time goes in v7:
time: 117 us; the launch traced here: 116 us
  starting transfers between devices  45 us (38%)
  blocking collectives  38.8 us (33%)
  waiting for transfers between devices  11.4 us (10%)
  Pallas kernels  9.97 us (9%)
  local copies, waits for them, and re-layouts  7.33 us (6%)
  other arithmetic  1.97 us (2%)
    all_to_all x1, blocking collectives, shards(): lax.all_to_all(coded, 'z', 0, 0, axis_index_groups=LAST_ORDER, tiled=True)  17.3 us
    all_to_all x1, starting transfers between devices, gather_plane(): lax.all_to_all(parts.reshape(128, width), 'z', 0, 0, axis_index_groups=FI...  15.9 us
    ppermute x3, starting transfers between devices, swap_cores(): return lax.ppermute(array, 'core', [(0, 1), (1, 0)])  13.6 us
    all_to_all x1, blocking collectives, shards(): parts = lax.all_to_all(parts, ('y_hi', 'y_lo', 'core'), 0, 0, tiled=True)  11.3 us
    ppermute x3, starting transfers between devices, redistribute(): block = lax.ppermute(block, 'x', [(i, (i + shift) % 4) for i in range(4)])  11.1 us
    all_to_all x1, blocking collectives, shards(): own_grads = lax.all_to_all(qkv_grads, 'x', 0, 0, tiled=True)  10.2 us
    all_to_all x1, waiting for transfers between devices, gather_plane(): lax.all_to_all(copies.reshape(2048, width), ('y_hi', 'x', 'y_lo'), 0, 0,...  8.41 us
    unnamed x32, local copies, waits for them, and re-layouts  4.69 us
  transfers between devices with their start and end apart: 8, of which 3 were waited for; matrix products, arithmetic and copies ran while one was open for 4% of the time, Pallas kernels for 3%

profile of v7, /device:TPU:1, one launch (start us, length us, event | category | flops | bytes accessed | tf_op | source)
XLA Modules:
  0.0 115.5 jit_solution(8263921910082584535)
XLA Ops:
  0.7 0.8 copy-done.11
  1.4 0.7 part_rows.1
  2.1 15.9 %all-to-all-start = ((bf16[16,8,384]{2,1,0:T(8,128)(2,1)}), bf16[16,8,384]{2,1,0:T(8,128)(2,1)S(1)}, u32[]{:S(2)}, u32[]{:S(2)}) async-start(bf16[16,8,384]{2,1,0:T(8,128)(2,1)} %part_rows.1), calls=%async_computation | async-start | bytes 196608 | tf_op jit(solution)/shard_map/all_to_all | solution.py:157
  18.1 1.2 %copy-done = bf16[128,4096]{1,0:T(8,128)(2,1)S(1)} copy-done((bf16[128,4096]{1,0:T(8,128)(2,1)S(1)}, bf16[128,4096]{1,0:T(8,128)(2,1)}, u32[]{:S(2)}) %copy-start) | copy-done | bytes 1048600
  19.3 0.3 cut_blocks.1
  19.6 4.7 %collective-permute-start = (bf16[2,144,512]{2,1,0:T(8,128)(2,1)S(1)}, bf16[2,144,512]{2,1,0:T(8,128)(2,1)}, u32[]{:S(2)}, u32[]{:S(2)}) collective-permute-start(bf16[2,144,512]{2,1,0:T(8,128)(2,1)S(1)} %get-tuple-element.27), channel_id=1, source_target_pairs={{0,128},{64,192},{128,0},{192,64},{1,129},{65,193},{129,1},{193,65... | collective-permute-start | bytes 884744 | tf_op jit(solution)/shard_map/ppermute | solution.py:224
  24.3 2.2 %collective-permute-start.1 = (bf16[2,144,512]{2,1,0:T(8,128)(2,1)S(1)}, bf16[2,144,512]{2,1,0:T(8,128)(2,1)}, u32[]{:S(2)}, u32[]{:S(2)}) collective-permute-start(bf16[2,144,512]{2,1,0:T(8,128)(2,1)S(1)} %get-tuple-element.28), channel_id=1, source_target_pairs={{0,64},{64,128},{128,192},{192,0},{1,65},{65,129},{129,193},{193,1... | collective-permute-start | bytes 884744 | tf_op jit(solution)/shard_map/ppermute | solution.py:224
  26.5 4.3 %collective-permute-start.2 = (bf16[2,144,512]{2,1,0:T(8,128)(2,1)S(1)}, bf16[2,144,512]{2,1,0:T(8,128)(2,1)S(1)}, u32[]{:S(2)}, u32[]{:S(2)}) collective-permute-start(bf16[2,144,512]{2,1,0:T(8,128)(2,1)S(1)} %get-tuple-element.29), channel_id=1, source_target_pairs={{0,192},{64,0},{128,64},{192,128},{1,193},{65,1},{129,65},{193,129... | collective-permute-start | bytes 884744 | tf_op jit(solution)/shard_map/ppermute | solution.py:224
  31.0 1.3 %copy_rows.1 = (bf16[16,128,384]{2,1,0:T(8,128)(2,1)}, bf16[1,512]{1,0:T(2,128)(2,1)S(1)}) custom-call(bf16[128,384]{1,0:T(8,128)(2,1)S(1)} %bitcast.32), custom_call_target="tpu_custom_call" | custom-call | tf_op jit(solution)/shard_map/copy_rows/pallas_call | solution.py:158
  32.4 4.3 %all-to-all-start.1 = ((bf16[16,128,384]{2,1,0:T(8,128)(2,1)}), bf16[16,128,384]{2,1,0:T(8,128)(2,1)S(1)}, u32[]{:S(2)}, u32[]{:S(2)}) async-start(bf16[16,128,384]{2,1,0:T(8,128)(2,1)} %get-tuple-element.24), calls=%async_computation.1 | async-start | bytes 3145728 | tf_op jit(solution)/shard_map/all_to_all | solution.py:164
  36.8 1.0 bitcast_dynamic-update-slice_fusion.2
  37.8 1.0 bitcast_dynamic-update-slice_fusion.1
  39.0 4.4 %collective-permute-start.3 = (bf16[4,2,144,256]{3,2,1,0:T(8,128)(2,1)S(1)}, bf16[4,2,144,256]{3,2,1,0:T(8,128)(2,1)S(1)}, u32[]{:S(2)}, u32[]{:S(2)}) collective-permute-start(bf16[4,2,144,256]{3,2,1,0:T(8,128)(2,1)S(1)} %get-tuple-element.46), channel_id=1, source_target_pairs={{0,1},{1,0},{2,3},{3,2},{4,5},{5,4},{6,7},{7,6},{8,9},{9,8},{10,11... | collective-permute-start | bytes 1769480 | tf_op jit(solution)/shard_map/ppermute | solution.py:126
  43.4 0.5 prepare_columns.2
  43.9 0.8 copy-done.7
  44.7 0.4 fusion
  45.1 1.3 %fusion.2.normed_ref = bf16[128,4096]{1,0:T(8,128)(2,1)} fusion(f32[4096]{0:T(1024)S(1)} %copy-done.13, f32[128]{0:T(128)S(1)} %add_rsqrt_fusion, bf16[128,4096]{1,0:T(8,128)(2,1)S(1)} %copy-done.1, bf16[4096]{0:T(1024)(128)(2,1)S(1)} %bitcast.34), kind=kLoop, calls=%fused_computation.4 | loop fusion | flops 2621440 | bytes 2122240 | tf_op jit(solution)/shard_map/convert_element_type | solution.py:37
  46.5 0.5 prepare_columns.3
  47.0 1.0 copy-done.5
  48.0 0.8 copy-done.9
  48.8 8.4 %all-to-all-done.1 = bf16[16,128,384]{2,1,0:T(8,128)(2,1)S(1)} async-done(((bf16[16,128,384]{2,1,0:T(8,128)(2,1)}), bf16[16,128,384]{2,1,0:T(8,128)(2,1)S(1)}, u32[]{:S(2)}, u32[]{:S(2)}) %all-to-all-start.1) | async-done | bytes 1572896 | tf_op jit(solution)/shard_map/all_to_all | solution.py:164
  57.3 6.1 %collective-permute-start.4 = (bf16[16,2,64,384]{3,2,1,0:T(8,128)(2,1)S(1)}, bf16[16,2,64,384]{3,2,1,0:T(8,128)(2,1)}, u32[]{:S(2)}, u32[]{:S(2)}) collective-permute-start(bf16[16,2,64,384]{3,2,1,0:T(8,128)(2,1)S(1)} %order_rows.1.own_ref), channel_id=1, source_target_pairs={{0,1},{1,0},{2,3},{3,2},{4,5},{5,4},{6,7},{7,6},{8,9},{9,8},{10,11... | collective-permute-start | bytes 4718600 | tf_op jit(solution)/shard_map/ppermute | solution.py:126
  64.1 2.5 %collective-permute-done.4.other_ref = bf16[16,2,64,384]{3,2,1,0:T(8,128)(2,1)} collective-permute-done((bf16[16,2,64,384]{3,2,1,0:T(8,128)(2,1)S(1)}, bf16[16,2,64,384]{3,2,1,0:T(8,128)(2,1)}, u32[]{:S(2)}, u32[]{:S(2)}) %collective-permute-start.4) | collective-permute-done | bytes 1572896 | tf_op jit(solution)/shard_map/ppermute | solution.py:126
  66.6 3.3 %attention_grads.1 = (bf16[4,128,384]{2,1,0:T(8,128)(2,1)S(1)}, bf16[512,384]{1,0:T(8,128)(2,1)S(1)}) custom-call(s32[2]{0:T(128)S(1)} %pad_add_fusion.core_ref, bf16[16,2,64,384]{3,2,1,0:T(8,128)(2,1)S(1)} %order_rows.1.own_ref, bf16[16,2,64,384]{3,2,1,0:T(8,128)(2,1)} %collective-permute-done.4.other_ref, bf16[128,4096]{1,0:T(8,128)(2,1)S(1)} %copy-done.2, ...), custom_call_target="tpu_custom_call" | custom-call | tf_op jit(solution)/shard_map/attention_grads/pallas_call | solution.py:96
  69.9 10.2 %all_to_all.41 = bf16[4,128,384]{2,1,0:T(8,128)(2,1)S(1)} all-to-all(bf16[4,128,384]{2,1,0:T(8,128)(2,1)S(1)} %get-tuple-element.38), channel_id=1, replica_groups=mesh['y_hi'=2,'x'=4,'z'=16,'y_lo'=2,'core'=2] {'x'}, dimensions={0} | all-to-all | bytes 786432 | tf_op jit(solution)/shard_map/all_to_all | solution.py:368
  80.1 3.1 %collective-permute-start.5 = (bf16[512,384]{1,0:T(8,128)(2,1)S(1)}, bf16[512,384]{1,0:T(8,128)(2,1)S(1)}, u32[]{:S(2)}, u32[]{:S(2)}) collective-permute-start(bf16[512,384]{1,0:T(8,128)(2,1)S(1)} %bitcast.28), channel_id=1, source_target_pairs={{0,1},{1,0},{2,3},{3,2},{4,5},{5,4},{6,7},{7,6},{8,9},{9,8},{10,11... | collective-permute-start | bytes 1179656 | tf_op jit(solution)/shard_map/ppermute | solution.py:126
  83.3 0.8 first_grads.1
  84.1 0.5 collective-permute-done.5.grads_ref
  84.6 1.3 %code_y.1 = s16[8,72,384]{2,1,0:T(8,128)(2,1)S(1)} custom-call(f32[512,384]{1,0:T(8,128)S(1)} %get-tuple-element.40.first_ref, f32[512,1]{1,0:T(8,128)S(1)} %get-tuple-element.41.first_gain_ref, bf16[512,512]{1,0:T(8,128)(2,1)S(1)} %copy-done.10, f32[512,512]{1,0:T(8,128)S(1)} %copy-done.6, bf16[512,384]{1,0:T(8,128)(2,1)S(1)} %collective-permute-done.5.grads_ref, ...), custom_call_target="tpu_custom_call" | custom-call | tf_op jit(solution)/shard_map/code_y/pallas_call | solution.py:378
  86.0 11.3 %all_to_all.42.parts_ref = s16[8,72,384]{2,1,0:T(8,128)(2,1)S(1)} all-to-all(s16[8,72,384]{2,1,0:T(8,128)(2,1)S(1)} %code_y.1), channel_id=1, replica_groups=mesh['y_hi'=2,'x'=4,'z'=16,'y_lo'=2,'core'=2] {'y_hi','y_lo','core'}, dimensions={0} | all-to-all | bytes 884736 | tf_op jit(solution)/shard_map/all_to_all | solution.py:385
  97.6 17.3 %all_to_all.43 = s16[16,8,512]{2,1,0:T(8,128)(2,1)S(1)} all-to-all(s16[16,8,512]{2,1,0:T(8,128)(2,1)S(1)} %bitcast.31), channel_id=1, replica_groups={{16,20,24,28,32,36,40,44,48,52,56,60,0,4,8,12},{17,21,25,29,33,37,41,45..., dimensions={0} | all-to-all | bytes 262144 | tf_op jit(solution)/shard_map/all_to_all | solution.py:389
  114.9 0.7 decode_rows.1
  (49 shorter events, 1.6 us)
Async XLA Ops:
  0.6 30.2 %copy-start.13 = (f32[4096]{0:T(1024)S(1)}, f32[4096]{0:T(1024)}, u32[]{:S(2)}) copy-start(f32[4096]{0:T(1024)} %param.6) | copy-start | bytes 49156
  0.6 0.8 copy-start.11
  2.1 28.9 %all-to-all-start = ((bf16[16,8,384]{2,1,0:T(8,128)(2,1)}), bf16[16,8,384]{2,1,0:T(8,128)(2,1)S(1)}, u32[]{:S(2)}, u32[]{:S(2)}) async-start(bf16[16,8,384]{2,1,0:T(8,128)(2,1)} %part_rows.1), calls=%async_computation | async-start | bytes 196608 | tf_op jit(solution)/shard_map/all_to_all | solution.py:157
  18.1 1.2 %copy-start = (bf16[128,4096]{1,0:T(8,128)(2,1)S(1)}, bf16[128,4096]{1,0:T(8,128)(2,1)}, u32[]{:S(2)}) copy-start(bf16[128,4096]{1,0:T(8,128)(2,1)} %activations_ref.1) | copy-start | bytes 3145732
  19.6 17.2 %collective-permute-start = (bf16[2,144,512]{2,1,0:T(8,128)(2,1)S(1)}, bf16[2,144,512]{2,1,0:T(8,128)(2,1)}, u32[]{:S(2)}, u32[]{:S(2)}) collective-permute-start(bf16[2,144,512]{2,1,0:T(8,128)(2,1)S(1)} %get-tuple-element.27), channel_id=1, source_target_pairs={{0,128},{64,192},{128,0},{192,64},{1,129},{65,193},{129,1},{193,65... | collective-permute-start | bytes 884744 | tf_op jit(solution)/shard_map/ppermute | solution.py:224
  24.3 13.6 %collective-permute-start.1 = (bf16[2,144,512]{2,1,0:T(8,128)(2,1)S(1)}, bf16[2,144,512]{2,1,0:T(8,128)(2,1)}, u32[]{:S(2)}, u32[]{:S(2)}) collective-permute-start(bf16[2,144,512]{2,1,0:T(8,128)(2,1)S(1)} %get-tuple-element.28), channel_id=1, source_target_pairs={{0,64},{64,128},{128,192},{192,0},{1,65},{65,129},{129,193},{193,1... | collective-permute-start | bytes 884744 | tf_op jit(solution)/shard_map/ppermute | solution.py:224
  26.5 12.3 %collective-permute-start.2 = (bf16[2,144,512]{2,1,0:T(8,128)(2,1)S(1)}, bf16[2,144,512]{2,1,0:T(8,128)(2,1)S(1)}, u32[]{:S(2)}, u32[]{:S(2)}) collective-permute-start(bf16[2,144,512]{2,1,0:T(8,128)(2,1)S(1)} %get-tuple-element.29), channel_id=1, source_target_pairs={{0,192},{64,0},{128,64},{192,128},{1,193},{65,1},{129,65},{193,129... | collective-permute-start | bytes 884744 | tf_op jit(solution)/shard_map/ppermute | solution.py:224
  32.4 24.8 %all-to-all-start.1 = ((bf16[16,128,384]{2,1,0:T(8,128)(2,1)}), bf16[16,128,384]{2,1,0:T(8,128)(2,1)S(1)}, u32[]{:S(2)}, u32[]{:S(2)}) async-start(bf16[16,128,384]{2,1,0:T(8,128)(2,1)} %get-tuple-element.24), calls=%async_computation.1 | async-start | bytes 3145728 | tf_op jit(solution)/shard_map/all_to_all | solution.py:164
  38.9 5.9 %copy-start.1 = (bf16[128,4096]{1,0:T(8,128)(2,1)S(1)}, bf16[128,4096]{1,0:T(8,128)(2,1)}, u32[]{:S(2)}) copy-start(bf16[128,4096]{1,0:T(8,128)(2,1)} %activations_ref.1) | copy-start | bytes 3145732
  39.0 7.4 %collective-permute-start.3 = (bf16[4,2,144,256]{3,2,1,0:T(8,128)(2,1)S(1)}, bf16[4,2,144,256]{3,2,1,0:T(8,128)(2,1)S(1)}, u32[]{:S(2)}, u32[]{:S(2)}) collective-permute-start(bf16[4,2,144,256]{3,2,1,0:T(8,128)(2,1)S(1)} %get-tuple-element.46), channel_id=1, source_target_pairs={{0,1},{1,0},{2,3},{3,2},{4,5},{5,4},{6,7},{7,6},{8,9},{9,8},{10,11... | collective-permute-start | bytes 1769480 | tf_op jit(solution)/shard_map/ppermute | solution.py:126
  43.9 0.8 copy-start.7
  44.7 1.7 %copy-start.3 = (f32[512,512]{1,0:T(8,128)}, f32[512,512]{1,0:T(8,128)S(1)}, u32[]{:S(2)}) copy-start(f32[512,512]{1,0:T(8,128)S(1)} %get-tuple-element.35.unit_ref) | copy-start | bytes 3145732
  47.0 1.0 copy-start.5
  48.0 0.8 copy-start.9
  57.2 6.3 %copy-start.14 = (s32[128]{0:T(128)S(1)}, s32[128]{0:T(128)}, u32[]{:S(2)}) copy-start(s32[128]{0:T(128)} %param.8) | copy-start | bytes 1540
  57.3 9.3 %copy-start.12 = (bf16[128,128]{1,0:T(8,128)(2,1)S(1)}, bf16[128,128]{1,0:T(8,128)(2,1)}, u32[]{:S(2)}) copy-start(bf16[128,128]{1,0:T(8,128)(2,1)} %cotangent_ref.1) | copy-start | bytes 98308
  57.3 9.3 %collective-permute-start.4 = (bf16[16,2,64,384]{3,2,1,0:T(8,128)(2,1)S(1)}, bf16[16,2,64,384]{3,2,1,0:T(8,128)(2,1)}, u32[]{:S(2)}, u32[]{:S(2)}) collective-permute-start(bf16[16,2,64,384]{3,2,1,0:T(8,128)(2,1)S(1)} %order_rows.1.own_ref), channel_id=1, source_target_pairs={{0,1},{1,0},{2,3},{3,2},{4,5},{5,4},{6,7},{7,6},{8,9},{9,8},{10,11... | collective-permute-start | bytes 4718600 | tf_op jit(solution)/shard_map/ppermute | solution.py:126
  63.6 3.0 %copy-start.2 = (bf16[128,4096]{1,0:T(8,128)(2,1)S(1)}, bf16[128,4096]{1,0:T(8,128)(2,1)}, u32[]{:S(2)}) copy-start(bf16[128,4096]{1,0:T(8,128)(2,1)} %fusion.2.normed_ref) | copy-start | bytes 3145732
  66.6 16.6 %copy-start.4 = (f32[512,512]{1,0:T(8,128)S(1)}, f32[512,512]{1,0:T(8,128)}, u32[]{:S(2)}) copy-start(f32[512,512]{1,0:T(8,128)} %copy-done.3) | copy-start | bytes 3145732
  66.6 16.6 %copy-start.8 = (bf16[512,512]{1,0:T(8,128)(2,1)S(1)}, bf16[512,512]{1,0:T(8,128)(2,1)}, u32[]{:S(2)}) copy-start(bf16[512,512]{1,0:T(8,128)(2,1)} %copy-done.7) | copy-start | bytes 1572868
  80.1 4.4 %collective-permute-start.5 = (bf16[512,384]{1,0:T(8,128)(2,1)S(1)}, bf16[512,384]{1,0:T(8,128)(2,1)S(1)}, u32[]{:S(2)}, u32[]{:S(2)}) collective-permute-start(bf16[512,384]{1,0:T(8,128)(2,1)S(1)} %bitcast.28), channel_id=1, source_target_pairs={{0,1},{1,0},{2,3},{3,2},{4,5},{5,4},{6,7},{7,6},{8,9},{9,8},{10,11... | collective-permute-start | bytes 1179656 | tf_op jit(solution)/shard_map/ppermute | solution.py:126
  83.3 1.3 %copy-start.6 = (f32[512,512]{1,0:T(8,128)S(1)}, f32[512,512]{1,0:T(8,128)}, u32[]{:S(2)}) copy-start(f32[512,512]{1,0:T(8,128)} %copy-done.5) | copy-start | bytes 3145732
  83.3 1.3 %copy-start.10 = (bf16[512,512]{1,0:T(8,128)(2,1)S(1)}, bf16[512,512]{1,0:T(8,128)(2,1)}, u32[]{:S(2)}) copy-start(bf16[512,512]{1,0:T(8,128)(2,1)} %copy-done.9) | copy-start | bytes 1572868
